TPU v7x, 512 devices: a whole 4x8x8 slice. The times are simulated.
512 devices in a mesh: chrom: 256 (over x, z, y_lo, core), chan: 2 (over y_hi).
Axes of the slice: x: 4, y: 8 (y_hi: 2, y_lo: 4; y = y_hi * 4 + y_lo), z: 8, core: 2. Of those that a mesh axis runs over, the one named last changes fastest.
Arguments:
- embedding: bfloat16 [4096, 512], P('chrom'), may hold values from -6 to 6
- window_start: int32 [1], replicated, may hold values from 0 to 59999
- band_width: int32 [1], replicated, may hold values from 257 to 512
- dilations: int32 [2], replicated, may hold values from 1 to 8, as said below
- near_weight: bfloat16 [512, 48], P(None, 'chan'), may hold values from -0.25 to 0.25
- far_weight: bfloat16 [512, 48], P(None, 'chan'), may hold values from -0.25 to 0.25
- distance_bias: float32 [48, 512], P('chan'), may hold values from -3 to 3
- conv_weight: bfloat16 [2, 9, 48, 48], replicated, may hold values from -0.3125 to 0.3125
- conv_bias: float32 [2, 48], P(None, 'chan'), may hold values from -3 to 3
- cotangent: bfloat16 [48, 4096, 512], P('chan', 'chrom'), may hold values from -0.59765625 to 0.59765625
Outputs:
- pair_out: bfloat16 [48, 4096, 512], P('chan', 'chrom')
- embedding_grad: bfloat16 [4096, 512], P('chrom', 'chan')
Inputs may be any that keep to these rules, and one draw needn't show every extreme that they name: Every entry of dilations is at least 1 and at most 8, and some layer's dilation equals 8.
All inputs are finite; a program needn't handle non-finite values.
Results may differ from a plain program's by a relative error of at most 0.0054.
Values may be sent and summed in bfloat16 or wider, within the bound.
No kernel may reach another device: no remote copies, remote signals or barrier semaphores. Data moves between devices by JAX's collectives and lax.ppermute only.
A program may use at most 64 MiB of HBM per device.

v0:
```python
import jax
import jax.numpy as jnp
from jax import lax
from jax.sharding import PartitionSpec as P

LAYERS = 2
DMAX = 8
NF = 16


two_pi = 6.283185307179586


def padded_2(cells, sides, width):
    for axis, dim in sides:
        count = lax.axis_size(axis)
        ends = count - 1
        head = lax.slice_in_dim(cells, 0, width, axis=dim)
        tail = lax.slice_in_dim(cells, cells.shape[dim] - width, cells.shape[dim], axis=dim)
        cells = jnp.concatenate(
            [
                lax.ppermute(tail, axis, [(i, (i + 1) % count) for i in range(ends)]),
                cells,
                lax.ppermute(head, axis, [((i + 1) % count, i) for i in range(ends)]),
            ],
            axis=dim,
        )
    return cells


def partner_2(block, axis, bit):
    count = lax.axis_size(axis)
    route = []
    for low in range(count):
        high = low | 1 << bit
        if high != low and high < count:
            route += [(low, high), (high, low)]
    return lax.ppermute(block, axis, route)


def from_behind(block, axis, distance):
    devices = range(lax.axis_size(axis))
    route = [(i - distance, i) for i in devices if i - distance in devices]
    return lax.ppermute(block, axis, route)


def gelu_exact(values):
    return jax.nn.gelu(values, approximate=False)


def encode(row_ids, start_bin, feature_count):
    octave = jnp.arange(NF, dtype=jnp.int32)
    period = jnp.power(jnp.int32(2), octave + 2).astype(jnp.int32)
    residue = jnp.remainder(start_bin + row_ids[:, None], period[None, :])
    angles = residue.astype(jnp.float32) * (two_pi / period.astype(jnp.float32))[None, :]
    encoding = jnp.concatenate((jnp.sin(angles), jnp.cos(angles)), axis=1)
    return jnp.pad(encoding, ((0, 0), (0, feature_count - 2 * NF)))


def band_mask(row_ids, width_value, band_slots, total_rows):
    offsets = jnp.arange(band_slots, dtype=jnp.int32)
    inside = (offsets[None, :] < width_value) & (row_ids[:, None] + offsets[None, :] < total_rows)
    return inside.astype(jnp.float32)


def tap_sum(source_act, weights, dilation, sign):
    in_count = source_act.shape[0]
    row_count = source_act.shape[1] - 2 * DMAX
    band_slots = source_act.shape[2]
    col_padded = jnp.pad(source_act, ((0, 0), (0, 0), (2 * DMAX, 2 * DMAX)))
    running = jnp.zeros((weights.shape[1], row_count * band_slots), jnp.float32)
    for tap_index in range(9):
        row_step = tap_index // 3 - 1
        col_step = tap_index % 3 - 1
        row_start = DMAX + sign * row_step * dilation
        col_start = 2 * DMAX + sign * (col_step - row_step) * dilation
        tap_slice = lax.dynamic_slice(
            col_padded, (jnp.int32(0), row_start, col_start), (in_count, row_count, band_slots)
        )
        running = running + jnp.dot(
            weights[tap_index],
            tap_slice.reshape(in_count, row_count * band_slots),
            preferred_element_type=jnp.float32,
        )
    return running.reshape(weights.shape[1], row_count, band_slots)


def convolve(active, kernel, dilation, sign):
    own_ch = active.shape[0]
    chan_index = lax.axis_index("chan")
    out_rows = lax.dynamic_slice_in_dim(kernel, chan_index * own_ch, own_ch, 1)
    own_cols = lax.dynamic_slice_in_dim(out_rows, chan_index * own_ch, own_ch, 2)
    partner_cols = lax.dynamic_slice_in_dim(out_rows, (1 - chan_index) * own_ch, own_ch, 2)
    weights = jnp.concatenate((own_cols, partner_cols), axis=2)
    padded = padded_2(active, (("chrom", 1),), DMAX)
    partner = partner_2(padded, "chan", 0)
    joined = jnp.concatenate((padded, partner), axis=0)
    return tap_sum(joined, weights, dilation, sign)


def fetch_ahead(far_proj, hop_total, rows_here):
    window = jnp.zeros((far_proj.shape[0], (hop_total + 1) * rows_here), jnp.float32)
    window = lax.dynamic_update_slice_in_dim(window, far_proj, 0, 1)

    def fetch_relay_step(step_index, carry):
        current, gathered = carry
        current = from_behind(current, "chrom", -1)
        gathered = lax.dynamic_update_slice_in_dim(
            gathered, current, (step_index * rows_here).astype(jnp.int32), 1
        )
        return (current, gathered)

    return lax.fori_loop(1, hop_total + 1, fetch_relay_step, (far_proj, window))[1]


def return_behind(partial_value, hop_total, rows_here):

    def return_relay_step(step_index, carry):
        received = from_behind(carry, "chrom", 1)
        start_col = ((hop_total - 1 - step_index) * rows_here).astype(jnp.int32)
        return received + lax.dynamic_slice_in_dim(partial_value, start_col, rows_here, 1)

    return lax.fori_loop(0, hop_total, return_relay_step, partial_value[:, hop_total * rows_here :])


def skew_rows(window, rows_here, band_slots):
    own_ch = window.shape[0]
    span = window.shape[1]
    tiled = jnp.broadcast_to(window[:, None, :], (own_ch, rows_here, span)).reshape(
        own_ch, rows_here * span
    )
    tiled = jnp.pad(tiled, ((0, 0), (0, rows_here)))
    return tiled.reshape(own_ch, rows_here, span + 1)[:, :, :band_slots]


def skew_sum(pair_grad):
    own_ch, rows_here, band_slots = pair_grad.shape
    padded = jnp.pad(pair_grad, ((0, 0), (0, 0), (0, rows_here)))
    flat = padded.reshape(own_ch, rows_here * (band_slots + rows_here))[
        :, : rows_here * (band_slots + rows_here - 1)
    ]
    summed = jnp.sum(flat.reshape(own_ch, rows_here, band_slots + rows_here - 1), axis=1)
    return jnp.pad(summed, ((0, 0), (0, 1)))


def back_project(grad_low, weight_low):
    return lax.dot_general(
        grad_low, weight_low, (((1,), (1,)), ((), ())), preferred_element_type=jnp.float32
    )


def shards(
    embedding,
    window_start,
    band_width,
    dilations,
    near_weight,
    far_weight,
    distance_bias,
    conv_weight,
    conv_bias,
    cotangent,
):
    rows_here = embedding.shape[0]
    band_slots = distance_bias.shape[1]
    hop_total = band_slots // rows_here
    first_row = lax.axis_index("chrom") * rows_here
    total_rows = lax.axis_size("chrom") * rows_here
    row_ids = first_row + jnp.arange(rows_here, dtype=jnp.int32)
    band_keep = band_mask(row_ids, band_width[0], band_slots, total_rows)
    features = (
        embedding.astype(jnp.float32) + encode(row_ids, window_start[0], embedding.shape[1])
    ).astype(jnp.bfloat16)
    near_proj = jnp.dot(features, near_weight, preferred_element_type=jnp.float32).T
    far_proj = jnp.dot(features, far_weight, preferred_element_type=jnp.float32).T
    window = fetch_ahead(far_proj, hop_total, rows_here)
    ahead = skew_rows(window, rows_here, band_slots)
    pair_state = band_keep[None] * (near_proj[:, :, None] + ahead + distance_bias[:, None, :])
    states = []
    for layer_idx in range(LAYERS):
        states.append(pair_state)
        active = gelu_exact(pair_state).astype(jnp.bfloat16)
        conv_out = convolve(active, conv_weight[layer_idx], dilations[layer_idx], 1)
        pair_state = band_keep[None] * (pair_state + conv_out + conv_bias[layer_idx][:, None, None])
    pair_out = pair_state.astype(jnp.bfloat16)
    pair_grad = band_keep[None] * cotangent.astype(jnp.float32)
    for layer_idx in reversed(range(LAYERS)):
        back_conv = convolve(
            pair_grad.astype(jnp.bfloat16),
            jnp.swapaxes(conv_weight[layer_idx], 1, 2),
            dilations[layer_idx],
            -1,
        )
        slope_term = jax.vjp(gelu_exact, states[layer_idx])[1](back_conv)[0]
        pair_grad = band_keep[None] * (pair_grad + slope_term)
    grad_near = jnp.sum(pair_grad, axis=2)
    grad_far = return_behind(skew_sum(pair_grad), hop_total, rows_here)
    near_low = grad_near.astype(jnp.bfloat16).T
    far_low = grad_far.astype(jnp.bfloat16).T
    partial_grad = back_project(near_low, near_weight) + back_project(far_low, far_weight)
    embedding_grad = lax.psum_scatter(partial_grad, "chan", scatter_dimension=1, tiled=True).astype(
        jnp.bfloat16
    )
    return (pair_out, embedding_grad)


def solution(mesh):
    in_specs = (
        P("chrom", None),
        P(),
        P(),
        P(),
        P(None, "chan"),
        P(None, "chan"),
        P("chan", None),
        P(),
        P(None, "chan"),
        P("chan", "chrom", None),
    )
    out_specs = (P("chan", "chrom", None), P("chrom", "chan"))
    return jax.shard_map(shards, mesh=mesh, in_specs=in_specs, out_specs=out_specs, check_vma=False)
```

profile of v0, /device:TPU:6, one launch (start us, length us, event | category | flops | bytes accessed | tf_op | source)
XLA Modules:
  0.0 860.7 jit_solution(16272253659021232265)
XLA Ops:
  9.2 318.0 %while.28 = (s32[]{:T(128)}, f32[24,16]{0,1:T(8,128)S(1)}, f32[24,528]{0,1:T(8,128)S(1)}, s32[]{:T(128)}, s32[]{:T(128)}, /*index=5*/s32[]{:T(128)}, s32[]{:T(128)}) while((s32[]{:T(128)}, f32[24,16]{0,1:T(8,128)S(1)}, f32[24,528]{0,1:T(8,128)S(1)}, s32[]{:T(128)}, s32[]{:T(128)}, /*index=5*/s32[]{:T(128)}, s32[]{:T(128)}) %tuple.113), condition=%wide.region_1.2_spmd, body=%wide.region_0.1_spmd.sunk | while | flops 6 | bytes 25767 | solution.py:113
  9.2 13.7 %collective-permute-start = (f32[24,16]{0,1:T(8,128)S(1)}, f32[24,16]{0,1:T(8,128)S(1)}, u32[]{:S(2)}, u32[]{:S(2)}) collective-permute-start(f32[24,16]{0,1:T(8,128)S(1)} %get-tuple-element.268), channel_id=1, source_target_pairs={{2,0},{4,2},{6,4},{8,6},{10,8},{12,10},{14,12},{16,14},{18,16},{20... | collective-permute-start | bytes 4616 | tf_op jit(solution)/shard_map/while/body/eval_jaxpr/ppermute | solution.py:44
  24.2 8.4 collective-permute-start
  34.0 8.4 collective-permute-start
  43.8 8.4 collective-permute-start
  53.5 8.4 collective-permute-start
  63.3 8.4 collective-permute-start
  82.9 8.4 collective-permute-start
  112.2 8.4 collective-permute-start
  141.5 8.4 collective-permute-start
  170.8 8.4 collective-permute-start
  200.1 8.4 collective-permute-start
  268.5 8.4 collective-permute-start
  297.8 8.4 collective-permute-start
  317.3 8.5 collective-permute-start
  334.6 8.4 collective-permute-start.3
  345.8 8.4 collective-permute-start.9
  354.3 13.5 %collective-permute-done.2 = bf16[24,8,512]{2,1,0:T(8,128)(2,1)S(1)} collective-permute-done((bf16[24,8,512]{2,1,0:T(8,128)(2,1)S(1)}, bf16[24,8,512]{2,1,0:T(8,128)(2,1)S(1)}, u32[]{:S(2)}, u32[]{:S(2)}) %collective-permute-start.2) | collective-permute-done | bytes 196640 | tf_op jit(solution)/shard_map/ppermute | solution.py:22
  427.9 8.4 collective-permute-start.6
  437.8 12.0 %collective-permute-done.6 = bf16[24,8,512]{2,1,0:T(8,128)(2,1)S(1)} collective-permute-done((bf16[24,8,512]{2,1,0:T(8,128)(2,1)S(1)}, bf16[24,8,512]{2,1,0:T(8,128)(2,1)S(1)}, u32[]{:S(2)}, u32[]{:S(2)}) %collective-permute-start.6) | collective-permute-done | bytes 196640 | tf_op jit(solution)/shard_map/ppermute | solution.py:24
  458.6 8.4 collective-permute-start.12
  467.0 22.5 %collective-permute-done.11 = bf16[24,8,512]{2,1,0:T(8,128)(2,1)S(1)} collective-permute-done((bf16[24,8,512]{2,1,0:T(8,128)(2,1)}, bf16[24,8,512]{2,1,0:T(8,128)(2,1)S(1)}, u32[]{:S(2)}, u32[]{:S(2)}) %collective-permute-start.11) | collective-permute-done | bytes 196640 | tf_op jit(solution)/shard_map/ppermute | solution.py:22
  524.5 312.6 %while.29 = (s32[]{:T(128)}, f32[24,16]{0,1:T(8,128)S(1)}, f32[24,528]{0,1:T(8,128)S(1)}, s32[]{:T(128)}, s32[]{:T(128)}, /*index=5*/s32[]{:T(128)}, s32[]{:T(128)}, s32[]{:T(128)}) while((s32[]{:T(128)}, f32[24,16]{0,1:T(8,128)S(1)}, f32[24,528]{0,1:T(8,128)S(1)}, s32[]{:T(128)}, s32[]{:T(128)}, /*index=5*/s32[]{:T(128)}, s32[]{:T(128)}, ...), condition=%wide.region_5.6_spmd, body=%wide.region_4.5_spmd.sunk | while | flops 391 | bytes 10939 | solution.py:123
  837.9 14.4 %reduce-scatter.2.cloned.1.call-done = f32[16,256]{1,0:T(8,128)} async-done(((f32[16,512]{1,0:T(8,128)}), f32[16,256]{1,0:T(8,128)}) %reduce-scatter.2.cloned.1.call-update) | async-done | bytes 16400 | tf_op jit(solution)/shard_map/reduce_scatter | solution.py:201
  (385 shorter events, 614.5 us)
Async XLA Ops:
  7.2 845.1 %reduce-scatter.2.cloned.1.call-start = ((), (), s32[]{:S(2)}) async-start(), calls=%async_computation.1 | async-start | bytes 49152 | tf_op jit(solution)/shard_map/reduce_scatter | solution.py:201
  9.2 15.0 %collective-permute-start = (f32[24,16]{0,1:T(8,128)S(1)}, f32[24,16]{0,1:T(8,128)S(1)}, u32[]{:S(2)}, u32[]{:S(2)}) collective-permute-start(f32[24,16]{0,1:T(8,128)S(1)} %get-tuple-element.268), channel_id=1, source_target_pairs={{2,0},{4,2},{6,4},{8,6},{10,8},{12,10},{14,12},{16,14},{18,16},{20... | collective-permute-start | bytes 4616 | tf_op jit(solution)/shard_map/while/body/eval_jaxpr/ppermute | solution.py:44
  24.2 9.8 %collective-permute-start = (f32[24,16]{0,1:T(8,128)S(1)}, f32[24,16]{0,1:T(8,128)S(1)}, u32[]{:S(2)}, u32[]{:S(2)}) collective-permute-start(f32[24,16]{0,1:T(8,128)S(1)} %get-tuple-element.268), channel_id=1, source_target_pairs={{2,0},{4,2},{6,4},{8,6},{10,8},{12,10},{14,12},{16,14},{18,16},{20... | collective-permute-start | bytes 4616 | tf_op jit(solution)/shard_map/while/body/eval_jaxpr/ppermute | solution.py:44
  34.0 9.8 %collective-permute-start = (f32[24,16]{0,1:T(8,128)S(1)}, f32[24,16]{0,1:T(8,128)S(1)}, u32[]{:S(2)}, u32[]{:S(2)}) collective-permute-start(f32[24,16]{0,1:T(8,128)S(1)} %get-tuple-element.268), channel_id=1, source_target_pairs={{2,0},{4,2},{6,4},{8,6},{10,8},{12,10},{14,12},{16,14},{18,16},{20... | collective-permute-start | bytes 4616 | tf_op jit(solution)/shard_map/while/body/eval_jaxpr/ppermute | solution.py:44
  53.5 9.8 %collective-permute-start = (f32[24,16]{0,1:T(8,128)S(1)}, f32[24,16]{0,1:T(8,128)S(1)}, u32[]{:S(2)}, u32[]{:S(2)}) collective-permute-start(f32[24,16]{0,1:T(8,128)S(1)} %get-tuple-element.268), channel_id=1, source_target_pairs={{2,0},{4,2},{6,4},{8,6},{10,8},{12,10},{14,12},{16,14},{18,16},{20... | collective-permute-start | bytes 4616 | tf_op jit(solution)/shard_map/while/body/eval_jaxpr/ppermute | solution.py:44
  63.3 9.8 %collective-permute-start = (f32[24,16]{0,1:T(8,128)S(1)}, f32[24,16]{0,1:T(8,128)S(1)}, u32[]{:S(2)}, u32[]{:S(2)}) collective-permute-start(f32[24,16]{0,1:T(8,128)S(1)} %get-tuple-element.268), channel_id=1, source_target_pairs={{2,0},{4,2},{6,4},{8,6},{10,8},{12,10},{14,12},{16,14},{18,16},{20... | collective-permute-start | bytes 4616 | tf_op jit(solution)/shard_map/while/body/eval_jaxpr/ppermute | solution.py:44
  82.9 9.8 %collective-permute-start = (f32[24,16]{0,1:T(8,128)S(1)}, f32[24,16]{0,1:T(8,128)S(1)}, u32[]{:S(2)}, u32[]{:S(2)}) collective-permute-start(f32[24,16]{0,1:T(8,128)S(1)} %get-tuple-element.268), channel_id=1, source_target_pairs={{2,0},{4,2},{6,4},{8,6},{10,8},{12,10},{14,12},{16,14},{18,16},{20... | collective-permute-start | bytes 4616 | tf_op jit(solution)/shard_map/while/body/eval_jaxpr/ppermute | solution.py:44
  92.6 9.8 %collective-permute-start = (f32[24,16]{0,1:T(8,128)S(1)}, f32[24,16]{0,1:T(8,128)S(1)}, u32[]{:S(2)}, u32[]{:S(2)}) collective-permute-start(f32[24,16]{0,1:T(8,128)S(1)} %get-tuple-element.268), channel_id=1, source_target_pairs={{2,0},{4,2},{6,4},{8,6},{10,8},{12,10},{14,12},{16,14},{18,16},{20... | collective-permute-start | bytes 4616 | tf_op jit(solution)/shard_map/while/body/eval_jaxpr/ppermute | solution.py:44
  112.2 9.8 %collective-permute-start = (f32[24,16]{0,1:T(8,128)S(1)}, f32[24,16]{0,1:T(8,128)S(1)}, u32[]{:S(2)}, u32[]{:S(2)}) collective-permute-start(f32[24,16]{0,1:T(8,128)S(1)} %get-tuple-element.268), channel_id=1, source_target_pairs={{2,0},{4,2},{6,4},{8,6},{10,8},{12,10},{14,12},{16,14},{18,16},{20... | collective-permute-start | bytes 4616 | tf_op jit(solution)/shard_map/while/body/eval_jaxpr/ppermute | solution.py:44
  121.9 9.8 %collective-permute-start = (f32[24,16]{0,1:T(8,128)S(1)}, f32[24,16]{0,1:T(8,128)S(1)}, u32[]{:S(2)}, u32[]{:S(2)}) collective-permute-start(f32[24,16]{0,1:T(8,128)S(1)} %get-tuple-element.268), channel_id=1, source_target_pairs={{2,0},{4,2},{6,4},{8,6},{10,8},{12,10},{14,12},{16,14},{18,16},{20... | collective-permute-start | bytes 4616 | tf_op jit(solution)/shard_map/while/body/eval_jaxpr/ppermute | solution.py:44
  317.3 9.9 %collective-permute-start = (f32[24,16]{0,1:T(8,128)S(1)}, f32[24,16]{0,1:T(8,128)S(1)}, u32[]{:S(2)}, u32[]{:S(2)}) collective-permute-start(f32[24,16]{0,1:T(8,128)S(1)} %get-tuple-element.268), channel_id=1, source_target_pairs={{2,0},{4,2},{6,4},{8,6},{10,8},{12,10},{14,12},{16,14},{18,16},{20... | collective-permute-start | bytes 4616 | tf_op jit(solution)/shard_map/while/body/eval_jaxpr/ppermute | solution.py:44
  332.5 35.3 %collective-permute-start.2 = (bf16[24,8,512]{2,1,0:T(8,128)(2,1)S(1)}, bf16[24,8,512]{2,1,0:T(8,128)(2,1)S(1)}, u32[]{:S(2)}, u32[]{:S(2)}) collective-permute-start(bf16[24,8,512]{2,1,0:T(8,128)(2,1)S(1)} %get-tuple-element.193), channel_id=1, source_target_pairs={{0,2},{2,4},{4,6},{6,8},{8,10},{10,12},{12,14},{14,16},{16,18},{18... | collective-permute-start | bytes 589832 | tf_op jit(solution)/shard_map/ppermute | solution.py:22
  334.6 33.2 %collective-permute-start.3 = (bf16[24,8,512]{2,1,0:T(8,128)(2,1)S(1)}, bf16[24,8,512]{2,1,0:T(8,128)(2,1)S(1)}, u32[]{:S(2)}, u32[]{:S(2)}) collective-permute-start(bf16[24,8,512]{2,1,0:T(8,128)(2,1)S(1)} %get-tuple-element.194), channel_id=1, source_target_pairs={{2,0},{4,2},{6,4},{8,6},{10,8},{12,10},{14,12},{16,14},{18,16},{20... | collective-permute-start | bytes 589832 | tf_op jit(solution)/shard_map/ppermute | solution.py:24
  343.8 39.9 %collective-permute-start.8 = (bf16[24,8,512]{2,1,0:T(8,128)(2,1)}, bf16[24,8,512]{2,1,0:T(8,128)(2,1)S(1)}, u32[]{:S(2)}, u32[]{:S(2)}) collective-permute-start(bf16[24,8,512]{2,1,0:T(8,128)(2,1)} %get-tuple-element.195), channel_id=1, source_target_pairs={{0,2},{2,4},{4,6},{6,8},{8,10},{10,12},{12,14},{14,16},{16,18},{18... | collective-permute-start | bytes 589832 | tf_op jit(solution)/shard_map/ppermute | solution.py:22
  345.8 37.9 %collective-permute-start.9 = (bf16[24,8,512]{2,1,0:T(8,128)(2,1)}, bf16[24,8,512]{2,1,0:T(8,128)(2,1)S(1)}, u32[]{:S(2)}, u32[]{:S(2)}) collective-permute-start(bf16[24,8,512]{2,1,0:T(8,128)(2,1)} %get-tuple-element.196), channel_id=1, source_target_pairs={{2,0},{4,2},{6,4},{8,6},{10,8},{12,10},{14,12},{16,14},{18,16},{20... | collective-permute-start | bytes 589832 | tf_op jit(solution)/shard_map/ppermute | solution.py:24
  368.8 26.7 %collective-permute-start.4 = (bf16[24,32,512]{2,1,0:T(8,128)(2,1)}, bf16[24,32,512]{2,1,0:T(8,128)(2,1)}, u32[]{:S(2)}, u32[]{:S(2)}) collective-permute-start(bf16[24,32,512]{2,1,0:T(8,128)(2,1)} %pad_maximum_fusion.4), channel_id=1, source_target_pairs={{0,1},{1,0},{2,3},{3,2},{4,5},{5,4},{6,7},{7,6},{8,9},{9,8},{10,11... | collective-permute-start | bytes 2359304 | tf_op jit(solution)/shard_map/ppermute | solution.py:38
  383.8 26.8 %collective-permute-start.10 = (bf16[24,32,512]{2,1,0:T(8,128)(2,1)S(1)}, bf16[24,32,512]{2,1,0:T(8,128)(2,1)S(1)}, u32[]{:S(2)}, u32[]{:S(2)}) collective-permute-start(bf16[24,32,512]{2,1,0:T(8,128)(2,1)S(1)} %pad_maximum_fusion.6), channel_id=1, source_target_pairs={{0,1},{1,0},{2,3},{3,2},{4,5},{5,4},{6,7},{7,6},{8,9},{9,8},{10,11... | collective-permute-start | bytes 2359304 | tf_op jit(solution)/shard_map/ppermute | solution.py:38
  426.0 11.8 %collective-permute-start.5 = (bf16[24,8,512]{2,1,0:T(8,128)(2,1)S(1)}, bf16[24,8,512]{2,1,0:T(8,128)(2,1)S(1)}, u32[]{:S(2)}, u32[]{:S(2)}) collective-permute-start(bf16[24,8,512]{2,1,0:T(8,128)(2,1)S(1)} %get-tuple-element.191), channel_id=1, source_target_pairs={{0,2},{2,4},{4,6},{6,8},{8,10},{10,12},{12,14},{14,16},{16,18},{18... | collective-permute-start | bytes 589832 | tf_op jit(solution)/shard_map/ppermute | solution.py:22
  427.9 21.9 %collective-permute-start.6 = (bf16[24,8,512]{2,1,0:T(8,128)(2,1)S(1)}, bf16[24,8,512]{2,1,0:T(8,128)(2,1)S(1)}, u32[]{:S(2)}, u32[]{:S(2)}) collective-permute-start(bf16[24,8,512]{2,1,0:T(8,128)(2,1)S(1)} %get-tuple-element.192), channel_id=1, source_target_pairs={{2,0},{4,2},{6,4},{8,6},{10,8},{12,10},{14,12},{16,14},{18,16},{20... | collective-permute-start | bytes 589832 | tf_op jit(solution)/shard_map/ppermute | solution.py:24
  450.8 44.1 %collective-permute-start.7 = (bf16[24,32,512]{2,1,0:T(8,128)(2,1)}, bf16[24,32,512]{2,1,0:T(8,128)(2,1)}, u32[]{:S(2)}, u32[]{:S(2)}) collective-permute-start(bf16[24,32,512]{2,1,0:T(8,128)(2,1)} %pad_maximum_fusion.5), channel_id=1, source_target_pairs={{0,1},{1,0},{2,3},{3,2},{4,5},{5,4},{6,7},{7,6},{8,9},{9,8},{10,11... | collective-permute-start | bytes 2359304 | tf_op jit(solution)/shard_map/ppermute | solution.py:38
  456.7 32.9 %collective-permute-start.11 = (bf16[24,8,512]{2,1,0:T(8,128)(2,1)}, bf16[24,8,512]{2,1,0:T(8,128)(2,1)S(1)}, u32[]{:S(2)}, u32[]{:S(2)}) collective-permute-start(bf16[24,8,512]{2,1,0:T(8,128)(2,1)} %get-tuple-element.189), channel_id=1, source_target_pairs={{0,2},{2,4},{4,6},{6,8},{8,10},{10,12},{12,14},{14,16},{16,18},{18... | collective-permute-start | bytes 589832 | tf_op jit(solution)/shard_map/ppermute | solution.py:22
  458.6 31.0 %collective-permute-start.12 = (bf16[24,8,512]{2,1,0:T(8,128)(2,1)}, bf16[24,8,512]{2,1,0:T(8,128)(2,1)S(1)}, u32[]{:S(2)}, u32[]{:S(2)}) collective-permute-start(bf16[24,8,512]{2,1,0:T(8,128)(2,1)} %get-tuple-element.190), channel_id=1, source_target_pairs={{2,0},{4,2},{6,4},{8,6},{10,8},{12,10},{14,12},{16,14},{18,16},{20... | collective-permute-start | bytes 589832 | tf_op jit(solution)/shard_map/ppermute | solution.py:24
  489.7 18.9 %collective-permute-start.13 = (bf16[24,32,512]{2,1,0:T(8,128)(2,1)S(1)}, bf16[24,32,512]{2,1,0:T(8,128)(2,1)S(1)}, u32[]{:S(2)}, u32[]{:S(2)}) collective-permute-start(bf16[24,32,512]{2,1,0:T(8,128)(2,1)S(1)} %pad_maximum_fusion.7), channel_id=1, source_target_pairs={{0,1},{1,0},{2,3},{3,2},{4,5},{5,4},{6,7},{7,6},{8,9},{9,8},{10,11... | collective-permute-start | bytes 2359304 | tf_op jit(solution)/shard_map/ppermute | solution.py:38
  524.5 9.8 %collective-permute-start.1 = (f32[24,16]{0,1:T(8,128)S(1)}, f32[24,16]{0,1:T(8,128)S(1)}, u32[]{:S(2)}, u32[]{:S(2)}) collective-permute-start(f32[24,16]{0,1:T(8,128)S(1)} %get-tuple-element.290), channel_id=1, source_target_pairs={{0,2},{2,4},{4,6},{6,8},{8,10},{10,12},{12,14},{14,16},{16,18},{18... | collective-permute-start | bytes 4616 | tf_op jit(solution)/shard_map/while/body/eval_jaxpr/ppermute | solution.py:44
  (67 other events, 1353.8 us)
Sparse Core Ops, SparseCore 0:
  838.0 14.2 reduce-scatter.1
where the time goes:
time: 873 us; the launch traced here: 861 us
  starting transfers between devices  398 us (46%)
  waiting for transfers between devices  366 us (42%)
  local copies, waits for them, and re-layouts  42 us (5%)
  between operations  25.6 us (3%)
  other arithmetic  14.6 us (2%)
  matrix products  13.5 us (2%)
    ppermute x64, starting transfers between devices, from_behind(): return lax.ppermute(block, axis, route)  336 us
    ppermute x64, waiting for transfers between devices, from_behind(): return lax.ppermute(block, axis, route)  294 us
    ppermute x4, waiting for transfers between devices, padded_2(): lax.ppermute(tail, axis, [(i, (i + 1) % count) for i in range(ends)])  37.5 us
    ppermute x4, starting transfers between devices, padded_2(): lax.ppermute(head, axis, [((i + 1) % count, i) for i in range(ends)])  33.8 us
    ppermute x4, starting transfers between devices, partner_2(): return lax.ppermute(block, axis, route)  20.2 us
    unnamed x69, local copies, waits for them, and re-layouts  18.7 us
    dynamic_slice x4, local copies, waits for them, and re-layouts, tap_sum(): lax.dynamic_slice(col_padded, (jnp.int32(0), row_start, col_start), (in_c...  18.1 us
  transfers between devices with their start and end apart: 77, of which 71 were waited for; matrix products, arithmetic and copies ran while one was open for 3% of the time, Pallas kernels for 0%

commit v1 on v0

v1 whole, which is shorter than its diff:
```python
import functools

import jax
import jax.numpy as jnp
from jax import lax
from jax.experimental import pallas as pl
from jax.experimental.pallas import tpu as pltpu
from jax.sharding import PartitionSpec as P

DMAX = 8
NF = 16
HALO = 2 * DMAX
LANES = 128
SHIFTS = (-2, -1, 0, 1, 2)

two_pi = 6.283185307179586
inv_sqrt2 = 0.7071067811865476
inv_sqrt_2pi = 0.3989422804014327


def encode(row_ids, start_bin, feature_count):
    octave = jnp.arange(NF, dtype=jnp.int32)
    period = jnp.power(jnp.int32(2), octave + 2).astype(jnp.int32)
    residue = jnp.remainder(start_bin + row_ids[:, None], period[None, :])
    angles = residue.astype(jnp.float32) * (two_pi / period.astype(jnp.float32))[None, :]
    encoding = jnp.concatenate((jnp.sin(angles), jnp.cos(angles)), axis=1)
    return jnp.pad(encoding, ((0, 0), (0, feature_count - 2 * NF)))


def from_ahead(block, distance):
    devices = range(lax.axis_size("chrom"))
    route = [(i + distance, i) for i in devices if i + distance in devices]
    return lax.ppermute(block, "chrom", route)


def from_partner(block):
    return lax.ppermute(block, "chan", [(0, 1), (1, 0)])


def diagonal_from_behind(block):
    count = lax.axis_size("chrom")
    route = [(2 * (i - 1) + 1 - c, 2 * i + c) for i in range(1, count) for c in range(2)]
    return lax.ppermute(block, ("chrom", "chan"), route)


def stacked_taps(kernel, sign, out_count):
    chan_count = kernel.shape[1]
    rows = []
    for m in SHIFTS:
        blocks = []
        for a in (-1, 0, 1):
            b = a + m
            if -1 <= b <= 1:
                tap = kernel[3 * (sign * a + 1) + sign * b + 1]
                blocks.append((tap if sign > 0 else tap.T)[:out_count])
            else:
                blocks.append(jnp.zeros((out_count, chan_count), kernel.dtype))
        rows.append(jnp.concatenate(blocks, axis=1))
    return jnp.concatenate(rows, axis=0)


def lane_ids():
    return lax.broadcasted_iota(jnp.int32, (1, LANES), 1)


def tiles_of(values):
    return [values[:, k : k + LANES] for k in range(0, values.shape[1], LANES)]


def pull(tiles, amount, count, lanes):
    turned = [pltpu.roll(tile, lax.rem(LANES - amount, LANES), 1) for tile in tiles]
    turned.append(jnp.zeros_like(turned[0]))
    inside = lanes < LANES - amount
    return [jnp.where(inside, turned[k], turned[k + 1]) for k in range(count)]


def push(tiles, amount, count, lanes):
    zero = jnp.zeros_like(tiles[0])
    turned = [zero] + [pltpu.roll(tile, amount, 1) for tile in tiles] + [zero]
    inside = lanes >= amount
    return [jnp.where(inside, turned[k + 1], turned[k]) for k in range(count)]


def tap_sum(weights, window, out_count, dilation, lanes):
    stacked = jnp.dot(weights, window, preferred_element_type=jnp.float32)
    part = [tiles_of(stacked[k * out_count : (k + 1) * out_count]) for k in range(5)]
    count = len(part[0])
    shifted = [
        push(part[0], 2 * dilation, count, lanes),
        push(part[1], dilation, count, lanes),
        part[2],
        pull(part[3], dilation, count, lanes),
        pull(part[4], 2 * dilation, count, lanes),
    ]
    return [sum(tile[1:], tile[0]) for tile in zip(*shifted)]


def three_rows(ref, row, dilation):
    return jnp.concatenate((ref[row - dilation], ref[row], ref[row + dilation]), axis=0)


def limit_of(row, first_row, band_width, total_rows):
    here = first_row - HALO + row
    return jnp.where(here < 0, 0, jnp.minimum(band_width, total_rows - here))


def gelu_cdf(values):
    return 0.5 + 0.5 * lax.erf(values * inv_sqrt2)


def gelu_slope(values, cdf):
    return cdf + values * (inv_sqrt_2pi * jnp.exp(-0.5 * values * values))


def forward_kernel(
    total_rows, scalars, near, far, bias, bias_0, bias_1, taps_0, taps_1,
    pair_out, slope_0, slope_1, pair_0, act_0, act_1, pair_1,
):
    band_width, first_row, step_0, step_1 = (scalars[k] for k in range(4))
    lanes = lane_ids()
    own = pair_out.shape[1]
    width = bias.shape[1]
    count = width // LANES
    rows = pair_out.shape[0]

    def keeps(row):
        limit = limit_of(row, first_row, band_width, total_rows)
        return [lanes + k * LANES < limit for k in range(count)]

    def seed(row, with_slope):
        near_col = pltpu.roll(near[...], lax.rem(LANES - row, LANES), 1)[:, 0:1]
        ahead = pull(tiles_of(far[...]), row, count, lanes)
        for k, keep in enumerate(keeps(row)):
            span = pl.ds(k * LANES, LANES)
            value = jnp.where(keep, near_col + ahead[k] + bias[:, span], 0.0)
            cdf = gelu_cdf(value)
            pair_0[row, :, span] = value
            act_0[row, :, span] = (value * cdf).astype(jnp.bfloat16)
            if with_slope:
                slope_0[row - HALO, :, span] = gelu_slope(value[:own], cdf[:own])

    def outer_seed(index, _):
        seed(jnp.where(index < HALO, index, index + rows), False)
        return 0

    def inner_seed(index, _):
        seed(index + HALO, True)
        return 0

    lax.fori_loop(0, 2 * HALO, outer_seed, 0)
    lax.fori_loop(0, rows, inner_seed, 0)

    def layer_0(index, _):
        row = index + DMAX
        conv = tap_sum(taps_0[...], three_rows(act_0, row, step_0), near.shape[0], step_0, lanes)
        for k, keep in enumerate(keeps(row)):
            span = pl.ds(k * LANES, LANES)
            value = jnp.where(keep, pair_0[row, :, span] + conv[k] + bias_0[...], 0.0)
            cdf = gelu_cdf(value)
            pair_1[index, :, span] = value[:own]
            act_1[index, :, span] = (value * cdf).astype(jnp.bfloat16)
            slope_1[index, :, span] = gelu_slope(value, cdf)
        return 0

    lax.fori_loop(0, rows + HALO, layer_0, 0)

    def layer_1(index, _):
        row = index + HALO
        conv = tap_sum(taps_1[...], three_rows(act_1, row - DMAX, step_1), own, step_1, lanes)
        for k, keep in enumerate(keeps(row)):
            span = pl.ds(k * LANES, LANES)
            value = jnp.where(keep, pair_1[row - DMAX, :, span] + conv[k] + bias_1[...], 0.0)
            pair_out[index, :, span] = value
        return 0

    lax.fori_loop(0, rows, layer_1, 0)


def backward_kernel(
    total_rows, scalars, cot_behind, cot_here, cot_ahead, slope_0, slope_1, taps_1, taps_0,
    near_sum, far_sum, grad_2, grad_1, low_1,
):
    band_width, first_row, step_0, step_1 = (scalars[k] for k in range(4))
    lanes = lane_ids()
    rows, chans, width = cot_here.shape
    own = slope_0.shape[1]
    count = width // LANES

    def keeps(row):
        limit = limit_of(row, first_row, band_width, total_rows)
        return [lanes + k * LANES < limit for k in range(count)]

    def lay(index, _):
        grad_2[index] = cot_behind[index]
        grad_2[index + rows] = cot_here[index]
        grad_2[index + 2 * rows] = cot_ahead[index]
        return 0

    lax.fori_loop(0, rows, lay, 0)

    def layer_1(index, _):
        row = index + DMAX
        conv = tap_sum(taps_1[...], three_rows(grad_2, row, step_1), chans, step_1, lanes)
        for k, keep in enumerate(keeps(row)):
            span = pl.ds(k * LANES, LANES)
            above = grad_2[row, :, span].astype(jnp.float32)
            value = jnp.where(keep, above + slope_1[index, :, span] * conv[k], 0.0)
            grad_1[index, :, span] = value[:own]
            low_1[index, :, span] = value.astype(jnp.bfloat16)
        return 0

    lax.fori_loop(0, rows + HALO, layer_1, 0)

    near_sum[...] = jnp.zeros_like(near_sum)
    far_sum[...] = jnp.zeros_like(far_sum)

    def layer_0(index, _):
        row = index + HALO
        conv = tap_sum(taps_0[...], three_rows(low_1, row - DMAX, step_0), own, step_0, lanes)
        values = []
        for k, keep in enumerate(keeps(row)):
            span = pl.ds(k * LANES, LANES)
            values.append(
                jnp.where(keep, grad_1[row - DMAX, :, span] + slope_0[index, :, span] * conv[k], 0.0)
            )
        total = jnp.sum(sum(values[1:], values[0]), axis=1, keepdims=True)
        near_sum[...] += jnp.where(lanes == index, total, 0.0)
        for k, tile in enumerate(push(values, index, count + 1, lanes)):
            far_sum[:, k * LANES : (k + 1) * LANES] += tile
        return 0

    lax.fori_loop(0, rows, layer_0, 0)


def call(kernel, out_shapes, scratch, flops, smem, *arrays):
    bytes_accessed = sum(a.size * a.dtype.itemsize for a in arrays)
    bytes_accessed += sum(s.size * s.dtype.itemsize for s in out_shapes)
    vmem = pl.BlockSpec(memory_space=pltpu.VMEM)
    return pl.pallas_call(
        kernel,
        out_shape=out_shapes,
        in_specs=[pl.BlockSpec(memory_space=pltpu.SMEM)] + [vmem] * len(arrays),
        out_specs=[vmem] * len(out_shapes),
        scratch_shapes=scratch,
        compiler_params=pltpu.CompilerParams(vmem_limit_bytes=40 * 2**20),
        cost_estimate=pl.CostEstimate(
            flops=flops, bytes_accessed=bytes_accessed, transcendentals=0
        ),
    )(smem, *arrays)


def gather_band(far, distance_blocks, rows_here):
    behind = from_ahead(far, -1)
    held = jnp.concatenate((far, from_ahead(far, 1)), axis=0)
    beyond = from_ahead(held, distance_blocks)
    step = 2
    while step < distance_blocks:
        held = jnp.concatenate((held, from_ahead(held, step)), axis=0)
        step *= 2
    return jnp.concatenate((behind, held, beyond), axis=0)


def return_band(partial, distance_blocks, rows_here):
    last = partial[distance_blocks * rows_here :]
    held = partial[: distance_blocks * rows_here]
    from_last = from_ahead(last, -distance_blocks)
    step = distance_blocks // 2
    while step > 1:
        cut = step * rows_here
        held = held[:cut] + from_ahead(held[cut:], -step)
        step //= 2
    return held[:rows_here] + from_last, held[rows_here:]


def shards(
    embedding, window_start, band_width, dilations, near_weight, far_weight,
    distance_bias, conv_weight, conv_bias, cotangent,
):
    rows = embedding.shape[0]
    own, width = distance_bias.shape
    blocks = width // rows
    chans = conv_weight.shape[2]
    features_half = embedding.shape[1] // 2
    chan = lax.axis_index("chan")
    first_row = lax.axis_index("chrom") * rows
    total_rows = lax.axis_size("chrom") * rows
    row_ids = first_row + jnp.arange(rows, dtype=jnp.int32)
    scalars = jnp.stack([band_width[0], first_row, dilations[0], dilations[1]]).astype(jnp.int32)

    cot_other = from_partner(cotangent)

    features = (
        embedding.astype(jnp.float32) + encode(row_ids, window_start[0], embedding.shape[1])
    ).astype(jnp.bfloat16)
    both = jnp.concatenate((near_weight, far_weight), axis=1)
    proj = jnp.dot(features, both, preferred_element_type=jnp.float32)
    proj_other = from_partner(proj)
    near = jnp.concatenate((proj[:, :own], proj_other[:, :own]), axis=1)
    far = jnp.concatenate((proj[:, own:], proj_other[:, own:]), axis=1)
    near_band = jnp.concatenate((from_ahead(near, -1), near, from_ahead(near, 1)), axis=0)
    far_band = gather_band(far, blocks, rows)
    near_t = jnp.pad(near_band.T, ((0, 0), (0, LANES - 3 * rows)))
    far_t = jnp.pad(far_band.T, ((0, 0), (0, width + LANES - far_band.shape[0])))

    small = jnp.concatenate((distance_bias, conv_bias.T, jnp.zeros((own, LANES - 2), jnp.float32)), axis=1)
    small = jnp.concatenate((small, from_partner(small)), axis=0)
    bias = small[:, :width]
    both_other = from_partner(lax.dynamic_slice_in_dim(both, (1 - chan) * features_half, features_half, 0))
    both_here = lax.dynamic_slice_in_dim(both, chan * features_half, features_half, 0)
    near_cols = jnp.concatenate((both_here[:, :own], both_other[:, :own]), axis=1)
    far_cols = jnp.concatenate((both_here[:, own:], both_other[:, own:]), axis=1)

    twice = jnp.concatenate((conv_weight, conv_weight), axis=2)
    twice = jnp.concatenate((twice, twice), axis=3)
    turned = lax.dynamic_slice(
        twice, (0, 0, chan * own, chan * own), conv_weight.shape
    )
    pad_rows = lambda taps: jnp.pad(taps, ((0, -taps.shape[0] % 16), (0, 0)))
    ahead_0 = stacked_taps(turned[0], 1, chans)
    ahead_1 = pad_rows(stacked_taps(turned[1], 1, own))
    back_1 = stacked_taps(turned[1], -1, chans)
    back_0 = pad_rows(stacked_taps(turned[0], -1, own))

    per_row = 2 * 15 * chans * chans * width
    f32 = functools.partial(jax.ShapeDtypeStruct, dtype=jnp.float32)
    pair_rows, slope_0, slope_1 = call(
        functools.partial(forward_kernel, total_rows),
        (f32((rows, own, width)), f32((rows, own, width)), f32((rows + HALO, chans, width))),
        [
            pltpu.VMEM((rows + 2 * HALO, chans, width), jnp.float32),
            pltpu.VMEM((rows + 2 * HALO, chans, width), jnp.bfloat16),
            pltpu.VMEM((rows + HALO, chans, width), jnp.bfloat16),
            pltpu.VMEM((rows + HALO, own, width), jnp.float32),
        ],
        per_row * 40,
        scalars, near_t, far_t, bias, small[:, width : width + 1], small[:own, width + 1 : width + 2],
        ahead_0, ahead_1,
    )
    pair_out = jnp.swapaxes(pair_rows.astype(jnp.bfloat16), 0, 1)

    offsets = jnp.arange(width, dtype=jnp.int32)
    keep = (offsets[None, :] < band_width[0]) & (row_ids[:, None] + offsets[None, :] < total_rows)
    cot = jnp.concatenate((cotangent, cot_other), axis=0)
    cot = jnp.where(keep[:, None, :], jnp.swapaxes(cot, 0, 1), 0).astype(jnp.bfloat16)
    cot_behind = from_ahead(cot, -1)
    cot_ahead = from_ahead(cot, 1)
    near_sum, far_sum = call(
        functools.partial(backward_kernel, total_rows),
        (f32((own, LANES)), f32((own, width + LANES))),
        [
            pltpu.VMEM((rows + 2 * HALO, chans, width), jnp.bfloat16),
            pltpu.VMEM((rows + HALO, own, width), jnp.float32),
            pltpu.VMEM((rows + HALO, chans, width), jnp.bfloat16),
        ],
        per_row * 40,
        scalars, cot_behind, cot, cot_ahead, slope_0, slope_1, back_1, back_0,
    )
    far_terms = far_sum[:, : width + rows].T
    grad_near = near_sum[:, :rows].T
    here, onward = return_band(far_terms, blocks, rows)
    near_here = jnp.concatenate((here, grad_near), axis=1)
    other = from_partner(near_here)
    grad_far = here + from_ahead(onward, -1)
    grad_far_other = other[:, :own] + diagonal_from_behind(onward)
    near_low = jnp.concatenate((grad_near, other[:, own:]), axis=1).astype(jnp.bfloat16)
    far_low = jnp.concatenate((grad_far, grad_far_other), axis=1).astype(jnp.bfloat16)
    lows = jnp.concatenate((near_low, far_low), axis=1)
    cols = jnp.concatenate((near_cols, far_cols), axis=1)
    embedding_grad = lax.dot_general(
        lows, cols, (((1,), (1,)), ((), ())), preferred_element_type=jnp.float32
    ).astype(jnp.bfloat16)
    return (pair_out, embedding_grad)


def solution(mesh):
    in_specs = (
        P("chrom", None),
        P(),
        P(),
        P(),
        P(None, "chan"),
        P(None, "chan"),
        P("chan", None),
        P(),
        P(None, "chan"),
        P("chan", "chrom", None),
    )
    out_specs = (P("chan", "chrom", None), P("chrom", "chan"))
    return jax.shard_map(shards, mesh=mesh, in_specs=in_specs, out_specs=out_specs, check_vma=False)
```

time: 873 us -> 208 us (0.24); the launches traced: 861 us -> 206 us
  waiting for transfers between devices: 366 us -> 42.3 us
  starting transfers between devices: 398 us -> 98.8 us
  Pallas kernels: 0 us -> 42.6 us
  local copies, waits for them, and re-layouts: 42 us -> 13.8 us
  between operations: 25.6 us -> 2.64 us
  matrix products: 13.5 us -> 1.67 us
  other arithmetic: 14.6 us -> 4.67 us
    ppermute x76 -> x23, waiting for transfers between devices: 352 us -> 42.3 us  [the longest x17 37.7 us: from_ahead(): return lax.ppermute(block, 'chrom', route)]
    ppermute x76 -> x23, starting transfers between devices: 398 us -> 98.8 us  [the longest x17 69.6 us: from_ahead(): return lax.ppermute(block, 'chrom', route)]
    pallas_call x0 -> x2, Pallas kernels: none -> 42.6 us  [call(): pl.pallas_call(kernel, out_shape=out_shapes, in_specs=[pl.BlockSpec(memor...]
    dynamic_slice x5 -> x1, local copies, waits for them, and re-layouts: 18.3 us -> 0.01 us  [shards(): lax.dynamic_slice_in_dim(both, (1 - chan) * features_half, features_half, 0)]
    reduce_scatter x1 -> x0, waiting for transfers between devices: 14.4 us -> none  [shards(): lax.psum_scatter(partial_grad, 'chan', scatter_dimension=1, tiled=True)]
    dot_general x40 -> x2, matrix products: 13.5 us -> 1.67 us  [the longest x1 0.86 us: shards(): proj = jnp.dot(features, both, preferred_element_type=jnp.float32)]
    unnamed x69 -> x30, local copies, waits for them, and re-layouts: 18.7 us -> 8.94 us
  transfers between devices with their start and end apart: 77 -> 23, of which waited for: 71 -> 10; matrix products, arithmetic and copies ran while one was open for 3% -> 6% of each run, Pallas kernels for 0% -> 12%
where the time goes in v1:
time: 208 us; the launch traced here: 206 us
  starting transfers between devices  98.8 us (48%)
  Pallas kernels  42.6 us (20%)
  waiting for transfers between devices  42.3 us (20%)
  local copies, waits for them, and re-layouts  13.8 us (7%)
  other arithmetic  4.67 us (2%)
  between operations  2.64 us (1%)
    ppermute x17, starting transfers between devices, from_ahead(): return lax.ppermute(block, 'chrom', route)  69.6 us
    pallas_call x2, Pallas kernels, call(): pl.pallas_call(kernel, out_shape=out_shapes, in_specs=[pl.BlockSpec(memor...  42.6 us
    ppermute x17, waiting for transfers between devices, from_ahead(): return lax.ppermute(block, 'chrom', route)  37.7 us
    ppermute x5, starting transfers between devices, from_partner(): return lax.ppermute(block, 'chan', [(0, 1), (1, 0)])  27.3 us
    unnamed x30, local copies, waits for them, and re-layouts  8.94 us
    ppermute x5, waiting for transfers between devices, from_partner(): return lax.ppermute(block, 'chan', [(0, 1), (1, 0)])  4.53 us
  transfers between devices with their start and end apart: 23, of which 10 were waited for; matrix products, arithmetic and copies ran while one was open for 6% of the time, Pallas kernels for 12%

profile of v1, /device:TPU:6, one launch (start us, length us, event | category | flops | bytes accessed | tf_op | source)
XLA Modules:
  0.0 206.5 jit_solution(6580932464879324725)
XLA Ops:
  3.9 7.8 %collective-permute-start = (f32[16,48]{1,0:T(8,128)S(1)}, f32[16,48]{1,0:T(8,128)S(1)}, u32[]{:S(2)}, u32[]{:S(2)}) collective-permute-start(f32[16,48]{1,0:T(8,128)S(1)} %fusion.16), channel_id=1, source_target_pairs={{0,1},{1,0},{2,3},{3,2},{4,5},{5,4},{6,7},{7,6},{8,9},{9,8},{10,11... | collective-permute-start | bytes 9224 | tf_op jit(solution)/shard_map/ppermute | solution.py:37
  13.4 2.0 collective-permute-start.10
  16.6 7.7 %collective-permute-start.11 = (bf16[24,16,512]{2,0,1:T(8,128)(2,1)S(1)}, bf16[24,16,512]{2,0,1:T(8,128)(2,1)S(1)}, u32[]{:S(2)}, u32[]{:S(2)}) collective-permute-start(bf16[24,16,512]{2,0,1:T(8,128)(2,1)S(1)} %copy.132), channel_id=1, source_target_pairs={{0,1},{1,0},{2,3},{3,2},{4,5},{5,4},{6,7},{7,6},{8,9},{9,8},{10,11... | collective-permute-start | bytes 1179656 | tf_op jit(solution)/shard_map/ppermute | solution.py:37
  28.9 10.1 %collective-permute-start.4 = (f32[16,48]{0,1:T(8,128)S(1)}, f32[16,48]{0,1:T(8,128)S(1)}, u32[]{:S(2)}, u32[]{:S(2)}) collective-permute-start(f32[16,48]{0,1:T(8,128)S(1)} %copy.113), channel_id=1, source_target_pairs={{2,0},{4,2},{6,4},{8,6},{10,8},{12,10},{14,12},{16,14},{18,16},{20... | collective-permute-start | bytes 9224 | tf_op jit(solution)/shard_map/ppermute | solution.py:33
  41.9 10.7 %collective-permute-start.5 = (f32[32,48]{0,1:T(8,128)S(1)}, f32[32,48]{0,1:T(8,128)S(1)}, u32[]{:S(2)}, u32[]{:S(2)}) collective-permute-start(f32[32,48]{0,1:T(8,128)S(1)} %pad_maximum_fusion.11), channel_id=1, source_target_pairs={{4,0},{6,2},{8,4},{10,6},{12,8},{14,10},{16,12},{18,14},{20,16},{2... | collective-permute-start | bytes 18440 | tf_op jit(solution)/shard_map/ppermute | solution.py:33
  52.8 1.9 collective-permute-start.12
  54.7 8.4 %collective-permute-start.13 = (bf16[16,48,512]{2,1,0:T(8,128)(2,1)S(1)}, bf16[16,48,512]{2,1,0:T(8,128)(2,1)S(1)}, u32[]{:S(2)}, u32[]{:S(2)}) collective-permute-start(bf16[16,48,512]{2,1,0:T(8,128)(2,1)S(1)} %fusion.cot_here), channel_id=1, source_target_pairs={{2,0},{4,2},{6,4},{8,6},{10,8},{12,10},{14,12},{16,14},{18,16},{20... | collective-permute-start | bytes 2359304 | tf_op jit(solution)/shard_map/ppermute | solution.py:33
  67.2 6.0 %collective-permute-done.6 = f32[64,48]{0,1:T(8,128)S(1)} collective-permute-done((f32[64,48]{0,1:T(8,128)S(1)}, f32[64,48]{0,1:T(8,128)S(1)}, u32[]{:S(2)}, u32[]{:S(2)}) %collective-permute-start.6) | collective-permute-done | bytes 12320 | tf_op jit(solution)/shard_map/ppermute | solution.py:33
  75.2 1.9 collective-permute-start.3
  77.2 6.0 %collective-permute-done.1 = f32[16,48]{0,1:T(8,128)S(1)} collective-permute-done((f32[16,48]{0,1:T(8,128)S(1)}, f32[16,48]{0,1:T(8,128)S(1)}, u32[]{:S(2)}, u32[]{:S(2)}) %collective-permute-start.1) | collective-permute-done | bytes 3104 | tf_op jit(solution)/shard_map/ppermute | solution.py:33
  83.2 3.4 %collective-permute-start.7 = (f32[128,48]{0,1:T(8,128)S(1)}, f32[128,48]{0,1:T(8,128)S(1)}, u32[]{:S(2)}, u32[]{:S(2)}) collective-permute-start(f32[128,48]{0,1:T(8,128)S(1)} %pad_maximum_fusion.13), channel_id=1, source_target_pairs={{16,0},{18,2},{20,4},{22,6},{24,8},{26,10},{28,12},{30,14},{32,16}... | collective-permute-start | bytes 73736 | tf_op jit(solution)/shard_map/ppermute | solution.py:33
  88.9 6.7 %collective-permute-start.9 = (f32[32,48]{0,1:T(8,128)S(1)}, f32[32,48]{0,1:T(8,128)S(1)}, u32[]{:S(2)}, u32[]{:S(2)}) collective-permute-start(f32[32,48]{0,1:T(8,128)S(1)} %pad_maximum_fusion.11), channel_id=1, source_target_pairs={{64,0},{66,2},{68,4},{70,6},{72,8},{74,10},{76,12},{78,14},{80,16}... | collective-permute-start | bytes 18440 | tf_op jit(solution)/shard_map/ppermute | solution.py:33
  98.5 4.4 %collective-permute-done.8 = f32[256,48]{0,1:T(8,128)S(1)} collective-permute-done((f32[256,48]{0,1:T(8,128)S(1)}, f32[256,48]{0,1:T(8,128)S(1)}, u32[]{:S(2)}, u32[]{:S(2)}) %collective-permute-start.8) | collective-permute-done | bytes 49184 | tf_op jit(solution)/shard_map/ppermute | solution.py:33
  106.6 25.2 %shard_map.113 = (f32[16,24,512]{2,1,0:T(8,128)S(1)}, f32[16,24,512]{2,1,0:T(8,128)S(1)}, f32[32,48,512]{2,1,0:T(8,128)S(1)}) custom-call(s32[4]{0:T(128)S(1)} %copy-done.4, f32[48,128]{1,0:T(8,128)S(1)} %copy-done.2, f32[48,640]{1,0:T(8,128)S(1)} %pad.29.far, f32[48,512]{1,0:T(8,128)S(1)} %slice.362.bias, f32[48,1]{1,0:T(8,128)S(1)} %copy-done.1, ...), custom_call_target="tpu_custom_call" | custom-call | flops 1415577600 | bytes 5070624 | tf_op jit(solution)/shard_map/pallas_call | solution.py:239
  131.8 17.4 %shard_map.114 = (f32[24,128]{1,0:T(8,128)S(1)}, f32[24,640]{1,0:T(8,128)S(1)}) custom-call(s32[4]{0:T(128)S(1)} %copy-done.4, bf16[16,48,512]{2,1,0:T(8,128)(2,1)S(1)} %collective-permute-done.12.cot_behind, bf16[16,48,512]{2,1,0:T(8,128)(2,1)S(1)} %fusion.cot_here, bf16[16,48,512]{2,1,0:T(8,128)(2,1)S(1)} %collective-permute-done.13.cot_ahead, ...), custom_call_target="tpu_custom_call" | custom-call | flops 1415577600 | bytes 6471168 | tf_op jit(solution)/shard_map/pallas_call | solution.py:239
  149.3 4.0 %collective-permute-start.14 = (f32[256,24]{0,1:T(8,128)S(1)}, f32[256,24]{0,1:T(8,128)S(1)}, u32[]{:S(2)}, u32[]{:S(2)}) collective-permute-start(f32[256,24]{0,1:T(8,128)S(1)} %slice.401), channel_id=1, source_target_pairs={{0,32},{2,34},{4,36},{6,38},{8,40},{10,42},{12,44},{14,46},{16,48}... | collective-permute-start | bytes 73736 | tf_op jit(solution)/shard_map/ppermute | solution.py:33
  153.3 4.8 %collective-permute-start.22 = (bf16[256,48]{0,1:T(8,128)(2,1)S(1)}, bf16[256,48]{0,1:T(8,128)(2,1)S(1)}, u32[]{:S(2)}, u32[]{:S(2)}) collective-permute-start(bf16[256,48]{0,1:T(8,128)(2,1)S(1)} %constant_dynamic-slice_fusion), channel_id=1, source_target_pairs={{0,1},{1,0},{2,3},{3,2},{4,5},{5,4},{6,7},{7,6},{8,9},{9,8},{10,11... | collective-permute-start | bytes 73736 | tf_op jit(solution)/shard_map/ppermute | solution.py:37
  158.2 6.0 %collective-permute-start.15 = (f32[128,24]{0,1:T(8,128)S(1)}, f32[128,24]{0,1:T(8,128)S(1)}, u32[]{:S(2)}, u32[]{:S(2)}) collective-permute-start(f32[128,24]{0,1:T(8,128)S(1)} %slice.403), channel_id=1, source_target_pairs={{0,16},{2,18},{4,20},{6,22},{8,24},{10,26},{12,28},{14,30},{16,32}... | collective-permute-start | bytes 36872 | tf_op jit(solution)/shard_map/ppermute | solution.py:33
  167.9 7.5 %collective-permute-done.16 = f32[64,24]{0,1:T(8,128)S(1)} collective-permute-done((f32[64,24]{0,1:T(8,128)S(1)}, f32[64,24]{0,1:T(8,128)S(1)}, u32[]{:S(2)}, u32[]{:S(2)}) %collective-permute-start.16) | collective-permute-done | bytes 6176 | tf_op jit(solution)/shard_map/ppermute | solution.py:33
  178.4 3.1 %collective-permute-start.18 = (f32[16,24]{0,1:T(8,128)S(1)}, f32[16,24]{0,1:T(8,128)S(1)}, u32[]{:S(2)}, u32[]{:S(2)}) collective-permute-start(f32[16,24]{0,1:T(8,128)S(1)} %slice.409), channel_id=1, source_target_pairs={{0,64},{2,66},{4,68},{6,70},{8,72},{10,74},{12,76},{14,78},{16,80}... | collective-permute-start | bytes 4616 | tf_op jit(solution)/shard_map/ppermute | solution.py:33
  181.5 4.5 %collective-permute-done.17 = f32[32,24]{0,1:T(8,128)S(1)} collective-permute-done((f32[32,24]{0,1:T(8,128)S(1)}, f32[32,24]{0,1:T(8,128)S(1)}, u32[]{:S(2)}, u32[]{:S(2)}) %collective-permute-start.17) | collective-permute-done | bytes 3104 | tf_op jit(solution)/shard_map/ppermute | solution.py:33
  189.9 5.9 %collective-permute-done.20 = f32[16,24]{0,1:T(8,128)S(1)} collective-permute-done((f32[16,24]{0,1:T(8,128)S(1)}, f32[16,24]{0,1:T(8,128)S(1)}, u32[]{:S(2)}, u32[]{:S(2)}) %collective-permute-start.20) | collective-permute-done | bytes 1568 | tf_op jit(solution)/shard_map/ppermute | solution.py:33
  195.8 4.9 %collective-permute-start.19 = (f32[16,48]{0,1:T(8,128)S(1)}, f32[16,48]{0,1:T(8,128)S(1)}, u32[]{:S(2)}, u32[]{:S(2)}) collective-permute-start(f32[16,48]{0,1:T(8,128)S(1)} %pad_maximum_fusion.14), channel_id=1, source_target_pairs={{0,1},{1,0},{2,3},{3,2},{4,5},{5,4},{6,7},{7,6},{8,9},{9,8},{10,11... | collective-permute-start | bytes 9224 | tf_op jit(solution)/shard_map/ppermute | solution.py:37
  200.9 4.5 %collective-permute-done.19 = f32[16,48]{0,1:T(8,128)S(1)} collective-permute-done((f32[16,48]{0,1:T(8,128)S(1)}, f32[16,48]{0,1:T(8,128)S(1)}, u32[]{:S(2)}, u32[]{:S(2)}) %collective-permute-start.19) | collective-permute-done | bytes 3104 | tf_op jit(solution)/shard_map/ppermute | solution.py:37
  (148 shorter events, 38.9 us)
Async XLA Ops:
  3.9 24.7 %collective-permute-start = (f32[16,48]{1,0:T(8,128)S(1)}, f32[16,48]{1,0:T(8,128)S(1)}, u32[]{:S(2)}, u32[]{:S(2)}) collective-permute-start(f32[16,48]{1,0:T(8,128)S(1)} %fusion.16), channel_id=1, source_target_pairs={{0,1},{1,0},{2,3},{3,2},{4,5},{5,4},{6,7},{7,6},{8,9},{9,8},{10,11... | collective-permute-start | bytes 9224 | tf_op jit(solution)/shard_map/ppermute | solution.py:37
  13.4 82.3 %collective-permute-start.10 = (f32[24,640]{1,0:T(8,128)S(1)}, f32[24,640]{1,0:T(8,128)S(1)}, u32[]{:S(2)}, u32[]{:S(2)}) collective-permute-start(f32[24,640]{1,0:T(8,128)S(1)} %pad_maximum_fusion.1), channel_id=1, source_target_pairs={{0,1},{1,0},{2,3},{3,2},{4,5},{5,4},{6,7},{7,6},{8,9},{9,8},{10,11... | collective-permute-start | bytes 184328 | tf_op jit(solution)/shard_map/ppermute | solution.py:37
  16.6 36.0 %collective-permute-start.11 = (bf16[24,16,512]{2,0,1:T(8,128)(2,1)S(1)}, bf16[24,16,512]{2,0,1:T(8,128)(2,1)S(1)}, u32[]{:S(2)}, u32[]{:S(2)}) collective-permute-start(bf16[24,16,512]{2,0,1:T(8,128)(2,1)S(1)} %copy.132), channel_id=1, source_target_pairs={{0,1},{1,0},{2,3},{3,2},{4,5},{5,4},{6,7},{7,6},{8,9},{9,8},{10,11... | collective-permute-start | bytes 1179656 | tf_op jit(solution)/shard_map/ppermute | solution.py:37
  28.9 12.9 %collective-permute-start.4 = (f32[16,48]{0,1:T(8,128)S(1)}, f32[16,48]{0,1:T(8,128)S(1)}, u32[]{:S(2)}, u32[]{:S(2)}) collective-permute-start(f32[16,48]{0,1:T(8,128)S(1)} %copy.113), channel_id=1, source_target_pairs={{2,0},{4,2},{6,4},{8,6},{10,8},{12,10},{14,12},{16,14},{18,16},{20... | collective-permute-start | bytes 9224 | tf_op jit(solution)/shard_map/ppermute | solution.py:33
  40.7 56.9 %copy-start.5 = (f32[24,512]{1,0:T(8,128)S(1)}, f32[24,512]{1,0:T(8,128)}, u32[]{:S(2)}) copy-start(f32[24,512]{1,0:T(8,128)} %param.16) | copy-start | bytes 147460
  41.9 21.3 %collective-permute-start.5 = (f32[32,48]{0,1:T(8,128)S(1)}, f32[32,48]{0,1:T(8,128)S(1)}, u32[]{:S(2)}, u32[]{:S(2)}) collective-permute-start(f32[32,48]{0,1:T(8,128)S(1)} %pad_maximum_fusion.11), channel_id=1, source_target_pairs={{4,0},{6,2},{8,4},{10,6},{12,8},{14,10},{16,12},{18,14},{20,16},{2... | collective-permute-start | bytes 18440 | tf_op jit(solution)/shard_map/ppermute | solution.py:33
  52.8 79.0 %collective-permute-start.12 = (bf16[16,48,512]{2,1,0:T(8,128)(2,1)S(1)}, bf16[16,48,512]{2,1,0:T(8,128)(2,1)S(1)}, u32[]{:S(2)}, u32[]{:S(2)}) collective-permute-start(bf16[16,48,512]{2,1,0:T(8,128)(2,1)S(1)} %fusion.cot_here), channel_id=1, source_target_pairs={{0,2},{2,4},{4,6},{6,8},{8,10},{10,12},{12,14},{14,16},{16,18},{18... | collective-permute-start | bytes 2359304 | tf_op jit(solution)/shard_map/ppermute | solution.py:33
  54.7 77.1 %collective-permute-start.13 = (bf16[16,48,512]{2,1,0:T(8,128)(2,1)S(1)}, bf16[16,48,512]{2,1,0:T(8,128)(2,1)S(1)}, u32[]{:S(2)}, u32[]{:S(2)}) collective-permute-start(bf16[16,48,512]{2,1,0:T(8,128)(2,1)S(1)} %fusion.cot_here), channel_id=1, source_target_pairs={{2,0},{4,2},{6,4},{8,6},{10,8},{12,10},{14,12},{16,14},{18,16},{20... | collective-permute-start | bytes 2359304 | tf_op jit(solution)/shard_map/ppermute | solution.py:33
  63.2 10.0 %collective-permute-start.6 = (f32[64,48]{0,1:T(8,128)S(1)}, f32[64,48]{0,1:T(8,128)S(1)}, u32[]{:S(2)}, u32[]{:S(2)}) collective-permute-start(f32[64,48]{0,1:T(8,128)S(1)} %pad_maximum_fusion.12), channel_id=1, source_target_pairs={{8,0},{10,2},{12,4},{14,6},{16,8},{18,10},{20,12},{22,14},{24,16},... | collective-permute-start | bytes 36872 | tf_op jit(solution)/shard_map/ppermute | solution.py:33
  65.3 9.9 %collective-permute-start.2 = (f32[16,48]{0,1:T(8,128)S(1)}, f32[16,48]{0,1:T(8,128)S(1)}, u32[]{:S(2)}, u32[]{:S(2)}) collective-permute-start(f32[16,48]{0,1:T(8,128)S(1)} %copy.110), channel_id=1, source_target_pairs={{2,0},{4,2},{6,4},{8,6},{10,8},{12,10},{14,12},{16,14},{18,16},{20... | collective-permute-start | bytes 9224 | tf_op jit(solution)/shard_map/ppermute | solution.py:33
  73.2 9.9 %collective-permute-start.1 = (f32[16,48]{0,1:T(8,128)S(1)}, f32[16,48]{0,1:T(8,128)S(1)}, u32[]{:S(2)}, u32[]{:S(2)}) collective-permute-start(f32[16,48]{0,1:T(8,128)S(1)} %copy.110), channel_id=1, source_target_pairs={{0,2},{2,4},{4,6},{6,8},{8,10},{10,12},{12,14},{14,16},{16,18},{18... | collective-permute-start | bytes 9224 | tf_op jit(solution)/shard_map/ppermute | solution.py:33
  75.2 23.1 %collective-permute-start.3 = (f32[16,48]{0,1:T(8,128)S(1)}, f32[16,48]{0,1:T(8,128)S(1)}, u32[]{:S(2)}, u32[]{:S(2)}) collective-permute-start(f32[16,48]{0,1:T(8,128)S(1)} %copy.113), channel_id=1, source_target_pairs={{0,2},{2,4},{4,6},{6,8},{8,10},{10,12},{12,14},{14,16},{16,18},{18... | collective-permute-start | bytes 9224 | tf_op jit(solution)/shard_map/ppermute | solution.py:33
  83.2 5.7 %collective-permute-start.7 = (f32[128,48]{0,1:T(8,128)S(1)}, f32[128,48]{0,1:T(8,128)S(1)}, u32[]{:S(2)}, u32[]{:S(2)}) collective-permute-start(f32[128,48]{0,1:T(8,128)S(1)} %pad_maximum_fusion.13), channel_id=1, source_target_pairs={{16,0},{18,2},{20,4},{22,6},{24,8},{26,10},{28,12},{30,14},{32,16}... | collective-permute-start | bytes 73736 | tf_op jit(solution)/shard_map/ppermute | solution.py:33
  88.9 9.6 %collective-permute-start.9 = (f32[32,48]{0,1:T(8,128)S(1)}, f32[32,48]{0,1:T(8,128)S(1)}, u32[]{:S(2)}, u32[]{:S(2)}) collective-permute-start(f32[32,48]{0,1:T(8,128)S(1)} %pad_maximum_fusion.11), channel_id=1, source_target_pairs={{64,0},{66,2},{68,4},{70,6},{72,8},{74,10},{76,12},{78,14},{80,16}... | collective-permute-start | bytes 18440 | tf_op jit(solution)/shard_map/ppermute | solution.py:33
  95.7 7.2 %collective-permute-start.8 = (f32[256,48]{0,1:T(8,128)S(1)}, f32[256,48]{0,1:T(8,128)S(1)}, u32[]{:S(2)}, u32[]{:S(2)}) collective-permute-start(f32[256,48]{0,1:T(8,128)S(1)} %concatenate.143), channel_id=1, source_target_pairs={{32,0},{34,2},{36,4},{38,6},{40,8},{42,10},{44,12},{46,14},{48,16}... | collective-permute-start | bytes 147464 | tf_op jit(solution)/shard_map/ppermute | solution.py:33
  149.3 8.9 %collective-permute-start.14 = (f32[256,24]{0,1:T(8,128)S(1)}, f32[256,24]{0,1:T(8,128)S(1)}, u32[]{:S(2)}, u32[]{:S(2)}) collective-permute-start(f32[256,24]{0,1:T(8,128)S(1)} %slice.401), channel_id=1, source_target_pairs={{0,32},{2,34},{4,36},{6,38},{8,40},{10,42},{12,44},{14,46},{16,48}... | collective-permute-start | bytes 73736 | tf_op jit(solution)/shard_map/ppermute | solution.py:33
  153.3 14.6 %collective-permute-start.22 = (bf16[256,48]{0,1:T(8,128)(2,1)S(1)}, bf16[256,48]{0,1:T(8,128)(2,1)S(1)}, u32[]{:S(2)}, u32[]{:S(2)}) collective-permute-start(bf16[256,48]{0,1:T(8,128)(2,1)S(1)} %constant_dynamic-slice_fusion), channel_id=1, source_target_pairs={{0,1},{1,0},{2,3},{3,2},{4,5},{5,4},{6,7},{7,6},{8,9},{9,8},{10,11... | collective-permute-start | bytes 73736 | tf_op jit(solution)/shard_map/ppermute | solution.py:37
  158.2 7.7 %collective-permute-start.15 = (f32[128,24]{0,1:T(8,128)S(1)}, f32[128,24]{0,1:T(8,128)S(1)}, u32[]{:S(2)}, u32[]{:S(2)}) collective-permute-start(f32[128,24]{0,1:T(8,128)S(1)} %slice.403), channel_id=1, source_target_pairs={{0,16},{2,18},{4,20},{6,22},{8,24},{10,26},{12,28},{14,30},{16,32}... | collective-permute-start | bytes 36872 | tf_op jit(solution)/shard_map/ppermute | solution.py:33
  166.0 9.5 %collective-permute-start.16 = (f32[64,24]{0,1:T(8,128)S(1)}, f32[64,24]{0,1:T(8,128)S(1)}, u32[]{:S(2)}, u32[]{:S(2)}) collective-permute-start(f32[64,24]{0,1:T(8,128)S(1)} %slice.405), channel_id=1, source_target_pairs={{0,8},{2,10},{4,12},{6,14},{8,16},{10,18},{12,20},{14,22},{16,24},... | collective-permute-start | bytes 18440 | tf_op jit(solution)/shard_map/ppermute | solution.py:33
  175.5 10.4 %collective-permute-start.17 = (f32[32,24]{0,1:T(8,128)S(1)}, f32[32,24]{0,1:T(8,128)S(1)}, u32[]{:S(2)}, u32[]{:S(2)}) collective-permute-start(f32[32,24]{0,1:T(8,128)S(1)} %slice.407), channel_id=1, source_target_pairs={{0,4},{2,6},{4,8},{6,10},{8,12},{10,14},{12,16},{14,18},{16,20},{1... | collective-permute-start | bytes 9224 | tf_op jit(solution)/shard_map/ppermute | solution.py:33
  178.4 11.5 %collective-permute-start.18 = (f32[16,24]{0,1:T(8,128)S(1)}, f32[16,24]{0,1:T(8,128)S(1)}, u32[]{:S(2)}, u32[]{:S(2)}) collective-permute-start(f32[16,24]{0,1:T(8,128)S(1)} %slice.409), channel_id=1, source_target_pairs={{0,64},{2,66},{4,68},{6,70},{8,72},{10,74},{12,76},{14,78},{16,80}... | collective-permute-start | bytes 4616 | tf_op jit(solution)/shard_map/ppermute | solution.py:33
  186.0 9.8 %collective-permute-start.20 = (f32[16,24]{0,1:T(8,128)S(1)}, f32[16,24]{0,1:T(8,128)S(1)}, u32[]{:S(2)}, u32[]{:S(2)}) collective-permute-start(f32[16,24]{0,1:T(8,128)S(1)} %slice.411), channel_id=1, source_target_pairs={{0,2},{2,4},{4,6},{6,8},{8,10},{10,12},{12,14},{14,16},{16,18},{18... | collective-permute-start | bytes 4616 | tf_op jit(solution)/shard_map/ppermute | solution.py:33
  187.9 13.0 %collective-permute-start.21 = (f32[16,24]{0,1:T(8,128)S(1)}, f32[16,24]{0,1:T(8,128)S(1)}, u32[]{:S(2)}, u32[]{:S(2)}) collective-permute-start(f32[16,24]{0,1:T(8,128)S(1)} %slice.411), channel_id=1, source_target_pairs={{1,2},{0,3},{3,4},{2,5},{5,6},{4,7},{7,8},{6,9},{9,10},{8,11},{11,... | collective-permute-start | bytes 4616 | tf_op jit(solution)/shard_map/ppermute | solution.py:43
  195.8 9.6 %collective-permute-start.19 = (f32[16,48]{0,1:T(8,128)S(1)}, f32[16,48]{0,1:T(8,128)S(1)}, u32[]{:S(2)}, u32[]{:S(2)}) collective-permute-start(f32[16,48]{0,1:T(8,128)S(1)} %pad_maximum_fusion.14), channel_id=1, source_target_pairs={{0,1},{1,0},{2,3},{3,2},{4,5},{5,4},{6,7},{7,6},{8,9},{9,8},{10,11... | collective-permute-start | bytes 9224 | tf_op jit(solution)/shard_map/ppermute | solution.py:37
  (8 other events, 69.1 us)

commit v2 on v1

v2 whole, which is shorter than its diff:
```python
import functools

import jax
import jax.numpy as jnp
from jax import lax
from jax.experimental import pallas as pl
from jax.experimental.pallas import tpu as pltpu
from jax.sharding import PartitionSpec as P

DMAX = 8
NF = 16
HALO = 2 * DMAX
LANES = 128
SPARE = 32
SHIFTS = (-2, -1, 0, 1, 2)
GROUP = 8

two_pi = 6.283185307179586
inv_sqrt2 = 0.7071067811865476
inv_sqrt_2pi = 0.3989422804014327


def encode(row_ids, start_bin, feature_count):
    octave = jnp.arange(NF, dtype=jnp.int32)
    period = jnp.power(jnp.int32(2), octave + 2).astype(jnp.int32)
    residue = jnp.remainder(start_bin + row_ids[:, None], period[None, :])
    angles = residue.astype(jnp.float32) * (two_pi / period.astype(jnp.float32))[None, :]
    encoding = jnp.concatenate((jnp.sin(angles), jnp.cos(angles)), axis=1)
    return jnp.pad(encoding, ((0, 0), (0, feature_count - 2 * NF)))


def from_ahead(block, distance):
    devices = range(lax.axis_size("chrom"))
    route = [(i + distance, i) for i in devices if i + distance in devices]
    return lax.ppermute(block, "chrom", route)


def from_partner(block):
    return lax.ppermute(block, "chan", [(0, 1), (1, 0)])


def stacked_taps(kernel, sign, out_count):
    chan_count = kernel.shape[1]
    rows = []
    for m in SHIFTS:
        blocks = []
        for a in (-1, 0, 1):
            b = a + m
            if -1 <= b <= 1:
                tap = kernel[3 * (sign * a + 1) + sign * b + 1]
                blocks.append((tap if sign > 0 else tap.T)[:out_count])
            else:
                blocks.append(jnp.zeros((out_count, chan_count), kernel.dtype))
        rows.append(jnp.concatenate(blocks, axis=1))
    return jnp.concatenate(rows, axis=0)


def lane_ids():
    return lax.broadcasted_iota(jnp.int32, (1, LANES), 1)


def tiles_of(values):
    return [values[:, k : k + LANES] for k in range(0, values.shape[1], LANES)]


def pull(tiles, amount, count, lanes):
    turned = [pltpu.roll(tile, lax.rem(LANES - amount, LANES), 1) for tile in tiles]
    turned.append(jnp.zeros_like(turned[0]))
    inside = lanes < LANES - amount
    return [jnp.where(inside, turned[k], turned[k + 1]) for k in range(count)]


def push(tiles, amount, count, lanes):
    zero = jnp.zeros_like(tiles[0])
    turned = [zero] + [pltpu.roll(tile, amount, 1) for tile in tiles] + [zero]
    inside = lanes >= amount
    return [jnp.where(inside, turned[k + 1], turned[k]) for k in range(count)]


def tap_sums(weights, ref, first, dilation, out_count, lanes):
    width = ref.shape[2]
    count = width // LANES
    window = jnp.concatenate(
        [
            jnp.concatenate([ref[first + g + a * dilation] for a in (-1, 0, 1)], axis=0)
            for g in range(GROUP)
        ],
        axis=1,
    )
    stacked = jnp.dot(weights[...], window, preferred_element_type=jnp.float32)
    sums = []
    for g in range(GROUP):
        part = [
            tiles_of(stacked[k * out_count : (k + 1) * out_count, g * width : (g + 1) * width])
            for k in range(5)
        ]
        shifted = [
            push(part[0], 2 * dilation, count, lanes),
            push(part[1], dilation, count, lanes),
            part[2],
            pull(part[3], dilation, count, lanes),
            pull(part[4], 2 * dilation, count, lanes),
        ]
        sums.append([sum(tile[1:], tile[0]) for tile in zip(*shifted)])
    return sums


def limit_of(row, first_row, band_width, total_rows):
    here = first_row - HALO + row
    return jnp.where(here < 0, 0, jnp.minimum(band_width, total_rows - here))


def gelu_cdf(values):
    return 0.5 + 0.5 * lax.erf(values * inv_sqrt2)


def gelu_slope(values, cdf):
    return cdf + values * (inv_sqrt_2pi * jnp.exp(-0.5 * values * values))


def forward_kernel(
    total_rows, scalars, terms, params, taps,
    pair_out, slope_0, slope_1, pair_0, act_0, act_1, pair_1, far_rows, near_rows, far, near,
):
    band_width, first_row, step_0, step_1, member = (scalars[k] for k in range(5))
    lanes = lane_ids()
    rows, own, width = pair_out.shape
    chans = 2 * own
    count = width // LANES
    members = terms.shape[0]
    taps_0, taps_1 = taps.at[: 5 * chans], taps.at[5 * chans :]
    bias = params.at[:, :width]
    bias_0 = params[:, width : width + LANES][:, 0:1]
    bias_1 = params[:own, width : width + LANES][:, 1:2]

    far_rows[...] = jnp.zeros_like(far_rows)
    near_rows[...] = jnp.zeros_like(near_rows)
    half = rows // 2
    for place in range(width // rows + 3):
        source = lax.rem(member + (members - 1 + place), members)
        tile = terms[source, place // members]
        far_rows[place * rows : place * rows + half] = tile
        far_rows[place * rows + half : (place + 1) * rows] = pltpu.roll(tile, LANES - chans, 1)
        if place < 3:
            tile = jnp.zeros((half, LANES), jnp.float32)
            for j in range(3):
                part = pltpu.roll(terms[source, j], SPARE * (j + 1), 1)
                tile = jnp.where(lanes // SPARE == j, part, tile)
            near_rows[place * rows : place * rows + half] = tile
            near_rows[place * rows + half : (place + 1) * rows] = pltpu.roll(tile, LANES - chans, 1)
    for k in range(count + 1):
        span = slice(k * LANES, (k + 1) * LANES)
        far[:, span] = far_rows[span].T[:chans]
    near[...] = near_rows[...].T[:chans]

    def keeps(row):
        limit = limit_of(row, first_row, band_width, total_rows)
        return [lanes + k * LANES < limit for k in range(count)]

    def seed(row, with_slope):
        near_col = pltpu.roll(near[...], lax.rem(LANES - row, LANES), 1)[:, 0:1]
        ahead = pull(tiles_of(far[...]), row, count, lanes)
        for k, keep in enumerate(keeps(row)):
            span = pl.ds(k * LANES, LANES)
            value = jnp.where(keep, near_col + ahead[k] + bias[:, span], 0.0)
            cdf = gelu_cdf(value)
            pair_0[row, :, span] = value
            act_0[row, :, span] = (value * cdf).astype(jnp.bfloat16)
            if with_slope:
                slope_0[row - HALO, :, span] = gelu_slope(value[:own], cdf[:own])

    def outer_seed(index, _):
        seed(jnp.where(index < HALO, index, index + rows), False)
        return 0

    def inner_seed(index, _):
        seed(index + HALO, True)
        return 0

    lax.fori_loop(0, 2 * HALO, outer_seed, 0)
    lax.fori_loop(0, rows, inner_seed, 0)

    def layer_0(block, _):
        first = block * GROUP
        convs = tap_sums(taps_0, act_0, first + DMAX, step_0, chans, lanes)
        for g, conv in enumerate(convs):
            index = first + g
            row = index + DMAX
            for k, keep in enumerate(keeps(row)):
                span = pl.ds(k * LANES, LANES)
                value = jnp.where(keep, pair_0[row, :, span] + conv[k] + bias_0, 0.0)
                cdf = gelu_cdf(value)
                pair_1[index, :, span] = value[:own]
                act_1[index, :, span] = (value * cdf).astype(jnp.bfloat16)
                slope_1[index, :, span] = gelu_slope(value, cdf)
        return 0

    lax.fori_loop(0, (rows + HALO) // GROUP, layer_0, 0)

    def layer_1(block, _):
        first = block * GROUP
        convs = tap_sums(taps_1, act_1, first + DMAX, step_1, own, lanes)
        for g, conv in enumerate(convs):
            index = first + g
            for k, keep in enumerate(keeps(index + HALO)):
                span = pl.ds(k * LANES, LANES)
                value = jnp.where(keep, pair_1[index + DMAX, :, span] + conv[k] + bias_1, 0.0)
                pair_out[index, :, span] = value
        return 0

    lax.fori_loop(0, rows // GROUP, layer_1, 0)


def backward_kernel(
    total_rows, scalars, cot_behind, cot_here, cot_ahead, slope_0, slope_1, taps,
    far_terms, near_terms, grad_2, grad_1, low_1, near_sum, far_sum, far_rows,
):
    band_width, first_row, step_0, step_1, member = (scalars[k] for k in range(5))
    lanes = lane_ids()
    rows, chans, width = cot_here.shape
    own = chans // 2
    count = width // LANES
    members = far_terms.shape[0]
    taps_1, taps_0 = taps.at[: 5 * chans], taps.at[5 * chans :]

    def keeps(row):
        limit = limit_of(row, first_row, band_width, total_rows)
        return [lanes + k * LANES < limit for k in range(count)]

    def lay(index, _):
        grad_2[index] = cot_behind[index]
        grad_2[index + rows] = cot_here[index]
        grad_2[index + 2 * rows] = cot_ahead[index]
        return 0

    lax.fori_loop(0, rows, lay, 0)

    def layer_1(block, _):
        first = block * GROUP
        convs = tap_sums(taps_1, grad_2, first + DMAX, step_1, chans, lanes)
        for g, conv in enumerate(convs):
            index = first + g
            row = index + DMAX
            for k, keep in enumerate(keeps(row)):
                span = pl.ds(k * LANES, LANES)
                above = grad_2[row, :, span].astype(jnp.float32)
                value = jnp.where(keep, above + slope_1[index, :, span] * conv[k], 0.0)
                grad_1[index, :, span] = value[:own]
                low_1[index, :, span] = value.astype(jnp.bfloat16)
        return 0

    lax.fori_loop(0, (rows + HALO) // GROUP, layer_1, 0)

    near_sum[...] = jnp.zeros_like(near_sum)
    far_sum[...] = jnp.zeros_like(far_sum)

    def layer_0(block, _):
        first = block * GROUP
        convs = tap_sums(taps_0, low_1, first + DMAX, step_0, own, lanes)
        for g, conv in enumerate(convs):
            index = first + g
            values = []
            for k, keep in enumerate(keeps(index + HALO)):
                span = pl.ds(k * LANES, LANES)
                above = grad_1[index + DMAX, :, span]
                values.append(jnp.where(keep, above + slope_0[index, :, span] * conv[k], 0.0))
            total = jnp.sum(sum(values[1:], values[0]), axis=1, keepdims=True)
            near_sum[:own] += jnp.where(lanes == index, total, 0.0)
            for k, tile in enumerate(push(values, index, count + 1, lanes)):
                far_sum[:own, k * LANES : (k + 1) * LANES] += tile
        return 0

    lax.fori_loop(0, rows // GROUP, layer_0, 0)

    far_rows[...] = jnp.zeros_like(far_rows)
    for k in range(count + 1):
        start = pl.multiple_of(member * rows, 8) + k * LANES
        far_rows[pl.ds(start, LANES)] = far_sum[:, k * LANES : (k + 1) * LANES].T
    half = rows // 2

    def halves(slot):
        return [far_rows[slot * rows + h * half : slot * rows + (h + 1) * half] for h in range(2)]

    for r in range(members):
        pieces = halves(r) + halves(members + r)
        far_terms[r, 0] = sum(
            [pltpu.roll(piece, k * own, 1) for k, piece in enumerate(pieces) if k], pieces[0]
        )
        pieces = halves(2 * members + r)
        far_terms[r, 1] = pieces[0] + pltpu.roll(pieces[1], own, 1)
    near_rows = near_sum[...].T
    near_terms[...] = pltpu.roll(near_rows[:half], 2 * own, 1) + pltpu.roll(
        near_rows[half:rows], 3 * own, 1
    )


def call(kernel, out_shapes, scratch, flops, smem, *arrays):
    bytes_accessed = sum(a.size * a.dtype.itemsize for a in arrays)
    bytes_accessed += sum(s.size * s.dtype.itemsize for s in out_shapes)
    vmem = pl.BlockSpec(memory_space=pltpu.VMEM)
    return pl.pallas_call(
        kernel,
        out_shape=out_shapes,
        in_specs=[pl.BlockSpec(memory_space=pltpu.SMEM)] + [vmem] * len(arrays),
        out_specs=[vmem] * len(out_shapes),
        scratch_shapes=scratch,
        compiler_params=pltpu.CompilerParams(vmem_limit_bytes=32 * 2**20),
        cost_estimate=pl.CostEstimate(
            flops=flops, bytes_accessed=bytes_accessed, transcendentals=0
        ),
    )(smem, *arrays)


def forward_call(total_rows, rows, scalars, terms, params, taps):
    chans, width = params.shape[0], params.shape[1] - LANES
    own = chans // 2
    f32 = functools.partial(jax.ShapeDtypeStruct, dtype=jnp.float32)
    return call(
        functools.partial(forward_kernel, total_rows),
        (f32((rows, own, width)), f32((rows, own, width)), f32((rows + HALO, chans, width))),
        [
            pltpu.VMEM((rows + 2 * HALO, chans, width), jnp.float32),
            pltpu.VMEM((rows + 2 * HALO, chans, width), jnp.bfloat16),
            pltpu.VMEM((rows + HALO, chans, width), jnp.bfloat16),
            pltpu.VMEM((rows + HALO, own, width), jnp.float32),
            pltpu.VMEM((width + LANES, LANES), jnp.float32),
            pltpu.VMEM((LANES, LANES), jnp.float32),
            pltpu.VMEM((chans, width + LANES), jnp.float32),
            pltpu.VMEM((chans, LANES), jnp.float32),
        ],
        2 * 15 * chans * chans * width * 40,
        scalars, terms, params, taps,
    )


def backward_call(total_rows, members, scalars, cot_behind, cot, cot_ahead, slope_0, slope_1, taps):
    rows, chans, width = cot.shape
    own = chans // 2
    slots = members + (width + LANES) // rows
    f32 = functools.partial(jax.ShapeDtypeStruct, dtype=jnp.float32)
    return call(
        functools.partial(backward_kernel, total_rows),
        (f32((members, 2, rows // 2, LANES)), f32((rows // 2, LANES))),
        [
            pltpu.VMEM((rows + 2 * HALO, chans, width), jnp.bfloat16),
            pltpu.VMEM((rows + HALO, own, width), jnp.float32),
            pltpu.VMEM((rows + HALO, chans, width), jnp.bfloat16),
            pltpu.VMEM((LANES, LANES), jnp.float32),
            pltpu.VMEM((LANES, width + LANES), jnp.float32),
            pltpu.VMEM((slots * rows, LANES), jnp.float32),
        ],
        2 * 15 * chans * chans * width * 40,
        scalars, cot_behind, cot, cot_ahead, slope_0, slope_1, taps,
    )


def group_sizes(blocks, devices):
    members = blocks // 2
    return members, devices // members


def exchange_in_group(chunks):
    members = chunks.shape[0]
    count = lax.axis_size("chrom")
    lists = [[q * members + k for k in range(members)] for q in range(count // members)]
    return lax.all_to_all(chunks, "chrom", 0, 0, axis_index_groups=lists)


def exchange_across_groups(chunks, members):
    groups = chunks.shape[0] // 2
    lists = [
        [2 * (t * members + r) + c for t in range(groups) for c in range(2)] for r in range(members)
    ]
    return lax.all_to_all(chunks, ("chrom", "chan"), 0, 0, axis_index_groups=lists)


def window_terms(proj, members, groups, group, member, chan):
    own = proj.shape[1] // 2
    half = proj.shape[0] // 2
    tile = jnp.pad(jnp.concatenate((proj[:half], proj[half:]), axis=1), ((0, 0), (0, LANES - 4 * own)))
    held = exchange_across_groups(jnp.broadcast_to(tile, (2 * groups, half, LANES)), members)
    held = held.reshape(groups, 2, half, LANES)
    held = jnp.where(chan == 0, held, held[:, ::-1])
    held = lax.dynamic_slice_in_dim(jnp.pad(held, ((1, 3), (0, 0), (0, 0), (0, 0))), group, 5, 0)

    def joined(first):
        pieces = [
            held[:, c, :, 2 * own * h + first : 2 * own * h + first + own] for h in range(2) for c in range(2)
        ]
        return jnp.concatenate(pieces, axis=2)

    near, far = joined(0), joined(own)
    to = jnp.arange(members, dtype=jnp.int32)[:, None, None, None]
    before = (member == members - 1) & (to == 0)
    after = (member == 0) & (to == members - 1)
    start = jnp.where(before, 0, jnp.where(member < to - 1, 2, 1))
    far = jnp.where(start == 0, far[None, 0:3], jnp.where(start == 1, far[None, 1:4], far[None, 2:5]))
    near = jnp.where(before, near[None, 0:1], jnp.where(after, near[None, 2:3], near[None, 1:2]))
    near = [near[:, :, :, SPARE * j : SPARE * (j + 1)] for j in range(3)]
    return exchange_in_group(jnp.concatenate((far, jnp.concatenate(near, axis=1)), axis=3))


def summed_terms(far_terms, near_terms, own, members, groups, group):
    part = jnp.sum(exchange_in_group(far_terms), axis=0)
    lanes = jnp.arange(LANES, dtype=jnp.int32)
    first = jnp.where(lanes < 2 * own, part[0], near_terms)
    second = jnp.where(lanes < 2 * own, jnp.roll(part[0], -2 * own, axis=1), 0)
    to = jnp.arange(groups, dtype=jnp.int32)[:, None, None, None]
    chunks = jnp.where(
        to == group, first, jnp.where(to == group + 1, second, jnp.where(to == group + 2, part[1], 0))
    )
    chunks = jnp.broadcast_to(chunks, (groups, 2) + part.shape[1:])
    recv = exchange_across_groups(chunks.reshape((2 * groups,) + part.shape[1:]), members)
    return jnp.sum(recv.reshape(chunks.shape), axis=0)


def shards(
    embedding, window_start, band_width, dilations, near_weight, far_weight,
    distance_bias, conv_weight, conv_bias, cotangent,
):
    rows = embedding.shape[0]
    own, width = distance_bias.shape
    chans = conv_weight.shape[2]
    features_half = embedding.shape[1] // 2
    chan = lax.axis_index("chan")
    place = lax.axis_index("chrom")
    first_row = place * rows
    total_rows = lax.axis_size("chrom") * rows
    members, groups = group_sizes(width // rows, lax.axis_size("chrom"))
    group, member = place // members, place % members
    row_ids = first_row + jnp.arange(rows, dtype=jnp.int32)
    scalars = jnp.stack([band_width[0], first_row, dilations[0], dilations[1], member]).astype(jnp.int32)

    features = (
        embedding.astype(jnp.float32) + encode(row_ids, window_start[0], embedding.shape[1])
    ).astype(jnp.bfloat16)
    both = jnp.concatenate((near_weight, far_weight), axis=1)
    proj = jnp.dot(features, both, preferred_element_type=jnp.float32)
    terms = window_terms(proj, members, groups, group, member, chan)

    cot_other = from_partner(cotangent)
    offsets = jnp.arange(width, dtype=jnp.int32)
    keep = (offsets[None, :] < band_width[0]) & (row_ids[:, None] + offsets[None, :] < total_rows)
    cot = jnp.concatenate((cotangent, cot_other), axis=0)
    cot = jnp.where(keep[:, None, :], jnp.swapaxes(cot, 0, 1), 0).astype(jnp.bfloat16)
    cot, terms = lax.optimization_barrier((cot, terms))
    cot_behind = from_ahead(cot, -1)
    cot_ahead = from_ahead(cot, 1)

    small = jnp.concatenate((distance_bias, conv_bias.T, jnp.zeros((own, LANES - 2), jnp.float32)), axis=1)
    params = jnp.concatenate((small, from_partner(small)), axis=0)
    other = from_partner(lax.dynamic_slice_in_dim(both, (1 - chan) * features_half, features_half, 0))
    here = lax.dynamic_slice_in_dim(both, chan * features_half, features_half, 0)
    back_project = []
    for cols in (jnp.where(chan == 0, here, other), jnp.where(chan == 0, other, here)):
        near_rows, far_rows = cols[:, :own].T, cols[:, own:].T
        gap = jnp.zeros((own, features_half), cols.dtype)
        rest = jnp.zeros((LANES - 4 * own, 2 * features_half), cols.dtype)
        for block in (far_rows, near_rows):
            back_project.append(jnp.concatenate((block, gap), axis=1))
            back_project.append(jnp.concatenate((gap, block), axis=1))
        back_project.append(rest)
    back_project = jnp.concatenate(back_project, axis=0)

    twice = jnp.concatenate((conv_weight, conv_weight), axis=2)
    twice = jnp.concatenate((twice, twice), axis=3)
    turned = lax.dynamic_slice(twice, (0, 0, chan * own, chan * own), conv_weight.shape)
    last = jnp.zeros((-5 * own % 16, 3 * chans), conv_weight.dtype)
    taps_ahead = jnp.concatenate(
        (stacked_taps(turned[0], 1, chans), stacked_taps(turned[1], 1, own), last), axis=0
    )
    taps_back = jnp.concatenate(
        (stacked_taps(turned[1], -1, chans), stacked_taps(turned[0], -1, own), last), axis=0
    )

    pair_rows, slope_0, slope_1 = forward_call(total_rows, rows, scalars, terms, params, taps_ahead)
    pair_out = jnp.swapaxes(pair_rows.astype(jnp.bfloat16), 0, 1)
    far_terms, near_terms = backward_call(
        total_rows, members, scalars, cot_behind, cot, cot_ahead, slope_0, slope_1, taps_back
    )
    sums = summed_terms(far_terms, near_terms, own, members, groups, group)
    lows = jnp.concatenate((sums[0], sums[1]), axis=1).astype(jnp.bfloat16)
    grads = jnp.dot(lows, back_project, preferred_element_type=jnp.float32)
    grads = jnp.concatenate((grads[:, :features_half], grads[:, features_half:]), axis=0)
    return (pair_out, grads.astype(jnp.bfloat16))


def solution(mesh):
    in_specs = (
        P("chrom", None),
        P(),
        P(),
        P(),
        P(None, "chan"),
        P(None, "chan"),
        P("chan", None),
        P(),
        P(None, "chan"),
        P("chan", "chrom", None),
    )
    out_specs = (P("chan", "chrom", None), P("chrom", "chan"))
    return jax.shard_map(shards, mesh=mesh, in_specs=in_specs, out_specs=out_specs, check_vma=False)
```

time: 208 us -> 136 us (0.65)
  starting transfers between devices: 98.8 us -> 60.9 us
  Pallas kernels: 42.6 us -> 25.6 us
  waiting for transfers between devices: 42.3 us -> 31.5 us
  local copies, waits for them, and re-layouts: 13.8 us -> 7.82 us
    ppermute x17 -> x2, starting transfers between devices: 69.6 us -> 10.4 us  [from_ahead(): return lax.ppermute(block, 'chrom', route)]
    ppermute x17 -> x2, waiting for transfers between devices: 37.7 us -> 0.01 us  [from_ahead(): return lax.ppermute(block, 'chrom', route)]
    all_to_all x0 -> x4, starting transfers between devices: none -> 33.1 us  [the longest x2 24.2 us: exchange_across_groups(): lax.all_to_all(chunks, ('chrom', 'chan'), 0, 0, axis_index_groups=lists)]
    all_to_all x0 -> x4, waiting for transfers between devices: none -> 28.5 us  [the longest x2 16.6 us: exchange_in_group(): return lax.all_to_all(chunks, 'chrom', 0, 0, axis_index_groups=lists)]
    pallas_call x2, Pallas kernels: 42.6 us -> 25.6 us  [call(): pl.pallas_call(kernel, out_shape=out_shapes, in_specs=[pl.BlockSpec(memor...]
    ppermute x5 -> x3, starting transfers between devices: 27.3 us -> 17.5 us  [from_partner(): return lax.ppermute(block, 'chan', [(0, 1), (1, 0)])]
    unnamed x30 -> x28, local copies, waits for them, and re-layouts: 8.94 us -> 4.38 us
    ppermute x5 -> x3, waiting for transfers between devices: 4.53 us -> 3.02 us  [from_partner(): return lax.ppermute(block, 'chan', [(0, 1), (1, 0)])]
  transfers between devices with their start and end apart: 23 -> 9, of which waited for: 10 -> 4; matrix products, arithmetic and copies ran while one was open for 6% -> 8% of each run, Pallas kernels for 12% -> 13%
where the time goes in v2:
time: 136 us; the launch traced here: 135 us
  starting transfers between devices  60.9 us (45%)
  waiting for transfers between devices  31.5 us (23%)
  Pallas kernels  25.6 us (19%)
  local copies, waits for them, and re-layouts  7.82 us (6%)
  other arithmetic  5.16 us (4%)
  between operations  2.61 us (2%)
    pallas_call x2, Pallas kernels, call(): pl.pallas_call(kernel, out_shape=out_shapes, in_specs=[pl.BlockSpec(memor...  25.6 us
    all_to_all x2, starting transfers between devices, exchange_across_groups(): lax.all_to_all(chunks, ('chrom', 'chan'), 0, 0, axis_index_groups=lists)  24.2 us
    ppermute x3, starting transfers between devices, from_partner(): return lax.ppermute(block, 'chan', [(0, 1), (1, 0)])  17.5 us
    all_to_all x2, waiting for transfers between devices, exchange_in_group(): return lax.all_to_all(chunks, 'chrom', 0, 0, axis_index_groups=lists)  16.6 us
    all_to_all x2, waiting for transfers between devices, exchange_across_groups(): lax.all_to_all(chunks, ('chrom', 'chan'), 0, 0, axis_index_groups=lists)  11.9 us
    ppermute x2, starting transfers between devices, from_ahead(): return lax.ppermute(block, 'chrom', route)  10.4 us
    all_to_all x2, starting transfers between devices, exchange_in_group(): return lax.all_to_all(chunks, 'chrom', 0, 0, axis_index_groups=lists)  8.91 us
    unnamed x28, local copies, waits for them, and re-layouts  4.38 us
  transfers between devices with their start and end apart: 9, of which 4 were waited for; matrix products, arithmetic and copies ran while one was open for 8% of the time, Pallas kernels for 13%

profile of v2, /device:TPU:6, one launch (start us, length us, event | category | flops | bytes accessed | tf_op | source)
XLA Modules:
  0.0 134.6 jit_solution(14199291545986805075)
XLA Ops:
  0.6 1.3 copy.85
  1.9 7.7 %collective-permute-start = (bf16[24,16,512]{2,0,1:T(8,128)(2,1)S(1)}, bf16[24,16,512]{2,0,1:T(8,128)(2,1)S(1)}, u32[]{:S(2)}, u32[]{:S(2)}) collective-permute-start(bf16[24,16,512]{2,0,1:T(8,128)(2,1)S(1)} %copy.85), channel_id=1, source_target_pairs={{0,1},{1,0},{2,3},{3,2},{4,5},{5,4},{6,7},{7,6},{8,9},{9,8},{10,11... | collective-permute-start | bytes 1179656 | tf_op jit(solution)/shard_map/ppermute | solution.py:39
  9.7 0.7 constant_dynamic-update-slice_fusion.1
  11.1 0.7 constant_dynamic-update-slice_fusion
  12.1 0.9 fusion.17
  13.8 13.4 %all-to-all-start = ((f32[32,8,128]{2,1,0:T(8,128)}), f32[32,8,128]{2,1,0:T(8,128)S(1)}, u32[]{:S(2)}, u32[]{:S(2)}) async-start(f32[32,8,128]{2,1,0:T(8,128)} %broadcast_in_dim.191), calls=%async_computation | async-start | bytes 262144 | tf_op jit(solution)/shard_map/all_to_all | solution.py:374
  27.2 0.8 copy.92
  28.0 0.9 pad_maximum_fusion.1
  28.9 7.3 %collective-permute-start.1 = (f32[24,640]{1,0:T(8,128)S(1)}, f32[24,640]{1,0:T(8,128)S(1)}, u32[]{:S(2)}, u32[]{:S(2)}) collective-permute-start(f32[24,640]{1,0:T(8,128)S(1)} %pad_maximum_fusion.1), channel_id=1, source_target_pairs={{0,1},{1,0},{2,3},{3,2},{4,5},{5,4},{6,7},{7,6},{8,9},{9,8},{10,11... | collective-permute-start | bytes 184328 | tf_op jit(solution)/shard_map/ppermute | solution.py:39
  36.2 2.5 %collective-permute-start.4 = (bf16[256,48]{0,1:T(8,128)(2,1)S(1)}, bf16[256,48]{0,1:T(8,128)(2,1)S(1)}, u32[]{:S(2)}, u32[]{:S(2)}) collective-permute-start(bf16[256,48]{0,1:T(8,128)(2,1)S(1)} %constant_dynamic-slice_fusion), channel_id=1, source_target_pairs={{0,1},{1,0},{2,3},{3,2},{4,5},{5,4},{6,7},{7,6},{8,9},{9,8},{10,11... | collective-permute-start | bytes 73736 | tf_op jit(solution)/shard_map/ppermute | solution.py:39
  38.9 0.8 fusion.2
  42.8 3.0 %collective-permute-done.4 = bf16[256,48]{0,1:T(8,128)(2,1)S(1)} collective-permute-done((bf16[256,48]{0,1:T(8,128)(2,1)S(1)}, bf16[256,48]{0,1:T(8,128)(2,1)S(1)}, u32[]{:S(2)}, u32[]{:S(2)}) %collective-permute-start.4) | collective-permute-done | bytes 24608 | tf_op jit(solution)/shard_map/ppermute | solution.py:39
  46.5 0.8 maximum_maximum_fusion
  47.4 5.4 %all-to-all-start.1 = ((f32[16,3,8,128]{3,2,1,0:T(8,128)}), f32[16,3,8,128]{3,2,1,0:T(8,128)S(1)}, u32[]{:S(2)}, u32[]{:S(2)}) async-start(f32[16,3,8,128]{3,2,1,0:T(8,128)} %maximum_maximum_fusion), calls=%async_computation.1 | async-start | bytes 393216 | tf_op jit(solution)/shard_map/all_to_all | solution.py:366
  53.0 8.8 %all-to-all-done.1.terms = f32[16,3,8,128]{3,2,1,0:T(8,128)S(1)} async-done(((f32[16,3,8,128]{3,2,1,0:T(8,128)}), f32[16,3,8,128]{3,2,1,0:T(8,128)S(1)}, u32[]{:S(2)}, u32[]{:S(2)}) %all-to-all-start.1) | async-done | bytes 196640 | tf_op jit(solution)/shard_map/all_to_all | solution.py:366
  61.8 1.9 %collective-permute-start.2 = (bf16[16,48,512]{2,1,0:T(8,128)(2,1)S(1)}, bf16[16,48,512]{2,1,0:T(8,128)(2,1)S(1)}, u32[]{:S(2)}, u32[]{:S(2)}) collective-permute-start(bf16[16,48,512]{2,1,0:T(8,128)(2,1)S(1)} %fusion.cot_here), channel_id=1, source_target_pairs={{0,2},{2,4},{4,6},{6,8},{8,10},{10,12},{12,14},{14,16},{16,18},{18... | collective-permute-start | bytes 2359304 | tf_op jit(solution)/shard_map/ppermute | solution.py:35
  63.7 8.4 %collective-permute-start.3 = (bf16[16,48,512]{2,1,0:T(8,128)(2,1)S(1)}, bf16[16,48,512]{2,1,0:T(8,128)(2,1)S(1)}, u32[]{:S(2)}, u32[]{:S(2)}) collective-permute-start(bf16[16,48,512]{2,1,0:T(8,128)(2,1)S(1)} %fusion.cot_here), channel_id=1, source_target_pairs={{2,0},{4,2},{6,4},{8,6},{10,8},{12,10},{14,12},{16,14},{18,16},{20... | collective-permute-start | bytes 2359304 | tf_op jit(solution)/shard_map/ppermute | solution.py:35
  72.3 17.3 %shard_map.113 = (f32[16,24,512]{2,1,0:T(8,128)S(1)}, f32[16,24,512]{2,1,0:T(8,128)S(1)}, f32[32,48,512]{2,1,0:T(8,128)S(1)}) custom-call(s32[5]{0:T(128)S(1)} %pad_add_fusion.scalars, f32[16,3,8,128]{3,2,1,0:T(8,128)S(1)} %all-to-all-done.1.terms, f32[48,640]{1,0:T(8,128)S(1)} %pad_maximum_fusion.params, bf16[368,144]{1,0:T(8,128)(2,1)S(1)} %copy.102.taps), custom_call_target="tpu_custom_call" | custom-call | flops 1415577600 | bytes 5144064 | tf_op jit(solution)/shard_map/pallas_call | solution.py:301
  89.6 8.3 %shard_map.114 = (f32[16,2,8,128]{3,2,1,0:T(8,128)}, f32[8,128]{1,0:T(8,128)S(1)}) custom-call(s32[5]{0:T(128)S(1)} %pad_add_fusion.scalars, bf16[16,48,512]{2,1,0:T(8,128)(2,1)S(1)} %collective-permute-done.2.cot_behind, bf16[16,48,512]{2,1,0:T(8,128)(2,1)S(1)} %fusion.cot_here, bf16[16,48,512]{2,1,0:T(8,128)(2,1)S(1)} %collective-permute-done.3.cot_ahead, ...), custom_call_target="tpu_custom_call" | custom-call | flops 1415577600 | bytes 6532608 | tf_op jit(solution)/shard_map/pallas_call | solution.py:301
  97.9 3.5 %all-to-all-start.2 = ((f32[16,2,8,128]{3,2,1,0:T(8,128)}), f32[16,2,8,128]{3,2,1,0:T(8,128)S(1)}, u32[]{:S(2)}, u32[]{:S(2)}) async-start(f32[16,2,8,128]{3,2,1,0:T(8,128)} %get-tuple-element.14), calls=%async_computation.2 | async-start | bytes 262144 | tf_op jit(solution)/shard_map/all_to_all | solution.py:366
  101.4 7.9 %all-to-all-done.2 = f32[16,2,8,128]{3,2,1,0:T(8,128)S(1)} async-done(((f32[16,2,8,128]{3,2,1,0:T(8,128)}), f32[16,2,8,128]{3,2,1,0:T(8,128)S(1)}, u32[]{:S(2)}, u32[]{:S(2)}) %all-to-all-start.2) | async-done | bytes 131104 | tf_op jit(solution)/shard_map/all_to_all | solution.py:366
  110.3 10.8 %all-to-all-start.3 = ((f32[32,8,128]{2,1,0:T(8,128)}), f32[32,8,128]{2,1,0:T(8,128)S(1)}, u32[]{:S(2)}, u32[]{:S(2)}) async-start(f32[32,8,128]{2,1,0:T(8,128)} %bitcast.66), calls=%async_computation.3 | async-start | bytes 262144 | tf_op jit(solution)/shard_map/all_to_all | solution.py:374
  121.1 0.9 copy.109
  121.9 11.9 %all-to-all-done.3 = f32[32,8,128]{2,1,0:T(8,128)S(1)} async-done(((f32[32,8,128]{2,1,0:T(8,128)}), f32[32,8,128]{2,1,0:T(8,128)S(1)}, u32[]{:S(2)}, u32[]{:S(2)}) %all-to-all-start.3) | async-done | bytes 131104 | tf_op jit(solution)/shard_map/all_to_all | solution.py:374
  (105 shorter events, 6.3 us)
Async XLA Ops:
  0.6 38.1 %copy-start = (bf16[2,9,48,48]{3,2,1,0:T(8,128)(2,1)S(1)}, bf16[2,9,48,48]{3,2,1,0:T(8,128)(2,1)}, u32[]{:S(2)}) copy-start(bf16[2,9,48,48]{3,2,1,0:T(8,128)(2,1)} %param.17) | copy-start | bytes 248836
  1.9 50.9 %collective-permute-start = (bf16[24,16,512]{2,0,1:T(8,128)(2,1)S(1)}, bf16[24,16,512]{2,0,1:T(8,128)(2,1)S(1)}, u32[]{:S(2)}, u32[]{:S(2)}) collective-permute-start(bf16[24,16,512]{2,0,1:T(8,128)(2,1)S(1)} %copy.85), channel_id=1, source_target_pairs={{0,1},{1,0},{2,3},{3,2},{4,5},{5,4},{6,7},{7,6},{8,9},{9,8},{10,11... | collective-permute-start | bytes 1179656 | tf_op jit(solution)/shard_map/ppermute | solution.py:39
  13.8 32.1 %all-to-all-start = ((f32[32,8,128]{2,1,0:T(8,128)}), f32[32,8,128]{2,1,0:T(8,128)S(1)}, u32[]{:S(2)}, u32[]{:S(2)}) async-start(f32[32,8,128]{2,1,0:T(8,128)} %broadcast_in_dim.191), calls=%async_computation | async-start | bytes 262144 | tf_op jit(solution)/shard_map/all_to_all | solution.py:374
  27.2 14.8 %copy-start.2 = (s32[2]{0:T(128)S(1)}, s32[2]{0:T(128)}, u32[]{:S(2)}) copy-start(s32[2]{0:T(128)} %param.13) | copy-start | bytes 28
  28.9 43.3 %collective-permute-start.1 = (f32[24,640]{1,0:T(8,128)S(1)}, f32[24,640]{1,0:T(8,128)S(1)}, u32[]{:S(2)}, u32[]{:S(2)}) collective-permute-start(f32[24,640]{1,0:T(8,128)S(1)} %pad_maximum_fusion.1), channel_id=1, source_target_pairs={{0,1},{1,0},{2,3},{3,2},{4,5},{5,4},{6,7},{7,6},{8,9},{9,8},{10,11... | collective-permute-start | bytes 184328 | tf_op jit(solution)/shard_map/ppermute | solution.py:39
  36.2 9.7 %collective-permute-start.4 = (bf16[256,48]{0,1:T(8,128)(2,1)S(1)}, bf16[256,48]{0,1:T(8,128)(2,1)S(1)}, u32[]{:S(2)}, u32[]{:S(2)}) collective-permute-start(bf16[256,48]{0,1:T(8,128)(2,1)S(1)} %constant_dynamic-slice_fusion), channel_id=1, source_target_pairs={{0,1},{1,0},{2,3},{3,2},{4,5},{5,4},{6,7},{7,6},{8,9},{9,8},{10,11... | collective-permute-start | bytes 73736 | tf_op jit(solution)/shard_map/ppermute | solution.py:39
  46.4 25.8 %copy-start.1 = (f32[24,512]{1,0:T(8,128)S(1)}, f32[24,512]{1,0:T(8,128)}, u32[]{:S(2)}) copy-start(f32[24,512]{1,0:T(8,128)} %param.16) | copy-start | bytes 147460
  47.4 14.4 %all-to-all-start.1 = ((f32[16,3,8,128]{3,2,1,0:T(8,128)}), f32[16,3,8,128]{3,2,1,0:T(8,128)S(1)}, u32[]{:S(2)}, u32[]{:S(2)}) async-start(f32[16,3,8,128]{3,2,1,0:T(8,128)} %maximum_maximum_fusion), calls=%async_computation.1 | async-start | bytes 393216 | tf_op jit(solution)/shard_map/all_to_all | solution.py:366
  61.8 27.8 %collective-permute-start.2 = (bf16[16,48,512]{2,1,0:T(8,128)(2,1)S(1)}, bf16[16,48,512]{2,1,0:T(8,128)(2,1)S(1)}, u32[]{:S(2)}, u32[]{:S(2)}) collective-permute-start(bf16[16,48,512]{2,1,0:T(8,128)(2,1)S(1)} %fusion.cot_here), channel_id=1, source_target_pairs={{0,2},{2,4},{4,6},{6,8},{8,10},{10,12},{12,14},{14,16},{16,18},{18... | collective-permute-start | bytes 2359304 | tf_op jit(solution)/shard_map/ppermute | solution.py:35
  63.7 25.9 %collective-permute-start.3 = (bf16[16,48,512]{2,1,0:T(8,128)(2,1)S(1)}, bf16[16,48,512]{2,1,0:T(8,128)(2,1)S(1)}, u32[]{:S(2)}, u32[]{:S(2)}) collective-permute-start(bf16[16,48,512]{2,1,0:T(8,128)(2,1)S(1)} %fusion.cot_here), channel_id=1, source_target_pairs={{2,0},{4,2},{6,4},{8,6},{10,8},{12,10},{14,12},{16,14},{18,16},{20... | collective-permute-start | bytes 2359304 | tf_op jit(solution)/shard_map/ppermute | solution.py:35
  97.9 11.4 %all-to-all-start.2 = ((f32[16,2,8,128]{3,2,1,0:T(8,128)}), f32[16,2,8,128]{3,2,1,0:T(8,128)S(1)}, u32[]{:S(2)}, u32[]{:S(2)}) async-start(f32[16,2,8,128]{3,2,1,0:T(8,128)} %get-tuple-element.14), calls=%async_computation.2 | async-start | bytes 262144 | tf_op jit(solution)/shard_map/all_to_all | solution.py:366
  110.3 23.6 %all-to-all-start.3 = ((f32[32,8,128]{2,1,0:T(8,128)}), f32[32,8,128]{2,1,0:T(8,128)S(1)}, u32[]{:S(2)}, u32[]{:S(2)}) async-start(f32[32,8,128]{2,1,0:T(8,128)} %bitcast.66), calls=%async_computation.3 | async-start | bytes 262144 | tf_op jit(solution)/shard_map/all_to_all | solution.py:374

commit v3 on v2

--- a/solution.py
+++ b/solution.py
@@ -14,6 +14,7 @@
 SPARE = 32
 SHIFTS = (-2, -1, 0, 1, 2)
 GROUP = 8
+SEEDS = 4
 
 two_pi = 6.283185307179586
 inv_sqrt2 = 0.7071067811865476
@@ -33,6 +34,10 @@
     devices = range(lax.axis_size("chrom"))
     route = [(i + distance, i) for i in devices if i + distance in devices]
     return lax.ppermute(block, "chrom", route)
+
+
+def after(block, earlier):
+    return lax.optimization_barrier((block, earlier))[0]
 
 
 def from_partner(block):
@@ -119,8 +124,8 @@
 
 
 def forward_kernel(
-    total_rows, scalars, terms, params, taps,
-    pair_out, slope_0, slope_1, pair_0, act_0, act_1, pair_1, far_rows, near_rows, far, near,
+    total_rows, scalars, terms, bias_other, bias_here, conv_bias, taps,
+    pair_out, slope_0, slope_1, pair_0, act_0, act_1, pair_1, far_rows, near_rows, far, near, bias,
 ):
     band_width, first_row, step_0, step_1, member = (scalars[k] for k in range(5))
     lanes = lane_ids()
@@ -129,9 +134,22 @@
     count = width // LANES
     members = terms.shape[0]
     taps_0, taps_1 = taps.at[: 5 * chans], taps.at[5 * chans :]
-    bias = params.at[:, :width]
-    bias_0 = params[:, width : width + LANES][:, 0:1]
-    bias_1 = params[:own, width : width + LANES][:, 1:2]
+    slabs = own // 8
+    per_tile = LANES // SPARE
+
+    bias[:own] = bias_here[...]
+    for k in range(count):
+        for j in range(slabs):
+            block = jnp.zeros((8, LANES), jnp.float32)
+            for t in range(per_tile):
+                piece = pltpu.roll(bias_other[k * per_tile + t], (t - j) % per_tile * SPARE, 1)
+                block = jnp.where(lanes // SPARE == t, piece, block)
+            bias[own + 8 * j : own + 8 * (j + 1), k * LANES : (k + 1) * LANES] = block
+    first = slabs * SPARE
+    bias_0 = jnp.concatenate(
+        [conv_bias[:, 0:1]] + [bias_other[0, :, first + j : first + j + 1] for j in range(slabs)], axis=0
+    )
+    bias_1 = conv_bias[:, 1:2]
 
     far_rows[...] = jnp.zeros_like(far_rows)
     near_rows[...] = jnp.zeros_like(near_rows)
@@ -169,16 +187,19 @@
             if with_slope:
                 slope_0[row - HALO, :, span] = gelu_slope(value[:own], cdf[:own])
 
-    def outer_seed(index, _):
-        seed(jnp.where(index < HALO, index, index + rows), False)
-        return 0
-
-    def inner_seed(index, _):
-        seed(index + HALO, True)
-        return 0
-
-    lax.fori_loop(0, 2 * HALO, outer_seed, 0)
-    lax.fori_loop(0, rows, inner_seed, 0)
+    def outer_seeds(block, _):
+        for g in range(SEEDS):
+            index = block * SEEDS + g
+            seed(jnp.where(index < HALO, index, index + rows), False)
+        return 0
+
+    def inner_seeds(block, _):
+        for g in range(SEEDS):
+            seed(block * SEEDS + g + HALO, True)
+        return 0
+
+    lax.fori_loop(0, 2 * HALO // SEEDS, outer_seeds, 0)
+    lax.fori_loop(0, rows // SEEDS, inner_seeds, 0)
 
     def layer_0(block, _):
         first = block * GROUP
@@ -213,7 +234,7 @@
 
 def backward_kernel(
     total_rows, scalars, cot_behind, cot_here, cot_ahead, slope_0, slope_1, taps,
-    far_terms, near_terms, grad_2, grad_1, low_1, near_sum, far_sum, far_rows,
+    far_terms, grad_2, grad_1, low_1, near_sum, far_sum, far_rows,
 ):
     band_width, first_row, step_0, step_1, member = (scalars[k] for k in range(5))
     lanes = lane_ids()
@@ -277,6 +298,8 @@
         start = pl.multiple_of(member * rows, 8) + k * LANES
         far_rows[pl.ds(start, LANES)] = far_sum[:, k * LANES : (k + 1) * LANES].T
     half = rows // 2
+    near_rows = near_sum[...].T
+    near_terms = pltpu.roll(near_rows[:half], 2 * own, 1) + pltpu.roll(near_rows[half:rows], 3 * own, 1)
 
     def halves(slot):
         return [far_rows[slot * rows + h * half : slot * rows + (h + 1) * half] for h in range(2)]
@@ -287,11 +310,8 @@
             [pltpu.roll(piece, k * own, 1) for k, piece in enumerate(pieces) if k], pieces[0]
         )
         pieces = halves(2 * members + r)
-        far_terms[r, 1] = pieces[0] + pltpu.roll(pieces[1], own, 1)
-    near_rows = near_sum[...].T
-    near_terms[...] = pltpu.roll(near_rows[:half], 2 * own, 1) + pltpu.roll(
-        near_rows[half:rows], 3 * own, 1
-    )
+        own_place = jnp.where(member == r, near_terms, 0.0)
+        far_terms[r, 1] = pieces[0] + pltpu.roll(pieces[1], own, 1) + own_place
 
 
 def call(kernel, out_shapes, scratch, flops, smem, *arrays):
@@ -311,9 +331,9 @@
     )(smem, *arrays)
 
 
-def forward_call(total_rows, rows, scalars, terms, params, taps):
-    chans, width = params.shape[0], params.shape[1] - LANES
-    own = chans // 2
+def forward_call(total_rows, rows, scalars, terms, bias_other, bias_here, conv_bias, taps):
+    own, width = bias_here.shape
+    chans = 2 * own
     f32 = functools.partial(jax.ShapeDtypeStruct, dtype=jnp.float32)
     return call(
         functools.partial(forward_kernel, total_rows),
@@ -327,9 +347,10 @@
             pltpu.VMEM((LANES, LANES), jnp.float32),
             pltpu.VMEM((chans, width + LANES), jnp.float32),
             pltpu.VMEM((chans, LANES), jnp.float32),
+            pltpu.VMEM((chans, width), jnp.float32),
         ],
         2 * 15 * chans * chans * width * 40,
-        scalars, terms, params, taps,
+        scalars, terms, bias_other, bias_here, conv_bias, taps,
     )
 
 
@@ -340,7 +361,7 @@
     f32 = functools.partial(jax.ShapeDtypeStruct, dtype=jnp.float32)
     return call(
         functools.partial(backward_kernel, total_rows),
-        (f32((members, 2, rows // 2, LANES)), f32((rows // 2, LANES))),
+        (f32((members, 2, rows // 2, LANES)),),
         [
             pltpu.VMEM((rows + 2 * HALO, chans, width), jnp.bfloat16),
             pltpu.VMEM((rows + HALO, own, width), jnp.float32),
@@ -359,11 +380,20 @@
     return members, devices // members
 
 
-def exchange_in_group(chunks):
+def exchange_in_group(chunks, both_halves=False):
     members = chunks.shape[0]
     count = lax.axis_size("chrom")
-    lists = [[q * members + k for k in range(members)] for q in range(count // members)]
-    return lax.all_to_all(chunks, "chrom", 0, 0, axis_index_groups=lists)
+    if not both_halves:
+        lists = [[q * members + k for k in range(members)] for q in range(count // members)]
+        return lax.all_to_all(chunks, "chrom", 0, 0, axis_index_groups=lists)
+    lists = [
+        [2 * (q * members + k) + c for k in range(members) for c in range(2)]
+        for q in range(count // members)
+    ]
+    twice = jnp.broadcast_to(chunks[:, None], (members, 2) + chunks.shape[1:])
+    twice = twice.reshape((2 * members,) + chunks.shape[1:])
+    recv = lax.all_to_all(twice, ("chrom", "chan"), 0, 0, axis_index_groups=lists)
+    return recv.reshape((members, 2) + chunks.shape[1:])
 
 
 def exchange_across_groups(chunks, members):
@@ -374,12 +404,20 @@
     return lax.all_to_all(chunks, ("chrom", "chan"), 0, 0, axis_index_groups=lists)
 
 
-def window_terms(proj, members, groups, group, member, chan):
+def window_terms(proj, distance_bias, conv_bias, members, groups, group, member, chan):
     own = proj.shape[1] // 2
     half = proj.shape[0] // 2
-    tile = jnp.pad(jnp.concatenate((proj[:half], proj[half:]), axis=1), ((0, 0), (0, LANES - 4 * own)))
-    held = exchange_across_groups(jnp.broadcast_to(tile, (2 * groups, half, LANES)), members)
-    held = held.reshape(groups, 2, half, LANES)
+    slabs = own // 8
+    tile = jnp.concatenate((proj[:half], proj[half:]), axis=1)
+    tile = jnp.pad(tile, ((0, 0), (0, LANES - tile.shape[1])))
+    piece = lax.dynamic_slice_in_dim(distance_bias, group * SPARE, SPARE, 1)
+    piece = [piece[8 * j : 8 * (j + 1)] for j in range(slabs)] + [conv_bias[0].reshape(slabs, 8).T]
+    piece = jnp.concatenate(piece, axis=1)
+    piece = jnp.pad(piece, ((0, 0), (0, LANES - piece.shape[1])))
+    sent = jnp.broadcast_to(jnp.stack((tile, piece)), (2 * groups, 2, half, LANES))
+    recv = exchange_across_groups(sent, members).reshape(groups, 2, 2, half, LANES)
+    bias_other = lax.dynamic_index_in_dim(recv, 1 - chan, 1, keepdims=False)[:, 1]
+    held = recv[:, :, 0]
     held = jnp.where(chan == 0, held, held[:, ::-1])
     held = lax.dynamic_slice_in_dim(jnp.pad(held, ((1, 3), (0, 0), (0, 0), (0, 0))), group, 5, 0)
 
@@ -397,21 +435,17 @@
     far = jnp.where(start == 0, far[None, 0:3], jnp.where(start == 1, far[None, 1:4], far[None, 2:5]))
     near = jnp.where(before, near[None, 0:1], jnp.where(after, near[None, 2:3], near[None, 1:2]))
     near = [near[:, :, :, SPARE * j : SPARE * (j + 1)] for j in range(3)]
-    return exchange_in_group(jnp.concatenate((far, jnp.concatenate(near, axis=1)), axis=3))
-
-
-def summed_terms(far_terms, near_terms, own, members, groups, group):
-    part = jnp.sum(exchange_in_group(far_terms), axis=0)
+    return sent, jnp.concatenate((far, jnp.concatenate(near, axis=1)), axis=3), bias_other
+
+
+def summed_terms(chunks, own):
+    members = chunks.shape[0]
+    part = jnp.sum(exchange_in_group(chunks, both_halves=True), axis=0)
+    ahead_1 = from_ahead(part[:, 0], -members)
+    ahead_2 = from_ahead(part[:, 1], -2 * members)
     lanes = jnp.arange(LANES, dtype=jnp.int32)
-    first = jnp.where(lanes < 2 * own, part[0], near_terms)
-    second = jnp.where(lanes < 2 * own, jnp.roll(part[0], -2 * own, axis=1), 0)
-    to = jnp.arange(groups, dtype=jnp.int32)[:, None, None, None]
-    chunks = jnp.where(
-        to == group, first, jnp.where(to == group + 1, second, jnp.where(to == group + 2, part[1], 0))
-    )
-    chunks = jnp.broadcast_to(chunks, (groups, 2) + part.shape[1:])
-    recv = exchange_across_groups(chunks.reshape((2 * groups,) + part.shape[1:]), members)
-    return jnp.sum(recv.reshape(chunks.shape), axis=0)
+    far = part[:, 0] + jnp.roll(ahead_1, -2 * own, axis=2) + ahead_2
+    return jnp.where(lanes < 2 * own, far, jnp.where(lanes < 4 * own, part[:, 1], 0))
 
 
 def shards(
@@ -436,24 +470,33 @@
     ).astype(jnp.bfloat16)
     both = jnp.concatenate((near_weight, far_weight), axis=1)
     proj = jnp.dot(features, both, preferred_element_type=jnp.float32)
-    terms = window_terms(proj, members, groups, group, member, chan)
-
-    cot_other = from_partner(cotangent)
+    sent, chunks, bias_other = window_terms(
+        proj, distance_bias, conv_bias, members, groups, group, member, chan
+    )
+    terms = exchange_in_group(chunks)
+
+    def weight_rows(half):
+        parts = [
+            lax.dynamic_slice_in_dim(w, half * features_half, features_half, 0).T
+            for w in (near_weight, far_weight)
+        ]
+        return jnp.concatenate(parts, axis=1)
+
+    cot_here = jnp.swapaxes(cotangent, 0, 1)
+    mixed = jnp.concatenate((cot_here, weight_rows(1 - chan)[None]), axis=0)
+    mixed = from_partner(after(mixed, sent))
     offsets = jnp.arange(width, dtype=jnp.int32)
     keep = (offsets[None, :] < band_width[0]) & (row_ids[:, None] + offsets[None, :] < total_rows)
-    cot = jnp.concatenate((cotangent, cot_other), axis=0)
-    cot = jnp.where(keep[:, None, :], jnp.swapaxes(cot, 0, 1), 0).astype(jnp.bfloat16)
-    cot, terms = lax.optimization_barrier((cot, terms))
+    mixed = after(mixed, terms)
+    cot = jnp.concatenate((cot_here, mixed[:rows]), axis=1)
+    cot = jnp.where(keep[:, None, :], cot, 0).astype(jnp.bfloat16)
     cot_behind = from_ahead(cot, -1)
     cot_ahead = from_ahead(cot, 1)
 
-    small = jnp.concatenate((distance_bias, conv_bias.T, jnp.zeros((own, LANES - 2), jnp.float32)), axis=1)
-    params = jnp.concatenate((small, from_partner(small)), axis=0)
-    other = from_partner(lax.dynamic_slice_in_dim(both, (1 - chan) * features_half, features_half, 0))
-    here = lax.dynamic_slice_in_dim(both, chan * features_half, features_half, 0)
+    here, other = weight_rows(chan), mixed[rows]
     back_project = []
     for cols in (jnp.where(chan == 0, here, other), jnp.where(chan == 0, other, here)):
-        near_rows, far_rows = cols[:, :own].T, cols[:, own:].T
+        near_rows, far_rows = cols[:, :features_half], cols[:, features_half:]
         gap = jnp.zeros((own, features_half), cols.dtype)
         rest = jnp.zeros((LANES - 4 * own, 2 * features_half), cols.dtype)
         for block in (far_rows, near_rows):
@@ -473,12 +516,14 @@
         (stacked_taps(turned[1], -1, chans), stacked_taps(turned[0], -1, own), last), axis=0
     )
 
-    pair_rows, slope_0, slope_1 = forward_call(total_rows, rows, scalars, terms, params, taps_ahead)
+    pair_rows, slope_0, slope_1 = forward_call(
+        total_rows, rows, scalars, terms, bias_other, distance_bias, conv_bias.T, taps_ahead
+    )
     pair_out = jnp.swapaxes(pair_rows.astype(jnp.bfloat16), 0, 1)
-    far_terms, near_terms = backward_call(
+    (terms_back,) = backward_call(
         total_rows, members, scalars, cot_behind, cot, cot_ahead, slope_0, slope_1, taps_back
     )
-    sums = summed_terms(far_terms, near_terms, own, members, groups, group)
+    sums = summed_terms(terms_back, own)
     lows = jnp.concatenate((sums[0], sums[1]), axis=1).astype(jnp.bfloat16)
     grads = jnp.dot(lows, back_project, preferred_element_type=jnp.float32)
     grads = jnp.concatenate((grads[:, :features_half], grads[:, features_half:]), axis=0)

time: 136 us -> 125 us (0.919)
  Pallas kernels: 25.6 us -> 20.3 us
  starting transfers between devices: 60.9 us -> 58.2 us
    all_to_all x0 -> x1, waiting for transfers between devices: none -> 11.9 us  [exchange_in_group(): lax.all_to_all(twice, ('chrom', 'chan'), 0, 0, axis_index_groups=lists)]
    all_to_all x2 -> x1, waiting for transfers between devices: 11.9 us -> 1.62 us  [exchange_across_groups(): lax.all_to_all(chunks, ('chrom', 'chan'), 0, 0, axis_index_groups=lists)]
    ppermute x3 -> x1, starting transfers between devices: 17.5 us -> 7.29 us  [from_partner(): return lax.ppermute(block, 'chan', [(0, 1), (1, 0)])]
    all_to_all x2 -> x1, waiting for transfers between devices: 16.6 us -> 7.75 us  [exchange_in_group(): return lax.all_to_all(chunks, 'chrom', 0, 0, axis_index_groups=lists)]
    ppermute x2 -> x4, starting transfers between devices: 10.4 us -> 18.6 us  [from_ahead(): return lax.ppermute(block, 'chrom', route)]
    ppermute x2 -> x4, waiting for transfers between devices: 0.01 us -> 7.99 us  [from_ahead(): return lax.ppermute(block, 'chrom', route)]
    all_to_all x2 -> x1, starting transfers between devices: 24.2 us -> 18.7 us  [exchange_across_groups(): lax.all_to_all(chunks, ('chrom', 'chan'), 0, 0, axis_index_groups=lists)]
    pallas_call x2, Pallas kernels: 25.6 us -> 20.3 us  [call(): pl.pallas_call(kernel, out_shape=out_shapes, in_specs=[pl.BlockSpec(memor...]
  transfers between devices with their start and end apart: 9 -> 8, of which waited for: 4 -> 6; matrix products, arithmetic and copies ran while one was open for 8% -> 6% of each run, Pallas kernels for 13% -> 10%
where the time goes in v3:
time: 125 us; the launch traced here: 124 us
  starting transfers between devices  58.2 us (47%)
  waiting for transfers between devices  30.2 us (24%)
  Pallas kernels  20.3 us (16%)
  local copies, waits for them, and re-layouts  7.52 us (6%)
  other arithmetic  4.22 us (3%)
  between operations  2.65 us (2%)
    pallas_call x2, Pallas kernels, call(): pl.pallas_call(kernel, out_shape=out_shapes, in_specs=[pl.BlockSpec(memor...  20.3 us
    all_to_all x1, starting transfers between devices, exchange_across_groups(): lax.all_to_all(chunks, ('chrom', 'chan'), 0, 0, axis_index_groups=lists)  18.7 us
    ppermute x4, starting transfers between devices, from_ahead(): return lax.ppermute(block, 'chrom', route)  18.6 us
    all_to_all x1, waiting for transfers between devices, exchange_in_group(): lax.all_to_all(twice, ('chrom', 'chan'), 0, 0, axis_index_groups=lists)  11.9 us
    all_to_all x1, starting transfers between devices, exchange_in_group(): return lax.all_to_all(chunks, 'chrom', 0, 0, axis_index_groups=lists)  9.68 us
    ppermute x4, waiting for transfers between devices, from_ahead(): return lax.ppermute(block, 'chrom', route)  7.99 us
    all_to_all x1, waiting for transfers between devices, exchange_in_group(): return lax.all_to_all(chunks, 'chrom', 0, 0, axis_index_groups=lists)  7.75 us
    ppermute x1, starting transfers between devices, from_partner(): return lax.ppermute(block, 'chan', [(0, 1), (1, 0)])  7.29 us
  transfers between devices with their start and end apart: 8, of which 6 were waited for; matrix products, arithmetic and copies ran while one was open for 6% of the time, Pallas kernels for 10%

profile of v3, /device:TPU:6, one launch (start us, length us, event | category | flops | bytes accessed | tf_op | source)
XLA Modules:
  0.0 124.1 jit_solution(14760041913413448430)
XLA Ops:
  0.7 0.7 slice_reduce_fusion
  2.6 0.9 fusion.3
  3.6 0.8 constant_dynamic-slice_fusion
  4.5 0.7 broadcast_in_dim.153
  5.2 18.7 %all-to-all-start = ((f32[32,2,8,128]{3,2,1,0:T(8,128)}), f32[32,2,8,128]{3,2,1,0:T(8,128)S(1)}, u32[]{:S(2)}, u32[]{:S(2)}) async-start(f32[32,2,8,128]{3,2,1,0:T(8,128)} %broadcast_in_dim.153), calls=%async_computation | async-start | bytes 524288 | tf_op jit(solution)/shard_map/all_to_all | solution.py:404
  24.0 1.2 copy.141
  25.3 7.3 %collective-permute-start = (bf16[17,24,512]{2,1,0:T(8,128)(2,1)S(1)}, bf16[17,24,512]{2,1,0:T(8,128)(2,1)S(1)}, u32[]{:S(2)}, u32[]{:S(2)}) collective-permute-start(bf16[17,24,512]{2,1,0:T(8,128)(2,1)S(1)} %pad_maximum_fusion), channel_id=1, source_target_pairs={{0,1},{1,0},{2,3},{3,2},{4,5},{5,4},{6,7},{7,6},{8,9},{9,8},{10,11... | collective-permute-start | bytes 1253384 | tf_op jit(solution)/shard_map/ppermute | solution.py:44
  32.8 0.8 fusion.1
  36.0 1.6 %all-to-all-done = f32[32,2,8,128]{3,2,1,0:T(8,128)S(1)} async-done(((f32[32,2,8,128]{3,2,1,0:T(8,128)}), f32[32,2,8,128]{3,2,1,0:T(8,128)S(1)}, u32[]{:S(2)}, u32[]{:S(2)}) %all-to-all-start) | async-done | bytes 262176 | tf_op jit(solution)/shard_map/all_to_all | solution.py:404
  38.3 0.8 maximum_maximum_fusion
  39.1 9.7 %all-to-all-start.1 = ((f32[16,3,8,128]{3,2,1,0:T(8,128)}), f32[16,3,8,128]{3,2,1,0:T(8,128)S(1)}, u32[]{:S(2)}, u32[]{:S(2)}) async-start(f32[16,3,8,128]{3,2,1,0:T(8,128)} %maximum_maximum_fusion), calls=%async_computation.1 | async-start | bytes 393216 | tf_op jit(solution)/shard_map/all_to_all | solution.py:388
  49.6 0.9 collective-permute-done
  50.5 7.7 %all-to-all-done.1.terms = f32[16,3,8,128]{3,2,1,0:T(8,128)S(1)} async-done(((f32[16,3,8,128]{3,2,1,0:T(8,128)}), f32[16,3,8,128]{3,2,1,0:T(8,128)S(1)}, u32[]{:S(2)}, u32[]{:S(2)}) %all-to-all-start.1) | async-done | bytes 196640 | tf_op jit(solution)/shard_map/all_to_all | solution.py:388
  58.5 2.0 %collective-permute-start.1 = (bf16[16,48,512]{2,1,0:T(8,128)(2,1)S(1)}, bf16[16,48,512]{2,1,0:T(8,128)(2,1)S(1)}, u32[]{:S(2)}, u32[]{:S(2)}) collective-permute-start(bf16[16,48,512]{2,1,0:T(8,128)(2,1)S(1)} %maximum_select_fusion.cot_here), channel_id=1, source_target_pairs={{0,2},{2,4},{4,6},{6,8},{8,10},{10,12},{12,14},{14,16},{16,18},{18... | collective-permute-start | bytes 2359304 | tf_op jit(solution)/shard_map/ppermute | solution.py:36
  60.5 8.3 %collective-permute-start.2 = (bf16[16,48,512]{2,1,0:T(8,128)(2,1)S(1)}, bf16[16,48,512]{2,1,0:T(8,128)(2,1)S(1)}, u32[]{:S(2)}, u32[]{:S(2)}) collective-permute-start(bf16[16,48,512]{2,1,0:T(8,128)(2,1)S(1)} %maximum_select_fusion.cot_here), channel_id=1, source_target_pairs={{2,0},{4,2},{6,4},{8,6},{10,8},{12,10},{14,12},{16,14},{18,16},{20... | collective-permute-start | bytes 2359304 | tf_op jit(solution)/shard_map/ppermute | solution.py:36
  69.0 12.6 %shard_map.113 = (f32[16,24,512]{2,1,0:T(8,128)S(1)}, f32[16,24,512]{2,1,0:T(8,128)S(1)}, f32[32,48,512]{2,1,0:T(8,128)S(1)}) custom-call(s32[5]{0:T(128)S(1)} %pad_add_fusion.scalars, f32[16,3,8,128]{3,2,1,0:T(8,128)S(1)} %all-to-all-done.1.terms, f32[16,8,128]{2,1,0:T(8,128)S(1)} %slice_bitcast_fusion.1.bias_other, f32[24,512]{1,0:T(8,128)S(1)} %copy-done, ...), custom_call_target="tpu_custom_call" | custom-call | flops 1415577600 | bytes 5136064 | tf_op jit(solution)/shard_map/pallas_call | solution.py:321
  81.6 2.2 %collective-permute-done.1.cot_behind = bf16[16,48,512]{2,1,0:T(8,128)(2,1)S(1)} collective-permute-done((bf16[16,48,512]{2,1,0:T(8,128)(2,1)S(1)}, bf16[16,48,512]{2,1,0:T(8,128)(2,1)S(1)}, u32[]{:S(2)}, u32[]{:S(2)}) %collective-permute-start.1) | collective-permute-done | bytes 786464 | tf_op jit(solution)/shard_map/ppermute | solution.py:36
  83.9 7.7 %shard_map.114 = f32[16,2,8,128]{3,2,1,0:T(8,128)S(1)} custom-call(s32[5]{0:T(128)S(1)} %pad_add_fusion.scalars, bf16[16,48,512]{2,1,0:T(8,128)(2,1)S(1)} %collective-permute-done.1.cot_behind, bf16[16,48,512]{2,1,0:T(8,128)(2,1)S(1)} %maximum_select_fusion.cot_here, bf16[16,48,512]{2,1,0:T(8,128)(2,1)S(1)} %collective-permute-done.2.cot_ahead, ...), custom_call_target="tpu_custom_call" | custom-call | flops 1415577600 | bytes 6528512 | tf_op jit(solution)/shard_map/pallas_call | solution.py:321
  92.3 3.9 %all-to-all-start.2 = ((f32[32,2,8,128]{3,2,1,0:T(8,128)}), f32[32,2,8,128]{3,2,1,0:T(8,128)S(1)}, u32[]{:S(2)}, u32[]{:S(2)}) async-start(f32[32,2,8,128]{3,2,1,0:T(8,128)} %bitcast.73), calls=%async_computation.2 | async-start | bytes 524288 | tf_op jit(solution)/shard_map/all_to_all | solution.py:395
  96.3 11.9 %all-to-all-done.2 = f32[32,2,8,128]{3,2,1,0:T(8,128)S(1)} async-done(((f32[32,2,8,128]{3,2,1,0:T(8,128)}), f32[32,2,8,128]{3,2,1,0:T(8,128)S(1)}, u32[]{:S(2)}, u32[]{:S(2)}) %all-to-all-start.2) | async-done | bytes 262176 | tf_op jit(solution)/shard_map/all_to_all | solution.py:395
  108.2 6.3 %collective-permute-start.4 = (f32[2,8,128]{2,1,0:T(8,128)S(1)}, f32[2,8,128]{2,1,0:T(8,128)S(1)}, u32[]{:S(2)}, u32[]{:S(2)}) collective-permute-start(f32[2,8,128]{2,1,0:T(8,128)S(1)} %get-tuple-element.83), channel_id=1, source_target_pairs={{0,64},{2,66},{4,68},{6,70},{8,72},{10,74},{12,76},{14,78},{16,80}... | collective-permute-start | bytes 24584 | tf_op jit(solution)/shard_map/ppermute | solution.py:36
  114.6 1.9 %collective-permute-start.3 = (f32[2,8,128]{2,1,0:T(8,128)S(1)}, f32[2,8,128]{2,1,0:T(8,128)S(1)}, u32[]{:S(2)}, u32[]{:S(2)}) collective-permute-start(f32[2,8,128]{2,1,0:T(8,128)S(1)} %get-tuple-element.82), channel_id=1, source_target_pairs={{0,32},{2,34},{4,36},{6,38},{8,40},{10,42},{12,44},{14,46},{16,48}... | collective-permute-start | bytes 24584 | tf_op jit(solution)/shard_map/ppermute | solution.py:36
  116.5 0.9 copy.113
  117.4 5.7 %collective-permute-done.3 = f32[2,8,128]{2,1,0:T(8,128)S(1)} collective-permute-done((f32[2,8,128]{2,1,0:T(8,128)S(1)}, f32[2,8,128]{2,1,0:T(8,128)S(1)}, u32[]{:S(2)}, u32[]{:S(2)}) %collective-permute-start.3) | collective-permute-done | bytes 8224 | tf_op jit(solution)/shard_map/ppermute | solution.py:36
  (115 shorter events, 6.0 us)
Async XLA Ops:
  0.6 24.5 %copy-start.2 = (bf16[512,24]{0,1:T(8,128)(2,1)S(1)}, bf16[512,24]{0,1:T(8,128)(2,1)}, u32[]{:S(2)}) copy-start(bf16[512,24]{0,1:T(8,128)(2,1)} %param.15) | copy-start | bytes 73732
  0.6 24.5 %copy-start.3 = (bf16[512,24]{0,1:T(8,128)(2,1)S(1)}, bf16[512,24]{0,1:T(8,128)(2,1)}, u32[]{:S(2)}) copy-start(bf16[512,24]{0,1:T(8,128)(2,1)} %param.14) | copy-start | bytes 73732
  0.7 31.9 %copy-start.1 = (bf16[2,9,48,48]{3,2,1,0:T(8,128)(2,1)S(1)}, bf16[2,9,48,48]{3,2,1,0:T(8,128)(2,1)}, u32[]{:S(2)}) copy-start(bf16[2,9,48,48]{3,2,1,0:T(8,128)(2,1)} %param.17) | copy-start | bytes 248836
  5.2 32.3 %all-to-all-start = ((f32[32,2,8,128]{3,2,1,0:T(8,128)}), f32[32,2,8,128]{3,2,1,0:T(8,128)S(1)}, u32[]{:S(2)}, u32[]{:S(2)}) async-start(f32[32,2,8,128]{3,2,1,0:T(8,128)} %broadcast_in_dim.153), calls=%async_computation | async-start | bytes 524288 | tf_op jit(solution)/shard_map/all_to_all | solution.py:404
  25.3 25.3 %collective-permute-start = (bf16[17,24,512]{2,1,0:T(8,128)(2,1)S(1)}, bf16[17,24,512]{2,1,0:T(8,128)(2,1)S(1)}, u32[]{:S(2)}, u32[]{:S(2)}) collective-permute-start(bf16[17,24,512]{2,1,0:T(8,128)(2,1)S(1)} %pad_maximum_fusion), channel_id=1, source_target_pairs={{0,1},{1,0},{2,3},{3,2},{4,5},{5,4},{6,7},{7,6},{8,9},{9,8},{10,11... | collective-permute-start | bytes 1253384 | tf_op jit(solution)/shard_map/ppermute | solution.py:44
  35.8 12.9 %copy-start.6 = (s32[2]{0:T(128)S(1)}, s32[2]{0:T(128)}, u32[]{:S(2)}) copy-start(s32[2]{0:T(128)} %param.13) | copy-start | bytes 28
  35.8 13.0 %copy-start.5 = (f32[2,24]{1,0:T(2,128)S(1)}, f32[2,24]{1,0:T(2,128)}, u32[]{:S(2)}) copy-start(f32[2,24]{1,0:T(2,128)} %param.18) | copy-start | bytes 580
  39.1 19.2 %all-to-all-start.1 = ((f32[16,3,8,128]{3,2,1,0:T(8,128)}), f32[16,3,8,128]{3,2,1,0:T(8,128)S(1)}, u32[]{:S(2)}, u32[]{:S(2)}) async-start(f32[16,3,8,128]{3,2,1,0:T(8,128)} %maximum_maximum_fusion), calls=%async_computation.1 | async-start | bytes 393216 | tf_op jit(solution)/shard_map/all_to_all | solution.py:388
  49.4 19.5 %copy-start.4 = (pred[512]{0:T(512)(128)(4,1)S(1)}, pred[512]{0:T(512)(128)(4,1)}, u32[]{:S(2)}) copy-start(pred[512]{0:T(512)(128)(4,1)} %constant.104.clone.1) | copy-start | bytes 1540
  49.6 19.4 %copy-start = (f32[24,512]{1,0:T(8,128)S(1)}, f32[24,512]{1,0:T(8,128)}, u32[]{:S(2)}) copy-start(f32[24,512]{1,0:T(8,128)} %bias_here.1) | copy-start | bytes 147460
  58.5 25.4 %collective-permute-start.1 = (bf16[16,48,512]{2,1,0:T(8,128)(2,1)S(1)}, bf16[16,48,512]{2,1,0:T(8,128)(2,1)S(1)}, u32[]{:S(2)}, u32[]{:S(2)}) collective-permute-start(bf16[16,48,512]{2,1,0:T(8,128)(2,1)S(1)} %maximum_select_fusion.cot_here), channel_id=1, source_target_pairs={{0,2},{2,4},{4,6},{6,8},{8,10},{10,12},{12,14},{14,16},{16,18},{18... | collective-permute-start | bytes 2359304 | tf_op jit(solution)/shard_map/ppermute | solution.py:36
  60.5 23.3 %collective-permute-start.2 = (bf16[16,48,512]{2,1,0:T(8,128)(2,1)S(1)}, bf16[16,48,512]{2,1,0:T(8,128)(2,1)S(1)}, u32[]{:S(2)}, u32[]{:S(2)}) collective-permute-start(bf16[16,48,512]{2,1,0:T(8,128)(2,1)S(1)} %maximum_select_fusion.cot_here), channel_id=1, source_target_pairs={{2,0},{4,2},{6,4},{8,6},{10,8},{12,10},{14,12},{16,14},{18,16},{20... | collective-permute-start | bytes 2359304 | tf_op jit(solution)/shard_map/ppermute | solution.py:36
  92.3 15.9 %all-to-all-start.2 = ((f32[32,2,8,128]{3,2,1,0:T(8,128)}), f32[32,2,8,128]{3,2,1,0:T(8,128)S(1)}, u32[]{:S(2)}, u32[]{:S(2)}) async-start(f32[32,2,8,128]{3,2,1,0:T(8,128)} %bitcast.73), calls=%async_computation.2 | async-start | bytes 524288 | tf_op jit(solution)/shard_map/all_to_all | solution.py:395
  108.2 15.0 %collective-permute-start.4 = (f32[2,8,128]{2,1,0:T(8,128)S(1)}, f32[2,8,128]{2,1,0:T(8,128)S(1)}, u32[]{:S(2)}, u32[]{:S(2)}) collective-permute-start(f32[2,8,128]{2,1,0:T(8,128)S(1)} %get-tuple-element.83), channel_id=1, source_target_pairs={{0,64},{2,66},{4,68},{6,70},{8,72},{10,74},{12,76},{14,78},{16,80}... | collective-permute-start | bytes 24584 | tf_op jit(solution)/shard_map/ppermute | solution.py:36
  114.6 8.6 %collective-permute-start.3 = (f32[2,8,128]{2,1,0:T(8,128)S(1)}, f32[2,8,128]{2,1,0:T(8,128)S(1)}, u32[]{:S(2)}, u32[]{:S(2)}) collective-permute-start(f32[2,8,128]{2,1,0:T(8,128)S(1)} %get-tuple-element.82), channel_id=1, source_target_pairs={{0,32},{2,34},{4,36},{6,38},{8,40},{10,42},{12,44},{14,46},{16,48}... | collective-permute-start | bytes 24584 | tf_op jit(solution)/shard_map/ppermute | solution.py:36

commit v4 on v3

--- a/solution.py
+++ b/solution.py
@@ -123,49 +123,134 @@
     return cdf + values * (inv_sqrt_2pi * jnp.exp(-0.5 * values * values))
 
 
+def fetch(sems, *pairs):
+    copies = [pltpu.make_async_copy(a, b, sems.at[k]) for k, (a, b) in enumerate(pairs)]
+    for copy in copies:
+        copy.start()
+    for copy in copies:
+        copy.wait()
+
+
+def lay_slabs(target, row, slabs):
+    lanes = lane_ids()
+    per_tile = LANES // SPARE
+    for j, pieces in enumerate(slabs):
+        for k in range(0, len(pieces), per_tile):
+            block = jnp.zeros((8, LANES), jnp.float32)
+            for t, (tile, at) in enumerate(pieces[k : k + per_tile]):
+                block = jnp.where(lanes // SPARE == t, pltpu.roll(tile, (t - at) % per_tile * SPARE, 1), block)
+            target[row + 8 * j : row + 8 * (j + 1), k * SPARE : k * SPARE + LANES] = block
+
+
+def chunk_kernel(scalars, tile, ahead_1, ahead_2, edge, conv_bias, bias, weights, chunks, last_slab):
+    member = scalars[4]
+    lanes = lane_ids()
+    members = chunks.shape[0]
+    own = bias.shape[0]
+    wide = 2 * own
+    slabs = own // 8
+
+    def slabs_of(ref):
+        turn = lax.rem(ref.shape[1] - member * SPARE, ref.shape[1])
+        piece = pltpu.roll(ref[...], turn, 1)[:, :LANES]
+        return [piece[8 * j : 8 * (j + 1)] for j in range(slabs)]
+
+    weight = [pltpu.roll(slab, 3 * SPARE, 1) for slab in slabs_of(weights)]
+    last_slab[...] = jnp.where(lanes >= 3 * SPARE, weight[2], 0.0)
+    third = jnp.zeros((8, LANES), jnp.float32)
+    for j, slab in enumerate(slabs_of(bias)):
+        third = jnp.where(lanes // SPARE == j, pltpu.roll(slab, j * SPARE, 1), third)
+        third = jnp.where(lanes == slabs * SPARE + j, conv_bias[8 * j : 8 * (j + 1), 0:1], third)
+    held = [edge[...], tile[...], ahead_1[...], ahead_2[...], edge[...]]
+    first = [pltpu.roll(block, LANES - wide, 1) for block in held]
+    near = [pltpu.roll(block, wide, 1) for block in held[:3]]
+    one = [jnp.where(lanes < wide, first[k], jnp.where(lanes < 2 * wide, held[k + 1], weight[0])) for k in range(3)]
+    for to in range(members):
+        before = (member == members - 1) & (to == 0)
+        after_last = (member == 0) & (to == members - 1)
+        start = jnp.where(before, 0, jnp.where(member < to - 1, 2, 1))
+
+        def chosen(blocks):
+            return jnp.where(start == 0, blocks[0], jnp.where(start == 1, blocks[1], blocks[2]))
+
+        near_to = jnp.where(before, near[0], jnp.where(after_last, near[2], near[1]))
+        two = jnp.where(lanes < wide, chosen(first[2:]), jnp.where(lanes < 2 * wide, near_to, weight[1]))
+        one_to = chosen(one)
+        for c in range(2):
+            chunks[to, c, 0] = one_to
+            chunks[to, c, 1] = two
+            chunks[to, c, 2] = third
+
+
+def last_kernel(scalars, part, ahead_1, ahead_2, terms, recv, weights, out, wide_weights, other):
+    chan = scalars[5]
+    lanes = lane_ids()
+    own = weights.shape[0]
+    wide = 2 * own
+    half = weights.shape[1] // 2
+    members = terms.shape[0]
+    slabs = [[(terms[k, 1 - chan, j], 3) for k in range(members)] for j in range(2)]
+    slabs.append([(recv[k, 1 - chan, 0], 3) for k in range(members)])
+    lay_slabs(other, 0, slabs)
+    total = jnp.zeros((part.shape[2], 2 * half), jnp.float32)
+    wide_weights[...] = jnp.zeros_like(wide_weights)
+    for source, c in ((weights, chan), (other, 1 - chan)):
+        for k, block in enumerate((source[:, half:], source[:, :half])):
+            wide_weights[2 * k * own : (2 * k + 1) * own, :half] = block
+            wide_weights[(2 * k + 1) * own : (2 * k + 2) * own, half:] = block
+        far = part[c, 0] + pltpu.roll(ahead_1[c], LANES - wide, 1) + ahead_2[c]
+        sums = jnp.where(lanes < wide, far, jnp.where(lanes < 2 * wide, part[c, 1], 0.0))
+        total += jnp.dot(
+            sums.astype(jnp.bfloat16),
+            wide_weights[...].astype(jnp.bfloat16),
+            preferred_element_type=jnp.float32,
+        )
+    out[...] = jnp.concatenate((total[:, :half], total[:, half:]), axis=0).astype(out.dtype)
+
+
 def forward_kernel(
-    total_rows, scalars, terms, bias_other, bias_here, conv_bias, taps,
+    total_rows, scalars, conv_bias, terms_at, bias_at, taps_at,
     pair_out, slope_0, slope_1, pair_0, act_0, act_1, pair_1, far_rows, near_rows, far, near, bias,
+    terms, taps, sems,
 ):
-    band_width, first_row, step_0, step_1, member = (scalars[k] for k in range(5))
+    band_width, first_row, step_0, step_1, member, chan = (scalars[k] for k in range(6))
     lanes = lane_ids()
     rows, own, width = pair_out.shape
     chans = 2 * own
     count = width // LANES
     members = terms.shape[0]
     taps_0, taps_1 = taps.at[: 5 * chans], taps.at[5 * chans :]
+    fetch(sems, (terms_at, terms), (bias_at, bias.at[:own]), (taps_at, taps))
     slabs = own // 8
-    per_tile = LANES // SPARE
-
-    bias[:own] = bias_here[...]
-    for k in range(count):
-        for j in range(slabs):
-            block = jnp.zeros((8, LANES), jnp.float32)
-            for t in range(per_tile):
-                piece = pltpu.roll(bias_other[k * per_tile + t], (t - j) % per_tile * SPARE, 1)
-                block = jnp.where(lanes // SPARE == t, piece, block)
-            bias[own + 8 * j : own + 8 * (j + 1), k * LANES : (k + 1) * LANES] = block
-    first = slabs * SPARE
+
+    lay_slabs(bias, own, [[(terms[k, 1 - chan, 2], j) for k in range(members)] for j in range(slabs)])
+    last = terms[0, 1 - chan, 2]
     bias_0 = jnp.concatenate(
-        [conv_bias[:, 0:1]] + [bias_other[0, :, first + j : first + j + 1] for j in range(slabs)], axis=0
+        [conv_bias[:, 0:1]] + [last[:, k : k + 1] for k in range(slabs * SPARE, slabs * SPARE + slabs)], axis=0
     )
     bias_1 = conv_bias[:, 1:2]
 
     far_rows[...] = jnp.zeros_like(far_rows)
     near_rows[...] = jnp.zeros_like(near_rows)
     half = rows // 2
+
+    def lay_rows(target, place, source, tile, first):
+        here, other = terms[source, chan, tile], terms[source, 1 - chan, tile]
+        for h in range(2):
+            from_lane = first + h * own
+            joined = jnp.where(
+                lanes < own,
+                pltpu.roll(here, (LANES - from_lane) % LANES, 1),
+                pltpu.roll(other, (LANES + own - from_lane) % LANES, 1),
+            )
+            target[place * rows + h * half : place * rows + (h + 1) * half] = joined
+
     for place in range(width // rows + 3):
         source = lax.rem(member + (members - 1 + place), members)
-        tile = terms[source, place // members]
-        far_rows[place * rows : place * rows + half] = tile
-        far_rows[place * rows + half : (place + 1) * rows] = pltpu.roll(tile, LANES - chans, 1)
+        j = place // members
+        lay_rows(far_rows, place, source, j // 2, j % 2 * 2 * own)
         if place < 3:
-            tile = jnp.zeros((half, LANES), jnp.float32)
-            for j in range(3):
-                part = pltpu.roll(terms[source, j], SPARE * (j + 1), 1)
-                tile = jnp.where(lanes // SPARE == j, part, tile)
-            near_rows[place * rows : place * rows + half] = tile
-            near_rows[place * rows + half : (place + 1) * rows] = pltpu.roll(tile, LANES - chans, 1)
+            lay_rows(near_rows, place, source, 1, 2 * own)
     for k in range(count + 1):
         span = slice(k * LANES, (k + 1) * LANES)
         far[:, span] = far_rows[span].T[:chans]
@@ -233,8 +318,8 @@
 
 
 def backward_kernel(
-    total_rows, scalars, cot_behind, cot_here, cot_ahead, slope_0, slope_1, taps,
-    far_terms, grad_2, grad_1, low_1, near_sum, far_sum, far_rows,
+    total_rows, scalars, slope_0, slope_1, last_slab, cot_behind, cot_here, cot_ahead, taps_at,
+    far_terms, grad_2, grad_1, low_1, near_sum, far_sum, far_rows, taps, sems,
 ):
     band_width, first_row, step_0, step_1, member = (scalars[k] for k in range(5))
     lanes = lane_ids()
@@ -248,13 +333,13 @@
         limit = limit_of(row, first_row, band_width, total_rows)
         return [lanes + k * LANES < limit for k in range(count)]
 
-    def lay(index, _):
-        grad_2[index] = cot_behind[index]
-        grad_2[index + rows] = cot_here[index]
-        grad_2[index + 2 * rows] = cot_ahead[index]
-        return 0
-
-    lax.fori_loop(0, rows, lay, 0)
+    fetch(
+        sems,
+        (cot_behind, grad_2.at[:rows]),
+        (cot_here, grad_2.at[rows : 2 * rows]),
+        (cot_ahead, grad_2.at[2 * rows :]),
+        (taps_at, taps),
+    )
 
     def layer_1(block, _):
         first = block * GROUP
@@ -306,22 +391,27 @@
 
     for r in range(members):
         pieces = halves(r) + halves(members + r)
-        far_terms[r, 0] = sum(
-            [pltpu.roll(piece, k * own, 1) for k, piece in enumerate(pieces) if k], pieces[0]
-        )
+        one = sum([pltpu.roll(piece, k * own, 1) for k, piece in enumerate(pieces) if k], pieces[0])
+        one = one + last_slab[...]
         pieces = halves(2 * members + r)
         own_place = jnp.where(member == r, near_terms, 0.0)
-        far_terms[r, 1] = pieces[0] + pltpu.roll(pieces[1], own, 1) + own_place
-
-
-def call(kernel, out_shapes, scratch, flops, smem, *arrays):
+        two = pieces[0] + pltpu.roll(pieces[1], own, 1) + own_place
+        for c in range(2):
+            far_terms[r, c, 0] = one
+            far_terms[r, c, 1] = two
+
+
+def call(kernel, out_shapes, scratch, flops, smem, near_arrays, far_arrays=()):
+    arrays = tuple(near_arrays) + tuple(far_arrays)
     bytes_accessed = sum(a.size * a.dtype.itemsize for a in arrays)
     bytes_accessed += sum(s.size * s.dtype.itemsize for s in out_shapes)
     vmem = pl.BlockSpec(memory_space=pltpu.VMEM)
     return pl.pallas_call(
         kernel,
         out_shape=out_shapes,
-        in_specs=[pl.BlockSpec(memory_space=pltpu.SMEM)] + [vmem] * len(arrays),
+        in_specs=[pl.BlockSpec(memory_space=pltpu.SMEM)]
+        + [vmem] * len(near_arrays)
+        + [pl.BlockSpec(memory_space=pl.ANY)] * len(far_arrays),
         out_specs=[vmem] * len(out_shapes),
         scratch_shapes=scratch,
         compiler_params=pltpu.CompilerParams(vmem_limit_bytes=32 * 2**20),
@@ -331,10 +421,36 @@
     )(smem, *arrays)
 
 
-def forward_call(total_rows, rows, scalars, terms, bias_other, bias_here, conv_bias, taps):
+f32 = functools.partial(jax.ShapeDtypeStruct, dtype=jnp.float32)
+
+
+def chunk_call(members, scalars, tile, ahead_1, ahead_2, edge, conv_bias, bias, weights):
+    return call(
+        chunk_kernel,
+        (f32((members, 2, 3) + tile.shape), f32(tile.shape)),
+        [],
+        0,
+        scalars,
+        (tile, ahead_1, ahead_2, edge, conv_bias, bias, weights),
+    )
+
+
+def last_call(scalars, part, ahead_1, ahead_2, terms, recv, weights):
+    own, width = weights.shape
+    (out,) = call(
+        last_kernel,
+        (jax.ShapeDtypeStruct((2 * part.shape[2], width // 2), jnp.bfloat16),),
+        [pltpu.VMEM((LANES, width), jnp.float32), pltpu.VMEM((own, width), jnp.float32)],
+        0,
+        scalars,
+        (part, ahead_1, ahead_2, terms, recv, weights),
+    )
+    return out
+
+
+def forward_call(total_rows, rows, scalars, terms, bias_here, conv_bias, taps):
     own, width = bias_here.shape
     chans = 2 * own
-    f32 = functools.partial(jax.ShapeDtypeStruct, dtype=jnp.float32)
     return call(
         functools.partial(forward_kernel, total_rows),
         (f32((rows, own, width)), f32((rows, own, width)), f32((rows + HALO, chans, width))),
@@ -348,20 +464,24 @@
             pltpu.VMEM((chans, width + LANES), jnp.float32),
             pltpu.VMEM((chans, LANES), jnp.float32),
             pltpu.VMEM((chans, width), jnp.float32),
+            pltpu.VMEM(terms.shape, terms.dtype),
+            pltpu.VMEM(taps.shape, taps.dtype),
+            pltpu.SemaphoreType.DMA((3,)),
         ],
         2 * 15 * chans * chans * width * 40,
-        scalars, terms, bias_other, bias_here, conv_bias, taps,
-    )
-
-
-def backward_call(total_rows, members, scalars, cot_behind, cot, cot_ahead, slope_0, slope_1, taps):
+        scalars,
+        (conv_bias,),
+        (terms, bias_here, taps),
+    )
+
+
+def backward_call(total_rows, members, scalars, cot_behind, cot, cot_ahead, slope_0, slope_1, last_slab, taps):
     rows, chans, width = cot.shape
     own = chans // 2
     slots = members + (width + LANES) // rows
-    f32 = functools.partial(jax.ShapeDtypeStruct, dtype=jnp.float32)
-    return call(
+    (terms,) = call(
         functools.partial(backward_kernel, total_rows),
-        (f32((members, 2, rows // 2, LANES)),),
+        (f32((members, 2, 2, rows // 2, LANES)),),
         [
             pltpu.VMEM((rows + 2 * HALO, chans, width), jnp.bfloat16),
             pltpu.VMEM((rows + HALO, own, width), jnp.float32),
@@ -369,83 +489,40 @@
             pltpu.VMEM((LANES, LANES), jnp.float32),
             pltpu.VMEM((LANES, width + LANES), jnp.float32),
             pltpu.VMEM((slots * rows, LANES), jnp.float32),
+            pltpu.VMEM(taps.shape, taps.dtype),
+            pltpu.SemaphoreType.DMA((4,)),
         ],
         2 * 15 * chans * chans * width * 40,
-        scalars, cot_behind, cot, cot_ahead, slope_0, slope_1, taps,
-    )
-
-
-def group_sizes(blocks, devices):
-    members = blocks // 2
-    return members, devices // members
-
-
-def exchange_in_group(chunks, both_halves=False):
+        scalars,
+        (slope_0, slope_1, last_slab),
+        (cot_behind, cot, cot_ahead, taps),
+    )
+    return terms
+
+
+def exchange_in_group(chunks):
     members = chunks.shape[0]
-    count = lax.axis_size("chrom")
-    if not both_halves:
-        lists = [[q * members + k for k in range(members)] for q in range(count // members)]
-        return lax.all_to_all(chunks, "chrom", 0, 0, axis_index_groups=lists)
     lists = [
         [2 * (q * members + k) + c for k in range(members) for c in range(2)]
-        for q in range(count // members)
+        for q in range(lax.axis_size("chrom") // members)
     ]
-    twice = jnp.broadcast_to(chunks[:, None], (members, 2) + chunks.shape[1:])
-    twice = twice.reshape((2 * members,) + chunks.shape[1:])
-    recv = lax.all_to_all(twice, ("chrom", "chan"), 0, 0, axis_index_groups=lists)
-    return recv.reshape((members, 2) + chunks.shape[1:])
-
-
-def exchange_across_groups(chunks, members):
-    groups = chunks.shape[0] // 2
-    lists = [
-        [2 * (t * members + r) + c for t in range(groups) for c in range(2)] for r in range(members)
-    ]
-    return lax.all_to_all(chunks, ("chrom", "chan"), 0, 0, axis_index_groups=lists)
-
-
-def window_terms(proj, distance_bias, conv_bias, members, groups, group, member, chan):
-    own = proj.shape[1] // 2
-    half = proj.shape[0] // 2
-    slabs = own // 8
-    tile = jnp.concatenate((proj[:half], proj[half:]), axis=1)
-    tile = jnp.pad(tile, ((0, 0), (0, LANES - tile.shape[1])))
-    piece = lax.dynamic_slice_in_dim(distance_bias, group * SPARE, SPARE, 1)
-    piece = [piece[8 * j : 8 * (j + 1)] for j in range(slabs)] + [conv_bias[0].reshape(slabs, 8).T]
-    piece = jnp.concatenate(piece, axis=1)
-    piece = jnp.pad(piece, ((0, 0), (0, LANES - piece.shape[1])))
-    sent = jnp.broadcast_to(jnp.stack((tile, piece)), (2 * groups, 2, half, LANES))
-    recv = exchange_across_groups(sent, members).reshape(groups, 2, 2, half, LANES)
-    bias_other = lax.dynamic_index_in_dim(recv, 1 - chan, 1, keepdims=False)[:, 1]
-    held = recv[:, :, 0]
-    held = jnp.where(chan == 0, held, held[:, ::-1])
-    held = lax.dynamic_slice_in_dim(jnp.pad(held, ((1, 3), (0, 0), (0, 0), (0, 0))), group, 5, 0)
-
-    def joined(first):
-        pieces = [
-            held[:, c, :, 2 * own * h + first : 2 * own * h + first + own] for h in range(2) for c in range(2)
-        ]
-        return jnp.concatenate(pieces, axis=2)
-
-    near, far = joined(0), joined(own)
-    to = jnp.arange(members, dtype=jnp.int32)[:, None, None, None]
-    before = (member == members - 1) & (to == 0)
-    after = (member == 0) & (to == members - 1)
-    start = jnp.where(before, 0, jnp.where(member < to - 1, 2, 1))
-    far = jnp.where(start == 0, far[None, 0:3], jnp.where(start == 1, far[None, 1:4], far[None, 2:5]))
-    near = jnp.where(before, near[None, 0:1], jnp.where(after, near[None, 2:3], near[None, 1:2]))
-    near = [near[:, :, :, SPARE * j : SPARE * (j + 1)] for j in range(3)]
-    return sent, jnp.concatenate((far, jnp.concatenate(near, axis=1)), axis=3), bias_other
-
-
-def summed_terms(chunks, own):
-    members = chunks.shape[0]
-    part = jnp.sum(exchange_in_group(chunks, both_halves=True), axis=0)
-    ahead_1 = from_ahead(part[:, 0], -members)
-    ahead_2 = from_ahead(part[:, 1], -2 * members)
-    lanes = jnp.arange(LANES, dtype=jnp.int32)
-    far = part[:, 0] + jnp.roll(ahead_1, -2 * own, axis=2) + ahead_2
-    return jnp.where(lanes < 2 * own, far, jnp.where(lanes < 4 * own, part[:, 1], 0))
+    flat = chunks.reshape((2 * members,) + chunks.shape[2:])
+    recv = lax.all_to_all(flat, ("chrom", "chan"), 0, 0, axis_index_groups=lists)
+    return recv.reshape(chunks.shape)
+
+
+def from_edges(block, members):
+    count = lax.axis_size("chrom")
+    route = [(i + 3 * members, i) for i in range(0, count - 3 * members, members)]
+    route += [(i - members, i) for i in range(2 * members - 1, count, members)]
+    return lax.ppermute(block, "chrom", route)
+
+
+def projection_tile(features, near_weight, far_weight):
+    half = features.shape[0] // 2
+    parts = [jnp.dot(features, w, preferred_element_type=jnp.float32) for w in (near_weight, far_weight)]
+    tile = jnp.concatenate([p[h * half : (h + 1) * half] for p in parts for h in range(2)], axis=1)
+    return jnp.pad(tile, ((0, 0), (0, LANES - tile.shape[1])))
 
 
 def shards(
@@ -460,51 +537,39 @@
     place = lax.axis_index("chrom")
     first_row = place * rows
     total_rows = lax.axis_size("chrom") * rows
-    members, groups = group_sizes(width // rows, lax.axis_size("chrom"))
-    group, member = place // members, place % members
+    members = width // rows // 2
+    member = place % members
     row_ids = first_row + jnp.arange(rows, dtype=jnp.int32)
-    scalars = jnp.stack([band_width[0], first_row, dilations[0], dilations[1], member]).astype(jnp.int32)
+    scalars = jnp.stack([band_width[0], first_row, dilations[0], dilations[1], member, chan]).astype(jnp.int32)
 
     features = (
         embedding.astype(jnp.float32) + encode(row_ids, window_start[0], embedding.shape[1])
     ).astype(jnp.bfloat16)
-    both = jnp.concatenate((near_weight, far_weight), axis=1)
-    proj = jnp.dot(features, both, preferred_element_type=jnp.float32)
-    sent, chunks, bias_other = window_terms(
-        proj, distance_bias, conv_bias, members, groups, group, member, chan
-    )
-    terms = exchange_in_group(chunks)
+    tile = projection_tile(features, near_weight, far_weight)
+    ahead = from_ahead(tile, members), from_ahead(tile, 2 * members), from_edges(tile, members)
 
     def weight_rows(half):
         parts = [
             lax.dynamic_slice_in_dim(w, half * features_half, features_half, 0).T
             for w in (near_weight, far_weight)
         ]
-        return jnp.concatenate(parts, axis=1)
-
-    cot_here = jnp.swapaxes(cotangent, 0, 1)
-    mixed = jnp.concatenate((cot_here, weight_rows(1 - chan)[None]), axis=0)
-    mixed = from_partner(after(mixed, sent))
+        return jnp.concatenate(parts, axis=1).astype(jnp.float32)
+
+    conv_columns = conv_bias.T
+    chunks, last_slab = chunk_call(
+        members, scalars, tile, *ahead, conv_columns, distance_bias, weight_rows(1 - chan)
+    )
+    terms = exchange_in_group(chunks)
+
+    cot_other = from_partner(cotangent)
     offsets = jnp.arange(width, dtype=jnp.int32)
     keep = (offsets[None, :] < band_width[0]) & (row_ids[:, None] + offsets[None, :] < total_rows)
-    mixed = after(mixed, terms)
-    cot = jnp.concatenate((cot_here, mixed[:rows]), axis=1)
-    cot = jnp.where(keep[:, None, :], cot, 0).astype(jnp.bfloat16)
+    cot = jnp.concatenate((cotangent, after(cot_other, chunks)), axis=0)
+    cot = jnp.where(keep[:, None, :], jnp.swapaxes(cot, 0, 1), 0).astype(jnp.bfloat16)
     cot_behind = from_ahead(cot, -1)
     cot_ahead = from_ahead(cot, 1)
 
-    here, other = weight_rows(chan), mixed[rows]
-    back_project = []
-    for cols in (jnp.where(chan == 0, here, other), jnp.where(chan == 0, other, here)):
-        near_rows, far_rows = cols[:, :features_half], cols[:, features_half:]
-        gap = jnp.zeros((own, features_half), cols.dtype)
-        rest = jnp.zeros((LANES - 4 * own, 2 * features_half), cols.dtype)
-        for block in (far_rows, near_rows):
-            back_project.append(jnp.concatenate((block, gap), axis=1))
-            back_project.append(jnp.concatenate((gap, block), axis=1))
-        back_project.append(rest)
-    back_project = jnp.concatenate(back_project, axis=0)
-
+    conv_weight = after(conv_weight, chunks)
     twice = jnp.concatenate((conv_weight, conv_weight), axis=2)
     twice = jnp.concatenate((twice, twice), axis=3)
     turned = lax.dynamic_slice(twice, (0, 0, chan * own, chan * own), conv_weight.shape)
@@ -517,17 +582,18 @@
     )
 
     pair_rows, slope_0, slope_1 = forward_call(
-        total_rows, rows, scalars, terms, bias_other, distance_bias, conv_bias.T, taps_ahead
+        total_rows, rows, scalars, terms, distance_bias, conv_columns, taps_ahead
     )
     pair_out = jnp.swapaxes(pair_rows.astype(jnp.bfloat16), 0, 1)
-    (terms_back,) = backward_call(
-        total_rows, members, scalars, cot_behind, cot, cot_ahead, slope_0, slope_1, taps_back
-    )
-    sums = summed_terms(terms_back, own)
-    lows = jnp.concatenate((sums[0], sums[1]), axis=1).astype(jnp.bfloat16)
-    grads = jnp.dot(lows, back_project, preferred_element_type=jnp.float32)
-    grads = jnp.concatenate((grads[:, :features_half], grads[:, features_half:]), axis=0)
-    return (pair_out, grads.astype(jnp.bfloat16))
+    terms_back = backward_call(
+        total_rows, members, scalars, cot_behind, cot, cot_ahead, slope_0, slope_1, last_slab, taps_back
+    )
+    recv = exchange_in_group(terms_back)
+    part = jnp.sum(recv, axis=0)
+    ahead_1 = from_ahead(part[:, 0], -members)
+    ahead_2 = from_ahead(part[:, 1], -2 * members)
+    grads = last_call(scalars, part, ahead_1, ahead_2, terms, recv, weight_rows(chan))
+    return (pair_out, grads)
 
 
 def solution(mesh):

time: 125 us -> 116 us (0.928)
  waiting for transfers between devices: 30.2 us -> 17.4 us
  Pallas kernels: 20.3 us -> 24.5 us
  local copies, waits for them, and re-layouts: 7.52 us -> 11.2 us
  starting transfers between devices: 58.2 us -> 55.3 us
  other arithmetic: 4.22 us -> 2.78 us
    all_to_all x3 -> x2, starting transfers between devices: 32.2 us -> 10.2 us  [exchange_in_group(): lax.all_to_all(flat, ('chrom', 'chan'), 0, 0, axis_index_groups=lists)]
    ppermute x4 -> x6, starting transfers between devices: 18.6 us -> 32.7 us  [from_ahead(): return lax.ppermute(block, 'chrom', route)]
    all_to_all x3 -> x2, waiting for transfers between devices: 21.3 us -> 11.4 us  [exchange_in_group(): lax.all_to_all(flat, ('chrom', 'chan'), 0, 0, axis_index_groups=lists)]
    ppermute x0 -> x1, starting transfers between devices: none -> 4.77 us  [from_edges(): return lax.ppermute(block, 'chrom', route)]
    unnamed x33 -> x29, local copies, waits for them, and re-layouts: 2.94 us -> 7.19 us
    pallas_call x2 -> x4, Pallas kernels: 20.3 us -> 24.5 us  [call(): pl.pallas_call(kernel, out_shape=out_shapes, in_specs=[pl.BlockSpec(memor...]
    ppermute x4 -> x6, waiting for transfers between devices: 7.99 us -> 5.94 us  [from_ahead(): return lax.ppermute(block, 'chrom', route)]
    slice x10 -> x2, local copies, waits for them, and re-layouts: 1.75 us -> 0.01 us  [projection_tile(): p[h * half:(h + 1) * half]]
  transfers between devices with their start and end apart: 8 -> 10, of which waited for: 6 -> 4; matrix products, arithmetic and copies ran while one was open for 6% -> 8% of each run, Pallas kernels for 10% -> 13%
where the time goes in v4:
time: 116 us; the launch traced here: 115 us
  starting transfers between devices  55.3 us (48%)
  Pallas kernels  24.5 us (21%)
  waiting for transfers between devices  17.4 us (15%)
  local copies, waits for them, and re-layouts  11.2 us (10%)
  other arithmetic  2.78 us (2%)
  between operations  2.41 us (2%)
  matrix products  1.86 us (2%)
    ppermute x6, starting transfers between devices, from_ahead(): return lax.ppermute(block, 'chrom', route)  32.7 us
    pallas_call x4, Pallas kernels, call(): pl.pallas_call(kernel, out_shape=out_shapes, in_specs=[pl.BlockSpec(memor...  24.5 us
    all_to_all x2, waiting for transfers between devices, exchange_in_group(): lax.all_to_all(flat, ('chrom', 'chan'), 0, 0, axis_index_groups=lists)  11.4 us
    all_to_all x2, starting transfers between devices, exchange_in_group(): lax.all_to_all(flat, ('chrom', 'chan'), 0, 0, axis_index_groups=lists)  10.2 us
    ppermute x1, starting transfers between devices, from_partner(): return lax.ppermute(block, 'chan', [(0, 1), (1, 0)])  7.73 us
    unnamed x29, local copies, waits for them, and re-layouts  7.19 us
    ppermute x6, waiting for transfers between devices, from_ahead(): return lax.ppermute(block, 'chrom', route)  5.94 us
    ppermute x1, starting transfers between devices, from_edges(): return lax.ppermute(block, 'chrom', route)  4.77 us
  transfers between devices with their start and end apart: 10, of which 4 were waited for; matrix products, arithmetic and copies ran while one was open for 8% of the time, Pallas kernels for 13%

profile of v4, /device:TPU:6, one launch (start us, length us, event | category | flops | bytes accessed | tf_op | source)
XLA Modules:
  0.0 115.5 jit_solution(9559904186323766022)
XLA Ops:
  1.7 0.9 fusion.17
  2.6 0.9 fusion.19
  3.6 11.2 %collective-permute-start = (f32[8,128]{1,0:T(8,128)S(1)}, f32[8,128]{1,0:T(8,128)S(1)}, u32[]{:S(2)}, u32[]{:S(2)}) collective-permute-start(f32[8,128]{1,0:T(8,128)S(1)} %select_maximum_fusion.1.tile), channel_id=1, source_target_pairs={{32,0},{34,2},{36,4},{38,6},{40,8},{42,10},{44,12},{46,14},{48,16}... | collective-permute-start | bytes 12296 | tf_op jit(solution)/shard_map/ppermute | solution.py:36
  14.8 1.9 %collective-permute-start.1 = (f32[8,128]{1,0:T(8,128)S(1)}, f32[8,128]{1,0:T(8,128)S(1)}, u32[]{:S(2)}, u32[]{:S(2)}) collective-permute-start(f32[8,128]{1,0:T(8,128)S(1)} %select_maximum_fusion.1.tile), channel_id=1, source_target_pairs={{64,0},{66,2},{68,4},{70,6},{72,8},{74,10},{76,12},{78,14},{80,16}... | collective-permute-start | bytes 12296 | tf_op jit(solution)/shard_map/ppermute | solution.py:36
  16.8 4.8 %collective-permute-start.2 = (f32[8,128]{1,0:T(8,128)S(1)}, f32[8,128]{1,0:T(8,128)S(1)}, u32[]{:S(2)}, u32[]{:S(2)}) collective-permute-start(f32[8,128]{1,0:T(8,128)S(1)} %select_maximum_fusion.1.tile), channel_id=1, source_target_pairs={{96,0},{128,32},{160,64},{192,96},{224,128},{256,160},{288,192},{3... | collective-permute-start | bytes 12296 | tf_op jit(solution)/shard_map/ppermute | solution.py:518
  21.6 1.2 %copy.71 = bf16[24,16,512]{2,0,1:T(8,128)(2,1)S(1)} copy(bf16[24,16,512]{2,1,0:T(8,128)(2,1)} %param.19) | data formatting | bytes 786432 | tf_op args[9]
  22.8 7.7 %collective-permute-start.3 = (bf16[24,16,512]{2,0,1:T(8,128)(2,1)S(1)}, bf16[24,16,512]{2,0,1:T(8,128)(2,1)S(1)}, u32[]{:S(2)}, u32[]{:S(2)}) collective-permute-start(bf16[24,16,512]{2,0,1:T(8,128)(2,1)S(1)} %copy.71), channel_id=1, source_target_pairs={{0,1},{1,0},{2,3},{3,2},{4,5},{5,4},{6,7},{7,6},{8,9},{9,8},{10,11... | collective-permute-start | bytes 1179656 | tf_op jit(solution)/shard_map/ppermute | solution.py:44
  31.2 1.4 %dynamic-slice_bitcast_fusion = (bf16[24,256]{1,0:T(8,128)(2,1)}, bf16[24,256]{1,0:T(8,128)(2,1)S(1)}, bf16[24,256]{1,0:T(8,128)(2,1)S(1)}, bf16[24,256]{1,0:T(8,128)(2,1)}) fusion(bf16[512,24]{0,1:T(8,128)(2,1)} %param.15, s32[]{:T(128)S(6)} %select_n.177, s32[]{:T(128)S(6)} %select_n.173, bf16[512,24]{0,1:T(8,128)(2,1)} %param.14), kind=kLoop, calls=%fused_computation.61 | loop fusion | bytes 98312 | tf_op jit(solution)/shard_map/transpose | solution.py:553
  35.0 1.5 %shard_map.113 = (f32[16,2,3,8,128]{4,3,2,1,0:T(8,128)}, f32[8,128]{1,0:T(8,128)S(1)}) custom-call(s32[6]{0:T(128)S(1)} %stack.15.scalars, f32[8,128]{1,0:T(8,128)S(1)} %select_maximum_fusion.1.tile, f32[8,128]{1,0:T(8,128)S(1)} %collective-permute-done.ahead_1, f32[8,128]{1,0:T(8,128)S(1)} %collective-permute-done.1.ahead_2, ...), custom_call_target="tpu_custom_call" | custom-call | bytes 512192 | tf_op jit(solution)/shard_map/pallas_call | solution.py:409
  38.0 3.9 %all-to-all-start = ((f32[32,3,8,128]{3,2,1,0:T(8,128)}), f32[32,3,8,128]{3,2,1,0:T(8,128)S(1)}, u32[]{:S(2)}, u32[]{:S(2)}) async-start(f32[32,3,8,128]{3,2,1,0:T(8,128)} %bitcast.7), calls=%async_computation | async-start | bytes 786432 | tf_op jit(solution)/shard_map/all_to_all | solution.py:510
  43.3 0.8 copy.69.taps_at
  44.7 2.1 %collective-permute-start.4 = (bf16[16,48,512]{2,1,0:T(8,128)(2,1)S(1)}, bf16[16,48,512]{2,1,0:T(8,128)(2,1)S(1)}, u32[]{:S(2)}, u32[]{:S(2)}) collective-permute-start(bf16[16,48,512]{2,1,0:T(8,128)(2,1)S(1)} %fusion.cot_here), channel_id=1, source_target_pairs={{0,2},{2,4},{4,6},{6,8},{8,10},{10,12},{12,14},{14,16},{16,18},{18... | collective-permute-start | bytes 2359304 | tf_op jit(solution)/shard_map/ppermute | solution.py:36
  46.8 8.3 %collective-permute-start.5 = (bf16[16,48,512]{2,1,0:T(8,128)(2,1)S(1)}, bf16[16,48,512]{2,1,0:T(8,128)(2,1)S(1)}, u32[]{:S(2)}, u32[]{:S(2)}) collective-permute-start(bf16[16,48,512]{2,1,0:T(8,128)(2,1)S(1)} %fusion.cot_here), channel_id=1, source_target_pairs={{2,0},{4,2},{6,4},{8,6},{10,8},{12,10},{14,12},{16,14},{18,16},{20... | collective-permute-start | bytes 2359304 | tf_op jit(solution)/shard_map/ppermute | solution.py:36
  56.3 0.9 copy-done.2
  58.0 13.1 %shard_map.114 = (f32[16,24,512]{2,1,0:T(8,128)S(1)}, f32[16,24,512]{2,1,0:T(8,128)S(1)}, f32[32,48,512]{2,1,0:T(8,128)S(1)}) custom-call(s32[6]{0:T(128)S(1)} %stack.15.scalars, f32[24,2]{1,0:T(8,128)S(1)} %bitcast.134, f32[16,2,3,8,128]{4,3,2,1,0:T(8,128)S(1)} %bitcast.131, f32[24,512]{1,0:T(8,128)S(1)} %copy-done.4, bf16[368,144]{1,0:T(8,128)(2,1)S(1)} %copy-done.2), custom_call_target="tpu_custom_call" | custom-call | flops 1415577600 | bytes 5267136 | tf_op jit(solution)/shard_map/pallas_call | solution.py:409
  71.1 1.2 %collective-permute-done.4.cot_behind = bf16[16,48,512]{2,1,0:T(8,128)(2,1)S(1)} collective-permute-done((bf16[16,48,512]{2,1,0:T(8,128)(2,1)S(1)}, bf16[16,48,512]{2,1,0:T(8,128)(2,1)S(1)}, u32[]{:S(2)}, u32[]{:S(2)}) %collective-permute-start.4) | collective-permute-done | bytes 786464 | tf_op jit(solution)/shard_map/ppermute | solution.py:36
  72.3 8.6 %shard_map.115 = f32[16,2,2,8,128]{4,3,2,1,0:T(8,128)} custom-call(s32[6]{0:T(128)S(1)} %stack.15.scalars, f32[16,24,512]{2,1,0:T(8,128)S(1)} %get-tuple-element.12.slope_0, f32[32,48,512]{2,1,0:T(8,128)S(1)} %get-tuple-element.13.slope_1, f32[8,128]{1,0:T(8,128)S(1)} %copy-done.6, bf16[16,48,512]{2,1,0:T(8,128)(2,1)S(1)} %collective-permute-done.4.cot_behind, ...), custom_call_target="tpu_custom_call" | custom-call | flops 1415577600 | bytes 6663680 | tf_op jit(solution)/shard_map/pallas_call | solution.py:409
  80.9 6.3 %all-to-all-start.1 = ((f32[32,2,8,128]{3,2,1,0:T(8,128)}), f32[32,2,8,128]{3,2,1,0:T(8,128)S(1)}, u32[]{:S(2)}, u32[]{:S(2)}) async-start(f32[32,2,8,128]{3,2,1,0:T(8,128)} %bitcast.57), calls=%async_computation.1 | async-start | bytes 524288 | tf_op jit(solution)/shard_map/all_to_all | solution.py:510
  87.9 11.3 %all-to-all-done.1 = f32[32,2,8,128]{3,2,1,0:T(8,128)S(1)} async-done(((f32[32,2,8,128]{3,2,1,0:T(8,128)}), f32[32,2,8,128]{3,2,1,0:T(8,128)S(1)}, u32[]{:S(2)}, u32[]{:S(2)}) %all-to-all-start.1) | async-done | bytes 262176 | tf_op jit(solution)/shard_map/all_to_all | solution.py:510
  99.2 4.5 %collective-permute-start.6 = (f32[2,8,128]{2,1,0:T(8,128)S(1)}, f32[2,8,128]{2,1,0:T(8,128)S(1)}, u32[]{:S(2)}, u32[]{:S(2)}) collective-permute-start(f32[2,8,128]{2,1,0:T(8,128)S(1)} %get-tuple-element.59), channel_id=1, source_target_pairs={{0,32},{2,34},{4,36},{6,38},{8,40},{10,42},{12,44},{14,46},{16,48}... | collective-permute-start | bytes 24584 | tf_op jit(solution)/shard_map/ppermute | solution.py:36
  103.7 4.6 %collective-permute-start.7 = (f32[2,8,128]{2,1,0:T(8,128)S(1)}, f32[2,8,128]{2,1,0:T(8,128)S(1)}, u32[]{:S(2)}, u32[]{:S(2)}) collective-permute-start(f32[2,8,128]{2,1,0:T(8,128)S(1)} %get-tuple-element.58), channel_id=1, source_target_pairs={{0,64},{2,66},{4,68},{6,70},{8,72},{10,74},{12,76},{14,78},{16,80}... | collective-permute-start | bytes 24584 | tf_op jit(solution)/shard_map/ppermute | solution.py:36
  108.4 0.9 copy.80
  109.3 4.8 %collective-permute-done.7.ahead_2 = f32[2,8,128]{2,1,0:T(8,128)S(1)} collective-permute-done((f32[2,8,128]{2,1,0:T(8,128)S(1)}, f32[2,8,128]{2,1,0:T(8,128)S(1)}, u32[]{:S(2)}, u32[]{:S(2)}) %collective-permute-start.7) | collective-permute-done | bytes 8224 | tf_op jit(solution)/shard_map/ppermute | solution.py:36
  114.1 1.4 %shard_map.116 = bf16[16,256]{1,0:T(8,128)(2,1)} custom-call(s32[6]{0:T(128)S(1)} %stack.15.scalars, f32[2,2,8,128]{3,2,1,0:T(8,128)S(1)} %reduce_sum.9.part, f32[2,8,128]{2,1,0:T(8,128)S(1)} %collective-permute-done.6.ahead_1, f32[2,8,128]{2,1,0:T(8,128)S(1)} %collective-permute-done.7.ahead_2, f32[16,2,3,8,128]{4,3,2,1,0:T(8,128)S(1)} %bitcast.132, ...), custom_call_target="tpu_custom_call" | custom-call | bytes 745472 | tf_op jit(solution)/shard_map/pallas_call | solution.py:409
  (85 shorter events, 8.9 us)
Async XLA Ops:
  0.6 36.4 %copy-start.7 = (bf16[2,9,48,48]{3,2,1,0:T(8,128)(2,1)S(1)}, bf16[2,9,48,48]{3,2,1,0:T(8,128)(2,1)}, u32[]{:S(2)}) copy-start(bf16[2,9,48,48]{3,2,1,0:T(8,128)(2,1)} %param.17) | copy-start | bytes 248836
  3.6 30.5 %collective-permute-start = (f32[8,128]{1,0:T(8,128)S(1)}, f32[8,128]{1,0:T(8,128)S(1)}, u32[]{:S(2)}, u32[]{:S(2)}) collective-permute-start(f32[8,128]{1,0:T(8,128)S(1)} %select_maximum_fusion.1.tile), channel_id=1, source_target_pairs={{32,0},{34,2},{36,4},{38,6},{40,8},{42,10},{44,12},{46,14},{48,16}... | collective-permute-start | bytes 12296 | tf_op jit(solution)/shard_map/ppermute | solution.py:36
  14.8 19.3 %collective-permute-start.1 = (f32[8,128]{1,0:T(8,128)S(1)}, f32[8,128]{1,0:T(8,128)S(1)}, u32[]{:S(2)}, u32[]{:S(2)}) collective-permute-start(f32[8,128]{1,0:T(8,128)S(1)} %select_maximum_fusion.1.tile), channel_id=1, source_target_pairs={{64,0},{66,2},{68,4},{70,6},{72,8},{74,10},{76,12},{78,14},{80,16}... | collective-permute-start | bytes 12296 | tf_op jit(solution)/shard_map/ppermute | solution.py:36
  16.8 17.4 %collective-permute-start.2 = (f32[8,128]{1,0:T(8,128)S(1)}, f32[8,128]{1,0:T(8,128)S(1)}, u32[]{:S(2)}, u32[]{:S(2)}) collective-permute-start(f32[8,128]{1,0:T(8,128)S(1)} %select_maximum_fusion.1.tile), channel_id=1, source_target_pairs={{96,0},{128,32},{160,64},{192,96},{224,128},{256,160},{288,192},{3... | collective-permute-start | bytes 12296 | tf_op jit(solution)/shard_map/ppermute | solution.py:518
  22.8 21.7 %collective-permute-start.3 = (bf16[24,16,512]{2,0,1:T(8,128)(2,1)S(1)}, bf16[24,16,512]{2,0,1:T(8,128)(2,1)S(1)}, u32[]{:S(2)}, u32[]{:S(2)}) collective-permute-start(bf16[24,16,512]{2,0,1:T(8,128)(2,1)S(1)} %copy.71), channel_id=1, source_target_pairs={{0,1},{1,0},{2,3},{3,2},{4,5},{5,4},{6,7},{7,6},{8,9},{9,8},{10,11... | collective-permute-start | bytes 1179656 | tf_op jit(solution)/shard_map/ppermute | solution.py:44
  34.2 0.8 copy-start.3
  36.4 0.6 copy-start.5
  38.0 18.2 %all-to-all-start = ((f32[32,3,8,128]{3,2,1,0:T(8,128)}), f32[32,3,8,128]{3,2,1,0:T(8,128)S(1)}, u32[]{:S(2)}, u32[]{:S(2)}) async-start(f32[32,3,8,128]{3,2,1,0:T(8,128)} %bitcast.7), calls=%async_computation | async-start | bytes 786432 | tf_op jit(solution)/shard_map/all_to_all | solution.py:510
  44.7 27.6 %collective-permute-start.4 = (bf16[16,48,512]{2,1,0:T(8,128)(2,1)S(1)}, bf16[16,48,512]{2,1,0:T(8,128)(2,1)S(1)}, u32[]{:S(2)}, u32[]{:S(2)}) collective-permute-start(bf16[16,48,512]{2,1,0:T(8,128)(2,1)S(1)} %fusion.cot_here), channel_id=1, source_target_pairs={{0,2},{2,4},{4,6},{6,8},{8,10},{10,12},{12,14},{14,16},{16,18},{18... | collective-permute-start | bytes 2359304 | tf_op jit(solution)/shard_map/ppermute | solution.py:36
  46.8 25.5 %collective-permute-start.5 = (bf16[16,48,512]{2,1,0:T(8,128)(2,1)S(1)}, bf16[16,48,512]{2,1,0:T(8,128)(2,1)S(1)}, u32[]{:S(2)}, u32[]{:S(2)}) collective-permute-start(bf16[16,48,512]{2,1,0:T(8,128)(2,1)S(1)} %fusion.cot_here), channel_id=1, source_target_pairs={{2,0},{4,2},{6,4},{8,6},{10,8},{12,10},{14,12},{16,14},{18,16},{20... | collective-permute-start | bytes 2359304 | tf_op jit(solution)/shard_map/ppermute | solution.py:36
  55.4 0.7 copy-start
  56.3 0.9 copy-start.2
  57.2 0.8 copy-start.4
  58.0 14.3 %copy-start.1 = (bf16[368,144]{1,0:T(8,128)(2,1)S(1)}, bf16[368,144]{1,0:T(8,128)(2,1)}, u32[]{:S(2)}) copy-start(bf16[368,144]{1,0:T(8,128)(2,1)} %copy-done) | copy-start | bytes 317956
  58.0 14.3 %copy-start.6 = (f32[8,128]{1,0:T(8,128)S(1)}, f32[8,128]{1,0:T(8,128)}, u32[]{:S(2)}) copy-start(f32[8,128]{1,0:T(8,128)} %copy-done.5) | copy-start | bytes 12292
  72.3 14.9 %copy-start.8 = (bf16[24,256]{1,0:T(8,128)(2,1)S(1)}, bf16[24,256]{1,0:T(8,128)(2,1)}, u32[]{:S(2)}) copy-start(bf16[24,256]{1,0:T(8,128)(2,1)} %get-tuple-element.56) | copy-start | bytes 36868
  80.9 18.3 %all-to-all-start.1 = ((f32[32,2,8,128]{3,2,1,0:T(8,128)}), f32[32,2,8,128]{3,2,1,0:T(8,128)S(1)}, u32[]{:S(2)}, u32[]{:S(2)}) async-start(f32[32,2,8,128]{3,2,1,0:T(8,128)} %bitcast.57), calls=%async_computation.1 | async-start | bytes 524288 | tf_op jit(solution)/shard_map/all_to_all | solution.py:510
  99.2 10.1 %collective-permute-start.6 = (f32[2,8,128]{2,1,0:T(8,128)S(1)}, f32[2,8,128]{2,1,0:T(8,128)S(1)}, u32[]{:S(2)}, u32[]{:S(2)}) collective-permute-start(f32[2,8,128]{2,1,0:T(8,128)S(1)} %get-tuple-element.59), channel_id=1, source_target_pairs={{0,32},{2,34},{4,36},{6,38},{8,40},{10,42},{12,44},{14,46},{16,48}... | collective-permute-start | bytes 24584 | tf_op jit(solution)/shard_map/ppermute | solution.py:36
  103.7 10.4 %collective-permute-start.7 = (f32[2,8,128]{2,1,0:T(8,128)S(1)}, f32[2,8,128]{2,1,0:T(8,128)S(1)}, u32[]{:S(2)}, u32[]{:S(2)}) collective-permute-start(f32[2,8,128]{2,1,0:T(8,128)S(1)} %get-tuple-element.58), channel_id=1, source_target_pairs={{0,64},{2,66},{4,68},{6,70},{8,72},{10,74},{12,76},{14,78},{16,80}... | collective-permute-start | bytes 24584 | tf_op jit(solution)/shard_map/ppermute | solution.py:36

commit v5 on v4

--- a/solution.py
+++ b/solution.py
@@ -12,22 +12,13 @@
 HALO = 2 * DMAX
 LANES = 128
 SPARE = 32
-SHIFTS = (-2, -1, 0, 1, 2)
-GROUP = 8
-SEEDS = 4
+GROUP = 16
+GRANT = 60
+SEEDS = 8
 
 two_pi = 6.283185307179586
 inv_sqrt2 = 0.7071067811865476
 inv_sqrt_2pi = 0.3989422804014327
-
-
-def encode(row_ids, start_bin, feature_count):
-    octave = jnp.arange(NF, dtype=jnp.int32)
-    period = jnp.power(jnp.int32(2), octave + 2).astype(jnp.int32)
-    residue = jnp.remainder(start_bin + row_ids[:, None], period[None, :])
-    angles = residue.astype(jnp.float32) * (two_pi / period.astype(jnp.float32))[None, :]
-    encoding = jnp.concatenate((jnp.sin(angles), jnp.cos(angles)), axis=1)
-    return jnp.pad(encoding, ((0, 0), (0, feature_count - 2 * NF)))
 
 
 def from_ahead(block, distance):
@@ -42,22 +33,6 @@
 
 def from_partner(block):
     return lax.ppermute(block, "chan", [(0, 1), (1, 0)])
-
-
-def stacked_taps(kernel, sign, out_count):
-    chan_count = kernel.shape[1]
-    rows = []
-    for m in SHIFTS:
-        blocks = []
-        for a in (-1, 0, 1):
-            b = a + m
-            if -1 <= b <= 1:
-                tap = kernel[3 * (sign * a + 1) + sign * b + 1]
-                blocks.append((tap if sign > 0 else tap.T)[:out_count])
-            else:
-                blocks.append(jnp.zeros((out_count, chan_count), kernel.dtype))
-        rows.append(jnp.concatenate(blocks, axis=1))
-    return jnp.concatenate(rows, axis=0)
 
 
 def lane_ids():
@@ -123,6 +98,17 @@
     return cdf + values * (inv_sqrt_2pi * jnp.exp(-0.5 * values * values))
 
 
+def position(rows, members):
+    place = lax.axis_index("chrom")
+    return place * rows, lax.rem(place, members), lax.axis_index("chan")
+
+
+def column(row):
+    count = row.shape[1]
+    same = [lax.broadcasted_iota(jnp.int32, (count, count), k) for k in range(2)]
+    return jnp.sum(jnp.where(same[0] == same[1], row, 0.0), axis=1, keepdims=True)
+
+
 def fetch(sems, *pairs):
     copies = [pltpu.make_async_copy(a, b, sems.at[k]) for k, (a, b) in enumerate(pairs)]
     for copy in copies:
@@ -142,25 +128,65 @@
             target[row + 8 * j : row + 8 * (j + 1), k * SPARE : k * SPARE + LANES] = block
 
 
-def chunk_kernel(scalars, tile, ahead_1, ahead_2, edge, conv_bias, bias, weights, chunks, last_slab):
-    member = scalars[4]
+def tile_kernel(start, embedding_at, near_at, far_at, tile, embedding, near, far, weights, sems):
+    fetch(sems, (embedding_at, embedding), (near_at, near), (far_at, far))
+    rows = embedding.shape[0]
+    own = near.shape[0]
+    weights[...] = jnp.zeros_like(weights)
+    for k, part in enumerate((near, near, far, far)):
+        weights[k * own : (k + 1) * own] = part[...].astype(jnp.float32)
+    lanes = lane_ids()
+    first_row = lax.axis_index("chrom") * rows
+    row_ids = start[0] + first_row + lax.broadcasted_iota(jnp.int32, (rows, LANES), 0)
+    octave = lax.broadcasted_iota(jnp.int32, (rows, LANES), 1) % NF
+    period = lax.shift_left(jnp.ones_like(octave), octave + 2)
+    residue = row_ids & (period - 1)
+    angles = residue.astype(jnp.float32) * (two_pi / period.astype(jnp.float32))
+    code = jnp.where(lanes < NF, jnp.sin(angles), jnp.where(lanes < 2 * NF, jnp.cos(angles), 0.0))
+    wide = embedding[...].astype(jnp.float32)
+    features = jnp.concatenate((wide[:, :LANES] + code, wide[:, LANES:]), axis=1).astype(jnp.bfloat16)
+    terms = lax.dot_general(
+        features,
+        weights[...].astype(jnp.bfloat16),
+        (((1,), (1,)), ((), ())),
+        preferred_element_type=jnp.float32,
+    )
+    odd = lanes // own % 2 == 1
+    tile[...] = jnp.where(odd, terms[rows // 2 :], terms[: rows // 2])
+
+
+def chunk_kernel(
+    tile_at, ahead_1_at, ahead_2_at, edge_at, conv_bias_at, bias_at, near_at, far_at,
+    chunks, last_slab, tile, ahead_1, ahead_2, edge, conv_bias, bias, near_weight, far_weight, sems,
+):
+    fetch(
+        sems, (tile_at, tile), (ahead_1_at, ahead_1), (ahead_2_at, ahead_2), (edge_at, edge),
+        (conv_bias_at, conv_bias), (bias_at, bias), (near_at, near_weight), (far_at, far_weight),
+    )
     lanes = lane_ids()
     members = chunks.shape[0]
-    own = bias.shape[0]
+    own, width = bias.shape
     wide = 2 * own
-    slabs = own // 8
-
-    def slabs_of(ref):
-        turn = lax.rem(ref.shape[1] - member * SPARE, ref.shape[1])
-        piece = pltpu.roll(ref[...], turn, 1)[:, :LANES]
-        return [piece[8 * j : 8 * (j + 1)] for j in range(slabs)]
-
-    weight = [pltpu.roll(slab, 3 * SPARE, 1) for slab in slabs_of(weights)]
+    rows = 2 * tile.shape[0]
+    _, member, chan = position(rows, members)
+    features = near_weight.shape[1]
+    turn = lax.rem(2 * features - (1 - chan) * (features // 2) - member * rows, features)
+    near_piece, far_piece = (
+        pltpu.roll(w[...].astype(jnp.float32), turn, 1)[:, :LANES] for w in (near_weight, far_weight)
+    )
+    weight = []
+    for j in range(3):
+        part = slice(8 * j, 8 * (j + 1))
+        both = jnp.where(lanes < rows, near_piece[part], pltpu.roll(far_piece[part], rows, 1))
+        weight.append(pltpu.roll(both, 3 * SPARE, 1))
     last_slab[...] = jnp.where(lanes >= 3 * SPARE, weight[2], 0.0)
+    piece = pltpu.roll(bias[...], lax.rem(width - member * SPARE, width), 1)[:, :LANES]
+    conv_column = column(conv_bias[0:1])
     third = jnp.zeros((8, LANES), jnp.float32)
-    for j, slab in enumerate(slabs_of(bias)):
-        third = jnp.where(lanes // SPARE == j, pltpu.roll(slab, j * SPARE, 1), third)
-        third = jnp.where(lanes == slabs * SPARE + j, conv_bias[8 * j : 8 * (j + 1), 0:1], third)
+    for j in range(own // 8):
+        part = slice(8 * j, 8 * (j + 1))
+        third = jnp.where(lanes // SPARE == j, pltpu.roll(piece[part], j * SPARE, 1), third)
+        third = jnp.where(lanes == own // 8 * SPARE + j, conv_column[part], third)
     held = [edge[...], tile[...], ahead_1[...], ahead_2[...], edge[...]]
     first = [pltpu.roll(block, LANES - wide, 1) for block in held]
     near = [pltpu.roll(block, wide, 1) for block in held[:3]]
@@ -182,53 +208,106 @@
             chunks[to, c, 2] = third
 
 
-def last_kernel(scalars, part, ahead_1, ahead_2, terms, recv, weights, out, wide_weights, other):
-    chan = scalars[5]
+def last_kernel(
+    part_at, ahead_1_at, ahead_2_at, terms_at, recv_at, near_at, far_at,
+    out, part, ahead_1, ahead_2, terms, recv, near_here, far_here, blocks, weights, sems,
+):
+    fetch(
+        sems, (part_at, part), (ahead_1_at, ahead_1), (ahead_2_at, ahead_2), (terms_at, terms),
+        (recv_at, recv), (near_at, near_here), (far_at, far_here),
+    )
     lanes = lane_ids()
-    own = weights.shape[0]
+    own, features = near_here.shape
+    half = features // 2
     wide = 2 * own
-    half = weights.shape[1] // 2
     members = terms.shape[0]
-    slabs = [[(terms[k, 1 - chan, j], 3) for k in range(members)] for j in range(2)]
-    slabs.append([(recv[k, 1 - chan, 0], 3) for k in range(members)])
-    lay_slabs(other, 0, slabs)
-    total = jnp.zeros((part.shape[2], 2 * half), jnp.float32)
-    wide_weights[...] = jnp.zeros_like(wide_weights)
-    for source, c in ((weights, chan), (other, 1 - chan)):
-        for k, block in enumerate((source[:, half:], source[:, :half])):
-            wide_weights[2 * k * own : (2 * k + 1) * own, :half] = block
-            wide_weights[(2 * k + 1) * own : (2 * k + 2) * own, half:] = block
+    rows = out.shape[0]
+    _, _, chan = position(rows, members)
+    for k, here in enumerate((far_here, near_here)):
+        values = here[...].astype(jnp.float32)
+        blocks[0, k * own : (k + 1) * own] = jnp.where(chan == 0, values[:, :half], values[:, half:])
+    per_tile = LANES // rows
+    for j in range(own // 8):
+        for at in range(0, members, per_tile):
+            far = near = jnp.zeros((8, LANES), jnp.float32)
+            for t in range(min(per_tile, members - at)):
+                tile = recv[at + t, 1 - chan].astype(jnp.float32)[: rows // 2] if j == 2 else terms[at + t, 1 - chan, j]
+                mine = lanes // rows == t
+                near = jnp.where(mine, pltpu.roll(tile, (SPARE + t * rows) % LANES, 1), near)
+                far = jnp.where(mine, pltpu.roll(tile, (SPARE - rows + t * rows) % LANES, 1), far)
+            span = slice(at * rows, min(at * rows + LANES, half))
+            blocks[1, 8 * j : 8 * (j + 1), span] = far[:, : span.stop - span.start]
+            blocks[1, own + 8 * j : own + 8 * (j + 1), span] = near[:, : span.stop - span.start]
+    total = jnp.zeros((rows // 2, 2 * half), jnp.float32)
+    weights[...] = jnp.zeros_like(weights)
+    for k, c in enumerate((chan, 1 - chan)):
+        for n in range(2):
+            block = blocks[k, n * own : (n + 1) * own]
+            weights[2 * n * own : (2 * n + 1) * own, :half] = block
+            weights[(2 * n + 1) * own : (2 * n + 2) * own, half:] = block
         far = part[c, 0] + pltpu.roll(ahead_1[c], LANES - wide, 1) + ahead_2[c]
         sums = jnp.where(lanes < wide, far, jnp.where(lanes < 2 * wide, part[c, 1], 0.0))
         total += jnp.dot(
             sums.astype(jnp.bfloat16),
-            wide_weights[...].astype(jnp.bfloat16),
+            weights[...].astype(jnp.bfloat16),
             preferred_element_type=jnp.float32,
         )
     out[...] = jnp.concatenate((total[:, :half], total[:, half:]), axis=0).astype(out.dtype)
 
 
+def taps_kernel(conv_weight_at, ahead, back, conv_weight, ahead_wide, back_wide, sems):
+    fetch(sems, (conv_weight_at, conv_weight))
+    chans = conv_weight.shape[2]
+    own = chans // 2
+    chan = lax.axis_index("chan")
+    ids = [lax.broadcasted_iota(jnp.int32, (chans, chans), k) for k in range(2)]
+    turn = (lax.rem(ids[0] + chan * own, chans) == ids[1]).astype(jnp.bfloat16)
+
+    def product(left, right, right_axis):
+        dims = (((1,), (right_axis,)), ((), ()))
+        return lax.dot_general(left, right, dims, preferred_element_type=jnp.float32)
+
+    for wide in (ahead_wide, back_wide):
+        wide[...] = jnp.zeros_like(wide)
+    for layer in range(2):
+        for tap in range(9):
+            step, side = tap // 3 - 1, tap % 3 - 1
+            for wide, sign in ((ahead_wide, 1), (back_wide, -1)):
+                turned = product(turn, conv_weight[layer, tap], 0 if sign > 0 else 1)
+                turned = product(turned.astype(jnp.bfloat16), turn, 1)
+                a, m = sign * step, sign * (side - step)
+                last = (layer == 1) == (sign > 0)
+                count = own if last else chans
+                row = (5 * chans if last else 0) + (m + 2) * count
+                wide[row : row + count, (a + 1) * chans : (a + 2) * chans] = turned[:count]
+    ahead[...] = ahead_wide[...].astype(jnp.bfloat16)
+    back[...] = back_wide[...].astype(jnp.bfloat16)
+
+
 def forward_kernel(
-    total_rows, scalars, conv_bias, terms_at, bias_at, taps_at,
+    total_rows, steps, band, terms_at, conv_bias_at, bias_at, taps_at,
     pair_out, slope_0, slope_1, pair_0, act_0, act_1, pair_1, far_rows, near_rows, far, near, bias,
-    terms, taps, sems,
+    conv_bias, terms, taps, sems,
 ):
-    band_width, first_row, step_0, step_1, member, chan = (scalars[k] for k in range(6))
+    band_width, step_0, step_1 = band[0], steps[0], steps[1]
     lanes = lane_ids()
     rows, own, width = pair_out.shape
+    first_row, member, chan = position(rows, terms.shape[0])
     chans = 2 * own
     count = width // LANES
     members = terms.shape[0]
     taps_0, taps_1 = taps.at[: 5 * chans], taps.at[5 * chans :]
-    fetch(sems, (terms_at, terms), (bias_at, bias.at[:own]), (taps_at, taps))
+    fetch(
+        sems, (conv_bias_at, conv_bias), (terms_at, terms), (bias_at, bias.at[:own]), (taps_at, taps)
+    )
     slabs = own // 8
 
     lay_slabs(bias, own, [[(terms[k, 1 - chan, 2], j) for k in range(members)] for j in range(slabs)])
     last = terms[0, 1 - chan, 2]
     bias_0 = jnp.concatenate(
-        [conv_bias[:, 0:1]] + [last[:, k : k + 1] for k in range(slabs * SPARE, slabs * SPARE + slabs)], axis=0
-    )
-    bias_1 = conv_bias[:, 1:2]
+        [column(conv_bias[0:1])] + [last[:, k : k + 1] for k in range(slabs * SPARE, slabs * SPARE + slabs)], axis=0
+    )
+    bias_1 = column(conv_bias[1:2])
 
     far_rows[...] = jnp.zeros_like(far_rows)
     near_rows[...] = jnp.zeros_like(near_rows)
@@ -318,12 +397,13 @@
 
 
 def backward_kernel(
-    total_rows, scalars, slope_0, slope_1, last_slab, cot_behind, cot_here, cot_ahead, taps_at,
-    far_terms, grad_2, grad_1, low_1, near_sum, far_sum, far_rows, taps, sems,
+    total_rows, steps, band, slope_0, slope_1, cot_behind, cot_here, cot_ahead, last_slab_at, taps_at,
+    far_terms, grad_2, grad_1, low_1, near_sum, far_sum, far_rows, taps, last_slab, sems,
 ):
-    band_width, first_row, step_0, step_1, member = (scalars[k] for k in range(5))
+    band_width, step_0, step_1 = band[0], steps[0], steps[1]
     lanes = lane_ids()
     rows, chans, width = cot_here.shape
+    first_row, member, _ = position(rows, far_terms.shape[0])
     own = chans // 2
     count = width // LANES
     members = far_terms.shape[0]
@@ -339,6 +419,7 @@
         (cot_here, grad_2.at[rows : 2 * rows]),
         (cot_ahead, grad_2.at[2 * rows :]),
         (taps_at, taps),
+        (last_slab_at, last_slab),
     )
 
     def layer_1(block, _):
@@ -396,54 +477,85 @@
         pieces = halves(2 * members + r)
         own_place = jnp.where(member == r, near_terms, 0.0)
         two = pieces[0] + pltpu.roll(pieces[1], own, 1) + own_place
+        both = jnp.concatenate((one, two), axis=0).astype(far_terms.dtype)
         for c in range(2):
-            far_terms[r, c, 0] = one
-            far_terms[r, c, 1] = two
-
-
-def call(kernel, out_shapes, scratch, flops, smem, near_arrays, far_arrays=()):
-    arrays = tuple(near_arrays) + tuple(far_arrays)
+            far_terms[r, c] = both
+
+
+def call(
+    kernel, out_shapes, scratch, flops, scalars, near_arrays, far_arrays=(), stored_arrays=(), grant=32
+):
+    arrays = tuple(near_arrays) + tuple(far_arrays) + tuple(stored_arrays)
     bytes_accessed = sum(a.size * a.dtype.itemsize for a in arrays)
     bytes_accessed += sum(s.size * s.dtype.itemsize for s in out_shapes)
     vmem = pl.BlockSpec(memory_space=pltpu.VMEM)
     return pl.pallas_call(
         kernel,
         out_shape=out_shapes,
-        in_specs=[pl.BlockSpec(memory_space=pltpu.SMEM)]
+        in_specs=[pl.BlockSpec(memory_space=pltpu.SMEM)] * len(scalars)
         + [vmem] * len(near_arrays)
-        + [pl.BlockSpec(memory_space=pl.ANY)] * len(far_arrays),
+        + [pl.BlockSpec(memory_space=pl.ANY)] * len(far_arrays)
+        + [pl.BlockSpec(memory_space=pltpu.HBM)] * len(stored_arrays),
         out_specs=[vmem] * len(out_shapes),
         scratch_shapes=scratch,
-        compiler_params=pltpu.CompilerParams(vmem_limit_bytes=32 * 2**20),
+        compiler_params=pltpu.CompilerParams(vmem_limit_bytes=grant * 2**20),
         cost_estimate=pl.CostEstimate(
             flops=flops, bytes_accessed=bytes_accessed, transcendentals=0
         ),
-    )(smem, *arrays)
+    )(*scalars, *arrays)
 
 
 f32 = functools.partial(jax.ShapeDtypeStruct, dtype=jnp.float32)
 
 
-def chunk_call(members, scalars, tile, ahead_1, ahead_2, edge, conv_bias, bias, weights):
+def fetching_call(kernel, out_shapes, scratch, scalars, far_arrays, stored_arrays, grant=32):
+    arrays = tuple(far_arrays) + tuple(stored_arrays)
+    held = [pltpu.VMEM(a.shape, a.dtype) for a in arrays]
+    sems = pltpu.SemaphoreType.DMA((len(arrays),))
     return call(
-        chunk_kernel,
-        (f32((members, 2, 3) + tile.shape), f32(tile.shape)),
-        [],
-        0,
-        scalars,
-        (tile, ahead_1, ahead_2, edge, conv_bias, bias, weights),
-    )
-
-
-def last_call(scalars, part, ahead_1, ahead_2, terms, recv, weights):
-    own, width = weights.shape
-    (out,) = call(
+        kernel, out_shapes, held + scratch + [sems], 0, scalars, (), far_arrays, stored_arrays, grant
+    )
+
+
+def tile_call(scalars, embedding, near_weight, far_weight):
+    shape = (embedding.shape[0] // 2, LANES)
+    weights = pltpu.VMEM((LANES, embedding.shape[1]), jnp.float32)
+    (tile,) = fetching_call(
+        tile_kernel, (f32(shape),), [weights], scalars, (), (embedding, near_weight, far_weight), GRANT
+    )
+    return tile
+
+
+def taps_call(conv_weight):
+    chans = conv_weight.shape[2]
+    shape = (-(-(5 * chans + 5 * chans // 2) // 16) * 16, 3 * chans)
+    return fetching_call(
+        taps_kernel,
+        (jax.ShapeDtypeStruct(shape, jnp.bfloat16),) * 2,
+        [pltpu.VMEM(shape, jnp.float32)] * 2,
+        (),
+        (),
+        (conv_weight,),
+    )
+
+
+def chunk_call(members, tiles, *arrays):
+    shape = tiles[0].shape
+    return fetching_call(chunk_kernel, (f32((members, 2, 3) + shape), f32(shape)), [], (), tiles, arrays, GRANT)
+
+
+def last_call(part, ahead_1, ahead_2, terms, recv, near_weight, far_weight):
+    own, features = near_weight.shape
+    (out,) = fetching_call(
         last_kernel,
-        (jax.ShapeDtypeStruct((2 * part.shape[2], width // 2), jnp.bfloat16),),
-        [pltpu.VMEM((LANES, width), jnp.float32), pltpu.VMEM((own, width), jnp.float32)],
-        0,
-        scalars,
-        (part, ahead_1, ahead_2, terms, recv, weights),
+        (jax.ShapeDtypeStruct((2 * part.shape[2], features // 2), jnp.bfloat16),),
+        [
+            pltpu.VMEM((2, 2 * own, features // 2), jnp.float32),
+            pltpu.VMEM((LANES, features), jnp.float32),
+        ],
+        (),
+        (part, ahead_1, ahead_2, terms, recv),
+        (near_weight, far_weight),
     )
     return out
 
@@ -464,14 +576,16 @@
             pltpu.VMEM((chans, width + LANES), jnp.float32),
             pltpu.VMEM((chans, LANES), jnp.float32),
             pltpu.VMEM((chans, width), jnp.float32),
+            pltpu.VMEM(conv_bias.shape, conv_bias.dtype),
             pltpu.VMEM(terms.shape, terms.dtype),
             pltpu.VMEM(taps.shape, taps.dtype),
-            pltpu.SemaphoreType.DMA((3,)),
+            pltpu.SemaphoreType.DMA((4,)),
         ],
         2 * 15 * chans * chans * width * 40,
         scalars,
-        (conv_bias,),
-        (terms, bias_here, taps),
+        (),
+        (terms,),
+        (conv_bias, bias_here, taps),
     )
 
 
@@ -481,7 +595,7 @@
     slots = members + (width + LANES) // rows
     (terms,) = call(
         functools.partial(backward_kernel, total_rows),
-        (f32((members, 2, 2, rows // 2, LANES)),),
+        (jax.ShapeDtypeStruct((members, 2, rows, LANES), jnp.bfloat16),),
         [
             pltpu.VMEM((rows + 2 * HALO, chans, width), jnp.bfloat16),
             pltpu.VMEM((rows + HALO, own, width), jnp.float32),
@@ -490,12 +604,14 @@
             pltpu.VMEM((LANES, width + LANES), jnp.float32),
             pltpu.VMEM((slots * rows, LANES), jnp.float32),
             pltpu.VMEM(taps.shape, taps.dtype),
-            pltpu.SemaphoreType.DMA((4,)),
+            pltpu.VMEM(last_slab.shape, last_slab.dtype),
+            pltpu.SemaphoreType.DMA((5,)),
         ],
         2 * 15 * chans * chans * width * 40,
         scalars,
-        (slope_0, slope_1, last_slab),
-        (cot_behind, cot, cot_ahead, taps),
+        (slope_0, slope_1),
+        (cot_behind, cot, cot_ahead, last_slab),
+        (taps,),
     )
     return terms
 
@@ -516,13 +632,6 @@
     route = [(i + 3 * members, i) for i in range(0, count - 3 * members, members)]
     route += [(i - members, i) for i in range(2 * members - 1, count, members)]
     return lax.ppermute(block, "chrom", route)
-
-
-def projection_tile(features, near_weight, far_weight):
-    half = features.shape[0] // 2
-    parts = [jnp.dot(features, w, preferred_element_type=jnp.float32) for w in (near_weight, far_weight)]
-    tile = jnp.concatenate([p[h * half : (h + 1) * half] for p in parts for h in range(2)], axis=1)
-    return jnp.pad(tile, ((0, 0), (0, LANES - tile.shape[1])))
 
 
 def shards(
@@ -540,24 +649,14 @@
     members = width // rows // 2
     member = place % members
     row_ids = first_row + jnp.arange(rows, dtype=jnp.int32)
-    scalars = jnp.stack([band_width[0], first_row, dilations[0], dilations[1], member, chan]).astype(jnp.int32)
-
-    features = (
-        embedding.astype(jnp.float32) + encode(row_ids, window_start[0], embedding.shape[1])
-    ).astype(jnp.bfloat16)
-    tile = projection_tile(features, near_weight, far_weight)
+    scalars = (dilations, band_width)
+
+    near_weight, far_weight = near_weight.T, far_weight.T
+    tile = tile_call((window_start,), embedding, near_weight, far_weight)
     ahead = from_ahead(tile, members), from_ahead(tile, 2 * members), from_edges(tile, members)
 
-    def weight_rows(half):
-        parts = [
-            lax.dynamic_slice_in_dim(w, half * features_half, features_half, 0).T
-            for w in (near_weight, far_weight)
-        ]
-        return jnp.concatenate(parts, axis=1).astype(jnp.float32)
-
-    conv_columns = conv_bias.T
     chunks, last_slab = chunk_call(
-        members, scalars, tile, *ahead, conv_columns, distance_bias, weight_rows(1 - chan)
+        members, (tile,) + ahead, conv_bias, distance_bias, near_weight, far_weight
     )
     terms = exchange_in_group(chunks)
 
@@ -569,30 +668,19 @@
     cot_behind = from_ahead(cot, -1)
     cot_ahead = from_ahead(cot, 1)
 
-    conv_weight = after(conv_weight, chunks)
-    twice = jnp.concatenate((conv_weight, conv_weight), axis=2)
-    twice = jnp.concatenate((twice, twice), axis=3)
-    turned = lax.dynamic_slice(twice, (0, 0, chan * own, chan * own), conv_weight.shape)
-    last = jnp.zeros((-5 * own % 16, 3 * chans), conv_weight.dtype)
-    taps_ahead = jnp.concatenate(
-        (stacked_taps(turned[0], 1, chans), stacked_taps(turned[1], 1, own), last), axis=0
-    )
-    taps_back = jnp.concatenate(
-        (stacked_taps(turned[1], -1, chans), stacked_taps(turned[0], -1, own), last), axis=0
-    )
-
+    taps_ahead, taps_back = taps_call(after(conv_weight, chunks))
     pair_rows, slope_0, slope_1 = forward_call(
-        total_rows, rows, scalars, terms, distance_bias, conv_columns, taps_ahead
+        total_rows, rows, scalars, terms, distance_bias, conv_bias, taps_ahead
     )
     pair_out = jnp.swapaxes(pair_rows.astype(jnp.bfloat16), 0, 1)
     terms_back = backward_call(
         total_rows, members, scalars, cot_behind, cot, cot_ahead, slope_0, slope_1, last_slab, taps_back
     )
     recv = exchange_in_group(terms_back)
-    part = jnp.sum(recv, axis=0)
+    part = jnp.sum(recv.astype(jnp.float32), axis=0).reshape(2, 2, rows // 2, LANES)
     ahead_1 = from_ahead(part[:, 0], -members)
     ahead_2 = from_ahead(part[:, 1], -2 * members)
-    grads = last_call(scalars, part, ahead_1, ahead_2, terms, recv, weight_rows(chan))
+    grads = last_call(part, ahead_1, ahead_2, terms, recv, near_weight, far_weight)
     return (pair_out, grads)
 
 

time: 116 us -> 111 us (0.957)
  blocking collectives: 0 us -> 17.1 us
  waiting for transfers between devices: 17.4 us -> 7.68 us
  local copies, waits for them, and re-layouts: 11.2 us -> 3.29 us
  other arithmetic: 2.78 us -> 0.34 us
  matrix products: 1.86 us -> 0 us
  Pallas kernels: 24.5 us -> 25.7 us
  starting transfers between devices: 55.3 us -> 54.1 us
    all_to_all x0 -> x1, blocking collectives: none -> 17.1 us  [exchange_in_group(): lax.all_to_all(flat, ('chrom', 'chan'), 0, 0, axis_index_groups=lists)]
    all_to_all x2 -> x1, waiting for transfers between devices: 11.4 us -> 1.23 us  [exchange_in_group(): lax.all_to_all(flat, ('chrom', 'chan'), 0, 0, axis_index_groups=lists)]
    all_to_all x2 -> x1, starting transfers between devices: 10.2 us -> 3.89 us  [exchange_in_group(): lax.all_to_all(flat, ('chrom', 'chan'), 0, 0, axis_index_groups=lists)]
    ppermute x6, starting transfers between devices: 32.7 us -> 37.7 us  [from_ahead(): return lax.ppermute(block, 'chrom', route)]
    unnamed x29 -> x22, local copies, waits for them, and re-layouts: 7.19 us -> 3.29 us
    dot_general x2 -> x0, matrix products: 1.86 us -> none  [projection_tile(): jnp.dot(features, w, preferred_element_type=jnp.float32)]
    transpose x3 -> x0, local copies, waits for them, and re-layouts: 1.4 us -> none  [the longest x1 1.37 us: weight_rows(): lax.dynamic_slice_in_dim(w, half * features_half, features_half, 0)]
    concatenate x9 -> x0, local copies, waits for them, and re-layouts: 1.29 us -> none  [the longest x2 1.02 us: shards(): jnp.concatenate((stacked_taps(turned[0], 1, chans), stacked_taps(turned[1...]
  transfers between devices with their start and end apart: 10 -> 9, of which waited for: 4 -> 4; matrix products, arithmetic and copies ran while one was open for 8% -> 2% of each run, Pallas kernels for 13% -> 14%
where the time goes in v5:
time: 111 us; the launch traced here: 110 us
  starting transfers between devices  54.1 us (49%)
  Pallas kernels  25.7 us (23%)
  blocking collectives  17.1 us (15%)
  waiting for transfers between devices  7.68 us (7%)
  local copies, waits for them, and re-layouts  3.29 us (3%)
  between operations  2.19 us (2%)
    ppermute x6, starting transfers between devices, from_ahead(): return lax.ppermute(block, 'chrom', route)  37.7 us
    pallas_call x6, Pallas kernels, call(): pl.pallas_call(kernel, out_shape=out_shapes, in_specs=[pl.BlockSpec(memor...  25.7 us
    all_to_all x1, blocking collectives, exchange_in_group(): lax.all_to_all(flat, ('chrom', 'chan'), 0, 0, axis_index_groups=lists)  17.1 us
    ppermute x1, starting transfers between devices, from_partner(): return lax.ppermute(block, 'chan', [(0, 1), (1, 0)])  7.73 us
    ppermute x6, waiting for transfers between devices, from_ahead(): return lax.ppermute(block, 'chrom', route)  5.85 us
    ppermute x1, starting transfers between devices, from_edges(): return lax.ppermute(block, 'chrom', route)  4.77 us
    all_to_all x1, starting transfers between devices, exchange_in_group(): lax.all_to_all(flat, ('chrom', 'chan'), 0, 0, axis_index_groups=lists)  3.89 us
    unnamed x22, local copies, waits for them, and re-layouts  3.29 us
  transfers between devices with their start and end apart: 9, of which 4 were waited for; matrix products, arithmetic and copies ran while one was open for 2% of the time, Pallas kernels for 14%

profile of v5, /device:TPU:6, one launch (start us, length us, event | category | flops | bytes accessed | tf_op | source)
XLA Modules:
  0.0 110.4 jit_solution(4452352489760535230)
XLA Ops:
  1.3 1.6 %shard_map.113.tile_at = f32[8,128]{1,0:T(8,128)} custom-call(s32[1]{0:T(128)S(6)} %copy.23.start, bf16[16,512]{1,0:T(8,128)(2,1)} %embedding_at.1, bf16[24,512]{1,0:T(8,128)(2,1)} %bitcast.26, bf16[24,512]{1,0:T(8,128)(2,1)} %bitcast.29), custom_call_target="tpu_custom_call" | custom-call | bytes 69632 | tf_op jit(solution)/shard_map/pallas_call | solution.py:492
  2.9 11.3 %collective-permute-start = (f32[8,128]{1,0:T(8,128)}, f32[8,128]{1,0:T(8,128)S(1)}, u32[]{:S(2)}, u32[]{:S(2)}) collective-permute-start(f32[8,128]{1,0:T(8,128)} %shard_map.113.tile_at), channel_id=1, source_target_pairs={{32,0},{34,2},{36,4},{38,6},{40,8},{42,10},{44,12},{46,14},{48,16}... | collective-permute-start | bytes 12296 | tf_op jit(solution)/shard_map/ppermute | solution.py:27
  14.2 1.9 %collective-permute-start.1 = (f32[8,128]{1,0:T(8,128)}, f32[8,128]{1,0:T(8,128)S(1)}, u32[]{:S(2)}, u32[]{:S(2)}) collective-permute-start(f32[8,128]{1,0:T(8,128)} %shard_map.113.tile_at), channel_id=1, source_target_pairs={{64,0},{66,2},{68,4},{70,6},{72,8},{74,10},{76,12},{78,14},{80,16}... | collective-permute-start | bytes 12296 | tf_op jit(solution)/shard_map/ppermute | solution.py:27
  16.2 4.8 %collective-permute-start.2 = (f32[8,128]{1,0:T(8,128)}, f32[8,128]{1,0:T(8,128)S(1)}, u32[]{:S(2)}, u32[]{:S(2)}) collective-permute-start(f32[8,128]{1,0:T(8,128)} %shard_map.113.tile_at), channel_id=1, source_target_pairs={{96,0},{128,32},{160,64},{192,96},{224,128},{256,160},{288,192},{3... | collective-permute-start | bytes 12296 | tf_op jit(solution)/shard_map/ppermute | solution.py:634
  21.0 1.2 %copy.17 = bf16[24,16,512]{2,0,1:T(8,128)(2,1)S(1)} copy(bf16[24,16,512]{2,1,0:T(8,128)(2,1)} %param.19) | data formatting | bytes 786432 | tf_op args[9]
  22.2 7.7 %collective-permute-start.3 = (bf16[24,16,512]{2,0,1:T(8,128)(2,1)S(1)}, bf16[24,16,512]{2,0,1:T(8,128)(2,1)S(1)}, u32[]{:S(2)}, u32[]{:S(2)}) collective-permute-start(bf16[24,16,512]{2,0,1:T(8,128)(2,1)S(1)} %copy.17), channel_id=1, source_target_pairs={{0,1},{1,0},{2,3},{3,2},{4,5},{5,4},{6,7},{7,6},{8,9},{9,8},{10,11... | collective-permute-start | bytes 1179656 | tf_op jit(solution)/shard_map/ppermute | solution.py:35
  30.7 0.5 copy-done.7
  31.3 0.6 copy-done.9
  31.9 1.9 %shard_map.114 = (f32[16,2,3,8,128]{4,3,2,1,0:T(8,128)}, f32[8,128]{1,0:T(8,128)}) custom-call(f32[8,128]{1,0:T(8,128)} %shard_map.113.tile_at, f32[8,128]{1,0:T(8,128)} %copy-done.7, f32[8,128]{1,0:T(8,128)} %copy-done.8, f32[8,128]{1,0:T(8,128)} %copy-done.9, f32[2,24]{1,0:T(2,128)} %conv_bias_at.3, f32[24,512]{1,0:T(8,128)} %bias_at.3, ...), custom_call_target="tpu_custom_call" | custom-call | bytes 512192 | tf_op jit(solution)/shard_map/pallas_call | solution.py:492
  33.8 3.9 %all-to-all-start = ((f32[32,3,8,128]{3,2,1,0:T(8,128)}), f32[32,3,8,128]{3,2,1,0:T(8,128)S(1)}, u32[]{:S(2)}, u32[]{:S(2)}) async-start(f32[32,3,8,128]{3,2,1,0:T(8,128)} %bitcast.34), calls=%async_computation | async-start | bytes 786432 | tf_op jit(solution)/shard_map/all_to_all | solution.py:626
  37.7 0.6 collective-permute-done.3
  38.5 1.9 %collective-permute-start.4 = (bf16[16,48,512]{2,1,0:T(8,128)(2,1)S(1)}, bf16[16,48,512]{2,1,0:T(8,128)(2,1)S(1)}, u32[]{:S(2)}, u32[]{:S(2)}) collective-permute-start(bf16[16,48,512]{2,1,0:T(8,128)(2,1)S(1)} %fusion.cot_here), channel_id=1, source_target_pairs={{0,2},{2,4},{4,6},{6,8},{8,10},{10,12},{12,14},{14,16},{16,18},{18... | collective-permute-start | bytes 2359304 | tf_op jit(solution)/shard_map/ppermute | solution.py:27
  40.4 12.4 %collective-permute-start.5 = (bf16[16,48,512]{2,1,0:T(8,128)(2,1)S(1)}, bf16[16,48,512]{2,1,0:T(8,128)(2,1)S(1)}, u32[]{:S(2)}, u32[]{:S(2)}) collective-permute-start(bf16[16,48,512]{2,1,0:T(8,128)(2,1)S(1)} %fusion.cot_here), channel_id=1, source_target_pairs={{2,0},{4,2},{6,4},{8,6},{10,8},{12,10},{14,12},{16,14},{18,16},{20... | collective-permute-start | bytes 2359304 | tf_op jit(solution)/shard_map/ppermute | solution.py:27
  52.8 1.1 %shard_map.115 = (bf16[368,144]{1,0:T(8,128)(2,1)S(1)}, bf16[368,144]{1,0:T(8,128)(2,1)S(1)}) custom-call(bf16[2,9,48,48]{3,2,1,0:T(8,128)(2,1)S(1)} %copy-done.2), custom_call_target="tpu_custom_call" | custom-call | bytes 294912 | tf_op jit(solution)/shard_map/pallas_call | solution.py:492
  53.9 1.2 %all-to-all-done = f32[32,3,8,128]{3,2,1,0:T(8,128)S(1)} async-done(((f32[32,3,8,128]{3,2,1,0:T(8,128)}), f32[32,3,8,128]{3,2,1,0:T(8,128)S(1)}, u32[]{:S(2)}, u32[]{:S(2)}) %all-to-all-start) | async-done | bytes 393248 | tf_op jit(solution)/shard_map/all_to_all | solution.py:626
  55.2 12.5 %shard_map.116 = (f32[16,24,512]{2,1,0:T(8,128)S(1)}, f32[16,24,512]{2,1,0:T(8,128)S(1)}, f32[32,48,512]{2,1,0:T(8,128)S(1)}) custom-call(s32[2]{0:T(128)S(1)} %copy-done.6, s32[1]{0:T(128)} %copy.24.band, f32[16,2,3,8,128]{4,3,2,1,0:T(8,128)S(1)} %bitcast.21, f32[2,24]{1,0:T(2,128)S(1)} %copy-done.5, f32[24,512]{1,0:T(8,128)S(1)} %copy-done.3, ...), custom_call_target="tpu_custom_call" | custom-call | flops 1415577600 | bytes 5267136 | tf_op jit(solution)/shard_map/pallas_call | solution.py:492
  67.7 1.9 %collective-permute-done.4.cot_behind = bf16[16,48,512]{2,1,0:T(8,128)(2,1)S(1)} collective-permute-done((bf16[16,48,512]{2,1,0:T(8,128)(2,1)S(1)}, bf16[16,48,512]{2,1,0:T(8,128)(2,1)S(1)}, u32[]{:S(2)}, u32[]{:S(2)}) %collective-permute-start.4) | collective-permute-done | bytes 786464 | tf_op jit(solution)/shard_map/ppermute | solution.py:27
  69.6 7.3 %shard_map.117 = bf16[16,2,16,128]{3,2,1,0:T(8,128)(2,1)S(1)} custom-call(s32[2]{0:T(128)S(1)} %copy-done.6, s32[1]{0:T(128)} %copy.24.band, f32[16,24,512]{2,1,0:T(8,128)S(1)} %get-tuple-element.15.slope_0, f32[32,48,512]{2,1,0:T(8,128)S(1)} %get-tuple-element.16.slope_1, bf16[16,48,512]{2,1,0:T(8,128)(2,1)S(1)} %collective-permute-done.4.cot_behind, ...), custom_call_target="tpu_custom_call" | custom-call | flops 1415577600 | bytes 6532608 | tf_op jit(solution)/shard_map/pallas_call | solution.py:492
  76.9 17.1 %all_to_all.10 = bf16[32,16,128]{2,1,0:T(8,128)(2,1)S(1)} all-to-all(bf16[32,16,128]{2,1,0:T(8,128)(2,1)S(1)} %bitcast.25), channel_id=1, replica_groups={{0,1,2,3,4,5,6,7,8,9,10,11,12,13,14,15,16,17,18,19,20,21,22,23,24,25,26..., dimensions={0} | all-to-all | bytes 262144 | tf_op jit(solution)/shard_map/all_to_all | solution.py:626
  94.0 4.6 %collective-permute-start.6 = (f32[2,8,128]{2,1,0:T(8,128)S(1)}, f32[2,8,128]{2,1,0:T(8,128)S(1)}, u32[]{:S(2)}, u32[]{:S(2)}) collective-permute-start(f32[2,8,128]{2,1,0:T(8,128)S(1)} %get-tuple-element.25), channel_id=1, source_target_pairs={{0,32},{2,34},{4,36},{6,38},{8,40},{10,42},{12,44},{14,46},{16,48}... | collective-permute-start | bytes 24584 | tf_op jit(solution)/shard_map/ppermute | solution.py:27
  98.6 5.5 %collective-permute-start.7 = (f32[2,8,128]{2,1,0:T(8,128)S(1)}, f32[2,8,128]{2,1,0:T(8,128)S(1)}, u32[]{:S(2)}, u32[]{:S(2)}) collective-permute-start(f32[2,8,128]{2,1,0:T(8,128)S(1)} %get-tuple-element.24), channel_id=1, source_target_pairs={{0,64},{2,66},{4,68},{6,70},{8,72},{10,74},{12,76},{14,78},{16,80}... | collective-permute-start | bytes 24584 | tf_op jit(solution)/shard_map/ppermute | solution.py:27
  104.2 0.9 copy.20
  105.1 3.9 %collective-permute-done.7.ahead_2_at = f32[2,8,128]{2,1,0:T(8,128)S(1)} collective-permute-done((f32[2,8,128]{2,1,0:T(8,128)S(1)}, f32[2,8,128]{2,1,0:T(8,128)S(1)}, u32[]{:S(2)}, u32[]{:S(2)}) %collective-permute-start.7) | collective-permute-done | bytes 8224 | tf_op jit(solution)/shard_map/ppermute | solution.py:27
  109.0 1.4 %shard_map.118 = bf16[16,256]{1,0:T(8,128)(2,1)} custom-call(f32[2,2,8,128]{3,2,1,0:T(8,128)S(1)} %bitcast.33, f32[2,8,128]{2,1,0:T(8,128)S(1)} %collective-permute-done.6.ahead_1_at, f32[2,8,128]{2,1,0:T(8,128)S(1)} %collective-permute-done.7.ahead_2_at, f32[16,2,3,8,128]{4,3,2,1,0:T(8,128)S(1)} %bitcast.22, bf16[16,2,16,128]{3,2,1,0:T(8,128)(2,1)S(1)} %bitcast.24, ...), custom_call_target="tpu_custom_call" | custom-call | bytes 614400 | tf_op jit(solution)/shard_map/pallas_call | solution.py:492
  (30 shorter events, 0.4 us)
Async XLA Ops:
  2.9 49.9 %copy-start.2 = (bf16[2,9,48,48]{3,2,1,0:T(8,128)(2,1)S(1)}, bf16[2,9,48,48]{3,2,1,0:T(8,128)(2,1)}, u32[]{:S(2)}) copy-start(bf16[2,9,48,48]{3,2,1,0:T(8,128)(2,1)} %conv_weight_at) | copy-start | bytes 248836
  2.9 52.3 %copy-start.3 = (f32[24,512]{1,0:T(8,128)S(1)}, f32[24,512]{1,0:T(8,128)}, u32[]{:S(2)}) copy-start(f32[24,512]{1,0:T(8,128)} %bias_at.3) | copy-start | bytes 147460
  2.9 52.3 %copy-start.5 = (f32[2,24]{1,0:T(2,128)S(1)}, f32[2,24]{1,0:T(2,128)}, u32[]{:S(2)}) copy-start(f32[2,24]{1,0:T(2,128)} %conv_bias_at.3) | copy-start | bytes 580
  2.9 52.3 %copy-start.6 = (s32[2]{0:T(128)S(1)}, s32[2]{0:T(128)}, u32[]{:S(2)}) copy-start(s32[2]{0:T(128)} %steps.3) | copy-start | bytes 28
  2.9 27.8 %collective-permute-start = (f32[8,128]{1,0:T(8,128)}, f32[8,128]{1,0:T(8,128)S(1)}, u32[]{:S(2)}, u32[]{:S(2)}) collective-permute-start(f32[8,128]{1,0:T(8,128)} %shard_map.113.tile_at), channel_id=1, source_target_pairs={{32,0},{34,2},{36,4},{38,6},{40,8},{42,10},{44,12},{46,14},{48,16}... | collective-permute-start | bytes 12296 | tf_op jit(solution)/shard_map/ppermute | solution.py:27
  14.2 16.4 %collective-permute-start.1 = (f32[8,128]{1,0:T(8,128)}, f32[8,128]{1,0:T(8,128)S(1)}, u32[]{:S(2)}, u32[]{:S(2)}) collective-permute-start(f32[8,128]{1,0:T(8,128)} %shard_map.113.tile_at), channel_id=1, source_target_pairs={{64,0},{66,2},{68,4},{70,6},{72,8},{74,10},{76,12},{78,14},{80,16}... | collective-permute-start | bytes 12296 | tf_op jit(solution)/shard_map/ppermute | solution.py:27
  16.2 14.5 %collective-permute-start.2 = (f32[8,128]{1,0:T(8,128)}, f32[8,128]{1,0:T(8,128)S(1)}, u32[]{:S(2)}, u32[]{:S(2)}) collective-permute-start(f32[8,128]{1,0:T(8,128)} %shard_map.113.tile_at), channel_id=1, source_target_pairs={{96,0},{128,32},{160,64},{192,96},{224,128},{256,160},{288,192},{3... | collective-permute-start | bytes 12296 | tf_op jit(solution)/shard_map/ppermute | solution.py:634
  22.2 16.1 %collective-permute-start.3 = (bf16[24,16,512]{2,0,1:T(8,128)(2,1)S(1)}, bf16[24,16,512]{2,0,1:T(8,128)(2,1)S(1)}, u32[]{:S(2)}, u32[]{:S(2)}) collective-permute-start(bf16[24,16,512]{2,0,1:T(8,128)(2,1)S(1)} %copy.17), channel_id=1, source_target_pairs={{0,1},{1,0},{2,3},{3,2},{4,5},{5,4},{6,7},{7,6},{8,9},{9,8},{10,11... | collective-permute-start | bytes 1179656 | tf_op jit(solution)/shard_map/ppermute | solution.py:35
  30.7 0.6 copy-start.7
  30.7 0.6 copy-start.8
  31.3 0.6 copy-start.9
  33.8 21.4 %all-to-all-start = ((f32[32,3,8,128]{3,2,1,0:T(8,128)}), f32[32,3,8,128]{3,2,1,0:T(8,128)S(1)}, u32[]{:S(2)}, u32[]{:S(2)}) async-start(f32[32,3,8,128]{3,2,1,0:T(8,128)} %bitcast.34), calls=%async_computation | async-start | bytes 786432 | tf_op jit(solution)/shard_map/all_to_all | solution.py:626
  38.5 31.1 %collective-permute-start.4 = (bf16[16,48,512]{2,1,0:T(8,128)(2,1)S(1)}, bf16[16,48,512]{2,1,0:T(8,128)(2,1)S(1)}, u32[]{:S(2)}, u32[]{:S(2)}) collective-permute-start(bf16[16,48,512]{2,1,0:T(8,128)(2,1)S(1)} %fusion.cot_here), channel_id=1, source_target_pairs={{0,2},{2,4},{4,6},{6,8},{8,10},{10,12},{12,14},{14,16},{16,18},{18... | collective-permute-start | bytes 2359304 | tf_op jit(solution)/shard_map/ppermute | solution.py:27
  40.4 29.2 %collective-permute-start.5 = (bf16[16,48,512]{2,1,0:T(8,128)(2,1)S(1)}, bf16[16,48,512]{2,1,0:T(8,128)(2,1)S(1)}, u32[]{:S(2)}, u32[]{:S(2)}) collective-permute-start(bf16[16,48,512]{2,1,0:T(8,128)(2,1)S(1)} %fusion.cot_here), channel_id=1, source_target_pairs={{2,0},{4,2},{6,4},{8,6},{10,8},{12,10},{14,12},{16,14},{18,16},{20... | collective-permute-start | bytes 2359304 | tf_op jit(solution)/shard_map/ppermute | solution.py:27
  55.2 14.4 %copy-start.4 = (f32[8,128]{1,0:T(8,128)S(1)}, f32[8,128]{1,0:T(8,128)}, u32[]{:S(2)}) copy-start(f32[8,128]{1,0:T(8,128)} %get-tuple-element.18.last_slab_at) | copy-start | bytes 12292
  76.9 32.1 %copy-start = (bf16[512,24]{0,1:T(8,128)(2,1)S(1)}, bf16[512,24]{0,1:T(8,128)(2,1)}, u32[]{:S(2)}) copy-start(bf16[512,24]{0,1:T(8,128)(2,1)} %param.14) | copy-start | bytes 73732
  76.9 32.1 %copy-start.1 = (bf16[512,24]{0,1:T(8,128)(2,1)S(1)}, bf16[512,24]{0,1:T(8,128)(2,1)}, u32[]{:S(2)}) copy-start(bf16[512,24]{0,1:T(8,128)(2,1)} %param.15) | copy-start | bytes 73732
  94.0 11.1 %collective-permute-start.6 = (f32[2,8,128]{2,1,0:T(8,128)S(1)}, f32[2,8,128]{2,1,0:T(8,128)S(1)}, u32[]{:S(2)}, u32[]{:S(2)}) collective-permute-start(f32[2,8,128]{2,1,0:T(8,128)S(1)} %get-tuple-element.25), channel_id=1, source_target_pairs={{0,32},{2,34},{4,36},{6,38},{8,40},{10,42},{12,44},{14,46},{16,48}... | collective-permute-start | bytes 24584 | tf_op jit(solution)/shard_map/ppermute | solution.py:27
  98.6 10.4 %collective-permute-start.7 = (f32[2,8,128]{2,1,0:T(8,128)S(1)}, f32[2,8,128]{2,1,0:T(8,128)S(1)}, u32[]{:S(2)}, u32[]{:S(2)}) collective-permute-start(f32[2,8,128]{2,1,0:T(8,128)S(1)} %get-tuple-element.24), channel_id=1, source_target_pairs={{0,64},{2,66},{4,68},{6,70},{8,72},{10,74},{12,76},{14,78},{16,80}... | collective-permute-start | bytes 24584 | tf_op jit(solution)/shard_map/ppermute | solution.py:27

commit v6 on v5

--- a/solution.py
+++ b/solution.py
@@ -652,7 +652,8 @@
     scalars = (dilations, band_width)
 
     near_weight, far_weight = near_weight.T, far_weight.T
-    tile = tile_call((window_start,), embedding, near_weight, far_weight)
+    staged = jnp.swapaxes(cotangent, 0, 1)
+    tile = tile_call((window_start,), after(embedding, staged), near_weight, far_weight)
     ahead = from_ahead(tile, members), from_ahead(tile, 2 * members), from_edges(tile, members)
 
     chunks, last_slab = chunk_call(
@@ -660,11 +661,11 @@
     )
     terms = exchange_in_group(chunks)
 
-    cot_other = from_partner(cotangent)
+    cot_other = from_partner(staged)
     offsets = jnp.arange(width, dtype=jnp.int32)
     keep = (offsets[None, :] < band_width[0]) & (row_ids[:, None] + offsets[None, :] < total_rows)
-    cot = jnp.concatenate((cotangent, after(cot_other, chunks)), axis=0)
-    cot = jnp.where(keep[:, None, :], jnp.swapaxes(cot, 0, 1), 0).astype(jnp.bfloat16)
+    cot = jnp.concatenate((staged, after(cot_other, chunks)), axis=1)
+    cot = jnp.where(keep[:, None, :], cot, 0).astype(jnp.bfloat16)
     cot_behind = from_ahead(cot, -1)
     cot_ahead = from_ahead(cot, 1)
 

time: 111 us -> 111 us (level)
  transfers between devices with their start and end apart: 9 -> 9, of which waited for: 4 -> 4; matrix products, arithmetic and copies ran while one was open for 2% -> 1% of each run, Pallas kernels for 14% -> 14%
where the time goes in v6:
time: 111 us; the launch traced here: 110 us
  starting transfers between devices  53.9 us (49%)
  Pallas kernels  25.7 us (23%)
  blocking collectives  17.1 us (15%)
  waiting for transfers between devices  7.76 us (7%)
  local copies, waits for them, and re-layouts  3.33 us (3%)
  between operations  2.19 us (2%)
    ppermute x6, starting transfers between devices, from_ahead(): return lax.ppermute(block, 'chrom', route)  37.5 us
    pallas_call x6, Pallas kernels, call(): pl.pallas_call(kernel, out_shape=out_shapes, in_specs=[pl.BlockSpec(memor...  25.7 us
    all_to_all x1, blocking collectives, exchange_in_group(): lax.all_to_all(flat, ('chrom', 'chan'), 0, 0, axis_index_groups=lists)  17.1 us
    ppermute x1, starting transfers between devices, from_partner(): return lax.ppermute(block, 'chan', [(0, 1), (1, 0)])  7.73 us
    ppermute x6, waiting for transfers between devices, from_ahead(): return lax.ppermute(block, 'chrom', route)  5.93 us
    ppermute x1, starting transfers between devices, from_edges(): return lax.ppermute(block, 'chrom', route)  4.77 us
    all_to_all x1, starting transfers between devices, exchange_in_group(): lax.all_to_all(flat, ('chrom', 'chan'), 0, 0, axis_index_groups=lists)  3.89 us
    unnamed x22, local copies, waits for them, and re-layouts  3.32 us
  transfers between devices with their start and end apart: 9, of which 4 were waited for; matrix products, arithmetic and copies ran while one was open for 1% of the time, Pallas kernels for 14%

profile of v6, /device:TPU:6, one launch (start us, length us, event | category | flops | bytes accessed | tf_op | source)
XLA Modules:
  0.0 110.4 jit_solution(16354449988743661822)
XLA Ops:
  1.3 1.3 %copy.22 = bf16[24,16,512]{2,0,1:T(8,128)(2,1)S(1)} copy(bf16[24,16,512]{2,1,0:T(8,128)(2,1)} %param.19) | data formatting | bytes 786432 | tf_op args[9]
  2.6 1.6 %shard_map.113.tile_at = f32[8,128]{1,0:T(8,128)} custom-call(s32[1]{0:T(128)S(6)} %copy.23.start, bf16[16,512]{1,0:T(8,128)(2,1)} %embedding_at, bf16[24,512]{1,0:T(8,128)(2,1)} %bitcast.27, bf16[24,512]{1,0:T(8,128)(2,1)} %bitcast.30), custom_call_target="tpu_custom_call" | custom-call | bytes 69632 | tf_op jit(solution)/shard_map/pallas_call | solution.py:492
  4.2 11.2 %collective-permute-start = (f32[8,128]{1,0:T(8,128)}, f32[8,128]{1,0:T(8,128)S(1)}, u32[]{:S(2)}, u32[]{:S(2)}) collective-permute-start(f32[8,128]{1,0:T(8,128)} %shard_map.113.tile_at), channel_id=1, source_target_pairs={{32,0},{34,2},{36,4},{38,6},{40,8},{42,10},{44,12},{46,14},{48,16}... | collective-permute-start | bytes 12296 | tf_op jit(solution)/shard_map/ppermute | solution.py:27
  15.4 1.9 %collective-permute-start.1 = (f32[8,128]{1,0:T(8,128)}, f32[8,128]{1,0:T(8,128)S(1)}, u32[]{:S(2)}, u32[]{:S(2)}) collective-permute-start(f32[8,128]{1,0:T(8,128)} %shard_map.113.tile_at), channel_id=1, source_target_pairs={{64,0},{66,2},{68,4},{70,6},{72,8},{74,10},{76,12},{78,14},{80,16}... | collective-permute-start | bytes 12296 | tf_op jit(solution)/shard_map/ppermute | solution.py:27
  17.3 4.8 %collective-permute-start.2 = (f32[8,128]{1,0:T(8,128)}, f32[8,128]{1,0:T(8,128)S(1)}, u32[]{:S(2)}, u32[]{:S(2)}) collective-permute-start(f32[8,128]{1,0:T(8,128)} %shard_map.113.tile_at), channel_id=1, source_target_pairs={{96,0},{128,32},{160,64},{192,96},{224,128},{256,160},{288,192},{3... | collective-permute-start | bytes 12296 | tf_op jit(solution)/shard_map/ppermute | solution.py:634
  22.1 7.7 %collective-permute-start.3 = (bf16[16,24,512]{2,1,0:T(8,128)(2,1)S(1)}, bf16[16,24,512]{2,1,0:T(8,128)(2,1)S(1)}, u32[]{:S(2)}, u32[]{:S(2)}) collective-permute-start(bf16[16,24,512]{2,1,0:T(8,128)(2,1)S(1)} %bitcast.35), channel_id=1, source_target_pairs={{0,1},{1,0},{2,3},{3,2},{4,5},{5,4},{6,7},{7,6},{8,9},{9,8},{10,11... | collective-permute-start | bytes 1179656 | tf_op jit(solution)/shard_map/ppermute | solution.py:35
  30.6 0.5 copy-done.7
  31.2 0.6 copy-done.9
  31.8 1.9 %shard_map.114 = (f32[16,2,3,8,128]{4,3,2,1,0:T(8,128)}, f32[8,128]{1,0:T(8,128)}) custom-call(f32[8,128]{1,0:T(8,128)} %shard_map.113.tile_at, f32[8,128]{1,0:T(8,128)} %copy-done.7, f32[8,128]{1,0:T(8,128)} %copy-done.8, f32[8,128]{1,0:T(8,128)} %copy-done.9, f32[2,24]{1,0:T(2,128)} %conv_bias_at.3, f32[24,512]{1,0:T(8,128)} %bias_at.3, ...), custom_call_target="tpu_custom_call" | custom-call | bytes 512192 | tf_op jit(solution)/shard_map/pallas_call | solution.py:492
  33.7 3.9 %all-to-all-start = ((f32[32,3,8,128]{3,2,1,0:T(8,128)}), f32[32,3,8,128]{3,2,1,0:T(8,128)S(1)}, u32[]{:S(2)}, u32[]{:S(2)}) async-start(f32[32,3,8,128]{3,2,1,0:T(8,128)} %bitcast.37), calls=%async_computation | async-start | bytes 786432 | tf_op jit(solution)/shard_map/all_to_all | solution.py:626
  37.6 0.6 collective-permute-done.3
  38.4 1.9 %collective-permute-start.4 = (bf16[16,48,512]{2,1,0:T(8,128)(2,1)S(1)}, bf16[16,48,512]{2,1,0:T(8,128)(2,1)S(1)}, u32[]{:S(2)}, u32[]{:S(2)}) collective-permute-start(bf16[16,48,512]{2,1,0:T(8,128)(2,1)S(1)} %maximum_select_fusion.cot_here), channel_id=1, source_target_pairs={{0,2},{2,4},{4,6},{6,8},{8,10},{10,12},{12,14},{14,16},{16,18},{18... | collective-permute-start | bytes 2359304 | tf_op jit(solution)/shard_map/ppermute | solution.py:27
  40.3 12.4 %collective-permute-start.5 = (bf16[16,48,512]{2,1,0:T(8,128)(2,1)S(1)}, bf16[16,48,512]{2,1,0:T(8,128)(2,1)S(1)}, u32[]{:S(2)}, u32[]{:S(2)}) collective-permute-start(bf16[16,48,512]{2,1,0:T(8,128)(2,1)S(1)} %maximum_select_fusion.cot_here), channel_id=1, source_target_pairs={{2,0},{4,2},{6,4},{8,6},{10,8},{12,10},{14,12},{16,14},{18,16},{20... | collective-permute-start | bytes 2359304 | tf_op jit(solution)/shard_map/ppermute | solution.py:27
  52.7 1.1 %shard_map.115 = (bf16[368,144]{1,0:T(8,128)(2,1)S(1)}, bf16[368,144]{1,0:T(8,128)(2,1)S(1)}) custom-call(bf16[2,9,48,48]{3,2,1,0:T(8,128)(2,1)S(1)} %copy-done.2), custom_call_target="tpu_custom_call" | custom-call | bytes 294912 | tf_op jit(solution)/shard_map/pallas_call | solution.py:492
  53.9 1.2 %all-to-all-done = f32[32,3,8,128]{3,2,1,0:T(8,128)S(1)} async-done(((f32[32,3,8,128]{3,2,1,0:T(8,128)}), f32[32,3,8,128]{3,2,1,0:T(8,128)S(1)}, u32[]{:S(2)}, u32[]{:S(2)}) %all-to-all-start) | async-done | bytes 393248 | tf_op jit(solution)/shard_map/all_to_all | solution.py:626
  55.1 12.5 %shard_map.116 = (f32[16,24,512]{2,1,0:T(8,128)S(1)}, f32[16,24,512]{2,1,0:T(8,128)S(1)}, f32[32,48,512]{2,1,0:T(8,128)S(1)}) custom-call(s32[2]{0:T(128)S(1)} %copy-done.6, s32[1]{0:T(128)} %copy.24.band, f32[16,2,3,8,128]{4,3,2,1,0:T(8,128)S(1)} %bitcast.22, f32[2,24]{1,0:T(2,128)S(1)} %copy-done.5, f32[24,512]{1,0:T(8,128)S(1)} %copy-done.3, ...), custom_call_target="tpu_custom_call" | custom-call | flops 1415577600 | bytes 5267136 | tf_op jit(solution)/shard_map/pallas_call | solution.py:492
  67.6 1.9 %collective-permute-done.4.cot_behind = bf16[16,48,512]{2,1,0:T(8,128)(2,1)S(1)} collective-permute-done((bf16[16,48,512]{2,1,0:T(8,128)(2,1)S(1)}, bf16[16,48,512]{2,1,0:T(8,128)(2,1)S(1)}, u32[]{:S(2)}, u32[]{:S(2)}) %collective-permute-start.4) | collective-permute-done | bytes 786464 | tf_op jit(solution)/shard_map/ppermute | solution.py:27
  69.5 7.3 %shard_map.117 = bf16[16,2,16,128]{3,2,1,0:T(8,128)(2,1)S(1)} custom-call(s32[2]{0:T(128)S(1)} %copy-done.6, s32[1]{0:T(128)} %copy.24.band, f32[16,24,512]{2,1,0:T(8,128)S(1)} %get-tuple-element.17.slope_0, f32[32,48,512]{2,1,0:T(8,128)S(1)} %get-tuple-element.18.slope_1, bf16[16,48,512]{2,1,0:T(8,128)(2,1)S(1)} %collective-permute-done.4.cot_behind, ...), custom_call_target="tpu_custom_call" | custom-call | flops 1415577600 | bytes 6532608 | tf_op jit(solution)/shard_map/pallas_call | solution.py:492
  76.8 17.1 %all_to_all.10 = bf16[32,16,128]{2,1,0:T(8,128)(2,1)S(1)} all-to-all(bf16[32,16,128]{2,1,0:T(8,128)(2,1)S(1)} %bitcast.26), channel_id=1, replica_groups={{0,1,2,3,4,5,6,7,8,9,10,11,12,13,14,15,16,17,18,19,20,21,22,23,24,25,26..., dimensions={0} | all-to-all | bytes 262144 | tf_op jit(solution)/shard_map/all_to_all | solution.py:626
  94.0 4.6 %collective-permute-start.6 = (f32[2,8,128]{2,1,0:T(8,128)S(1)}, f32[2,8,128]{2,1,0:T(8,128)S(1)}, u32[]{:S(2)}, u32[]{:S(2)}) collective-permute-start(f32[2,8,128]{2,1,0:T(8,128)S(1)} %get-tuple-element.27), channel_id=1, source_target_pairs={{0,32},{2,34},{4,36},{6,38},{8,40},{10,42},{12,44},{14,46},{16,48}... | collective-permute-start | bytes 24584 | tf_op jit(solution)/shard_map/ppermute | solution.py:27
  98.6 5.4 %collective-permute-start.7 = (f32[2,8,128]{2,1,0:T(8,128)S(1)}, f32[2,8,128]{2,1,0:T(8,128)S(1)}, u32[]{:S(2)}, u32[]{:S(2)}) collective-permute-start(f32[2,8,128]{2,1,0:T(8,128)S(1)} %get-tuple-element.26), channel_id=1, source_target_pairs={{0,64},{2,66},{4,68},{6,70},{8,72},{10,74},{12,76},{14,78},{16,80}... | collective-permute-start | bytes 24584 | tf_op jit(solution)/shard_map/ppermute | solution.py:27
  104.1 0.9 copy.18
  105.0 4.0 %collective-permute-done.7.ahead_2_at = f32[2,8,128]{2,1,0:T(8,128)S(1)} collective-permute-done((f32[2,8,128]{2,1,0:T(8,128)S(1)}, f32[2,8,128]{2,1,0:T(8,128)S(1)}, u32[]{:S(2)}, u32[]{:S(2)}) %collective-permute-start.7) | collective-permute-done | bytes 8224 | tf_op jit(solution)/shard_map/ppermute | solution.py:27
  109.0 1.4 %shard_map.118 = bf16[16,256]{1,0:T(8,128)(2,1)} custom-call(f32[2,2,8,128]{3,2,1,0:T(8,128)S(1)} %bitcast.34, f32[2,8,128]{2,1,0:T(8,128)S(1)} %collective-permute-done.6.ahead_1_at, f32[2,8,128]{2,1,0:T(8,128)S(1)} %collective-permute-done.7.ahead_2_at, f32[16,2,3,8,128]{4,3,2,1,0:T(8,128)S(1)} %bitcast.23, bf16[16,2,16,128]{3,2,1,0:T(8,128)(2,1)S(1)} %bitcast.25, ...), custom_call_target="tpu_custom_call" | custom-call | bytes 614400 | tf_op jit(solution)/shard_map/pallas_call | solution.py:492
  (30 shorter events, 0.4 us)
Async XLA Ops:
  1.3 51.4 %copy-start.2 = (bf16[2,9,48,48]{3,2,1,0:T(8,128)(2,1)S(1)}, bf16[2,9,48,48]{3,2,1,0:T(8,128)(2,1)}, u32[]{:S(2)}) copy-start(bf16[2,9,48,48]{3,2,1,0:T(8,128)(2,1)} %conv_weight_at) | copy-start | bytes 248836
  2.5 52.6 %copy-start.3 = (f32[24,512]{1,0:T(8,128)S(1)}, f32[24,512]{1,0:T(8,128)}, u32[]{:S(2)}) copy-start(f32[24,512]{1,0:T(8,128)} %bias_at.3) | copy-start | bytes 147460
  2.6 52.6 %copy-start.5 = (f32[2,24]{1,0:T(2,128)S(1)}, f32[2,24]{1,0:T(2,128)}, u32[]{:S(2)}) copy-start(f32[2,24]{1,0:T(2,128)} %conv_bias_at.3) | copy-start | bytes 580
  2.6 52.5 %copy-start.6 = (s32[2]{0:T(128)S(1)}, s32[2]{0:T(128)}, u32[]{:S(2)}) copy-start(s32[2]{0:T(128)} %steps.3) | copy-start | bytes 28
  4.2 26.4 %collective-permute-start = (f32[8,128]{1,0:T(8,128)}, f32[8,128]{1,0:T(8,128)S(1)}, u32[]{:S(2)}, u32[]{:S(2)}) collective-permute-start(f32[8,128]{1,0:T(8,128)} %shard_map.113.tile_at), channel_id=1, source_target_pairs={{32,0},{34,2},{36,4},{38,6},{40,8},{42,10},{44,12},{46,14},{48,16}... | collective-permute-start | bytes 12296 | tf_op jit(solution)/shard_map/ppermute | solution.py:27
  15.4 15.2 %collective-permute-start.1 = (f32[8,128]{1,0:T(8,128)}, f32[8,128]{1,0:T(8,128)S(1)}, u32[]{:S(2)}, u32[]{:S(2)}) collective-permute-start(f32[8,128]{1,0:T(8,128)} %shard_map.113.tile_at), channel_id=1, source_target_pairs={{64,0},{66,2},{68,4},{70,6},{72,8},{74,10},{76,12},{78,14},{80,16}... | collective-permute-start | bytes 12296 | tf_op jit(solution)/shard_map/ppermute | solution.py:27
  17.3 13.3 %collective-permute-start.2 = (f32[8,128]{1,0:T(8,128)}, f32[8,128]{1,0:T(8,128)S(1)}, u32[]{:S(2)}, u32[]{:S(2)}) collective-permute-start(f32[8,128]{1,0:T(8,128)} %shard_map.113.tile_at), channel_id=1, source_target_pairs={{96,0},{128,32},{160,64},{192,96},{224,128},{256,160},{288,192},{3... | collective-permute-start | bytes 12296 | tf_op jit(solution)/shard_map/ppermute | solution.py:634
  22.1 16.1 %collective-permute-start.3 = (bf16[16,24,512]{2,1,0:T(8,128)(2,1)S(1)}, bf16[16,24,512]{2,1,0:T(8,128)(2,1)S(1)}, u32[]{:S(2)}, u32[]{:S(2)}) collective-permute-start(bf16[16,24,512]{2,1,0:T(8,128)(2,1)S(1)} %bitcast.35), channel_id=1, source_target_pairs={{0,1},{1,0},{2,3},{3,2},{4,5},{5,4},{6,7},{7,6},{8,9},{9,8},{10,11... | collective-permute-start | bytes 1179656 | tf_op jit(solution)/shard_map/ppermute | solution.py:35
  30.6 0.6 copy-start.7
  30.6 0.6 copy-start.8
  31.2 0.6 copy-start.9
  33.7 21.4 %all-to-all-start = ((f32[32,3,8,128]{3,2,1,0:T(8,128)}), f32[32,3,8,128]{3,2,1,0:T(8,128)S(1)}, u32[]{:S(2)}, u32[]{:S(2)}) async-start(f32[32,3,8,128]{3,2,1,0:T(8,128)} %bitcast.37), calls=%async_computation | async-start | bytes 786432 | tf_op jit(solution)/shard_map/all_to_all | solution.py:626
  38.4 31.1 %collective-permute-start.4 = (bf16[16,48,512]{2,1,0:T(8,128)(2,1)S(1)}, bf16[16,48,512]{2,1,0:T(8,128)(2,1)S(1)}, u32[]{:S(2)}, u32[]{:S(2)}) collective-permute-start(bf16[16,48,512]{2,1,0:T(8,128)(2,1)S(1)} %maximum_select_fusion.cot_here), channel_id=1, source_target_pairs={{0,2},{2,4},{4,6},{6,8},{8,10},{10,12},{12,14},{14,16},{16,18},{18... | collective-permute-start | bytes 2359304 | tf_op jit(solution)/shard_map/ppermute | solution.py:27
  40.3 29.2 %collective-permute-start.5 = (bf16[16,48,512]{2,1,0:T(8,128)(2,1)S(1)}, bf16[16,48,512]{2,1,0:T(8,128)(2,1)S(1)}, u32[]{:S(2)}, u32[]{:S(2)}) collective-permute-start(bf16[16,48,512]{2,1,0:T(8,128)(2,1)S(1)} %maximum_select_fusion.cot_here), channel_id=1, source_target_pairs={{2,0},{4,2},{6,4},{8,6},{10,8},{12,10},{14,12},{16,14},{18,16},{20... | collective-permute-start | bytes 2359304 | tf_op jit(solution)/shard_map/ppermute | solution.py:27
  55.1 14.4 %copy-start.4 = (f32[8,128]{1,0:T(8,128)S(1)}, f32[8,128]{1,0:T(8,128)}, u32[]{:S(2)}) copy-start(f32[8,128]{1,0:T(8,128)} %get-tuple-element.20.last_slab_at) | copy-start | bytes 12292
  76.8 32.2 %copy-start = (bf16[512,24]{0,1:T(8,128)(2,1)S(1)}, bf16[512,24]{0,1:T(8,128)(2,1)}, u32[]{:S(2)}) copy-start(bf16[512,24]{0,1:T(8,128)(2,1)} %param.14) | copy-start | bytes 73732
  76.8 32.2 %copy-start.1 = (bf16[512,24]{0,1:T(8,128)(2,1)S(1)}, bf16[512,24]{0,1:T(8,128)(2,1)}, u32[]{:S(2)}) copy-start(bf16[512,24]{0,1:T(8,128)(2,1)} %param.15) | copy-start | bytes 73732
  94.0 11.0 %collective-permute-start.6 = (f32[2,8,128]{2,1,0:T(8,128)S(1)}, f32[2,8,128]{2,1,0:T(8,128)S(1)}, u32[]{:S(2)}, u32[]{:S(2)}) collective-permute-start(f32[2,8,128]{2,1,0:T(8,128)S(1)} %get-tuple-element.27), channel_id=1, source_target_pairs={{0,32},{2,34},{4,36},{6,38},{8,40},{10,42},{12,44},{14,46},{16,48}... | collective-permute-start | bytes 24584 | tf_op jit(solution)/shard_map/ppermute | solution.py:27
  98.6 10.4 %collective-permute-start.7 = (f32[2,8,128]{2,1,0:T(8,128)S(1)}, f32[2,8,128]{2,1,0:T(8,128)S(1)}, u32[]{:S(2)}, u32[]{:S(2)}) collective-permute-start(f32[2,8,128]{2,1,0:T(8,128)S(1)} %get-tuple-element.26), channel_id=1, source_target_pairs={{0,64},{2,66},{4,68},{6,70},{8,72},{10,74},{12,76},{14,78},{16,80}... | collective-permute-start | bytes 24584 | tf_op jit(solution)/shard_map/ppermute | solution.py:27
